TPU v7x, 32 devices: a whole 2x2x4 slice. The times are simulated.
32 devices in a mesh: dp: 8 (over z, x), tensor: 4 (over y, core).
Axes of the slice: x: 2, y: 2, z: 4, core: 2. Of those that a mesh axis runs over, the one named last changes fastest.
Arguments:
- encoder_rows: bfloat16 [8192, 768], P(('dp', 'tensor')), may hold values from -6 to 6
- decoder_rows: bfloat16 [4096, 768], P(('dp', 'tensor')), may hold values from -6 to 6
- encoder_segments: int32 [8, 1024], P('dp'), may hold values from 0 to 3, as said below
- decoder_segments: int32 [8, 512], P('dp'), may hold values from 0 to 3, as said below
- norm_gains: float32 [6, 768], replicated, may hold values from 0.5 to 1.5
- encoder_attention_in: bfloat16 [768, 3, 768], P(None, None, 'tensor'), may hold values from -0.109375 to 0.109375
- encoder_attention_out: bfloat16 [768, 768], P('tensor'), may hold values from -1.75 to 1.75
- encoder_gate_up: bfloat16 [768, 2, 2048], P(None, None, 'tensor'), may hold values from -0.21875 to 0.21875
- encoder_down: bfloat16 [2048, 768], P('tensor'), may hold values from -0.1875 to 0.1875
- decoder_attention_in: bfloat16 [768, 3, 768], P(None, None, 'tensor'), may hold values from -0.109375 to 0.109375
- decoder_attention_out: bfloat16 [768, 768], P('tensor'), may hold values from -1.75 to 1.75
- cross_queries: bfloat16 [768, 768], P(None, 'tensor'), may hold values from -0.109375 to 0.109375
- cross_key_value_rows: bfloat16 [768, 2, 768], P(None, None, 'tensor'), may hold values from -0.109375 to 0.109375
- cross_output: bfloat16 [768, 768], P('tensor'), may hold values from -1.75 to 1.75
- decoder_gate_up: bfloat16 [768, 2, 2048], P(None, None, 'tensor'), may hold values from -0.21875 to 0.21875
- decoder_down: bfloat16 [2048, 768], P('tensor'), may hold values from -0.1875 to 0.1875
- position_tables: float32 [2, 32, 12], P(None, None, 'tensor'), may hold values from -6 to 6
- encoder_cotangent: bfloat16 [8192, 768], P(('dp', 'tensor')), may hold values from -6 to 6
- decoder_cotangent: bfloat16 [4096, 768], P(('dp', 'tensor')), may hold values from -6 to 6
Outputs:
- encoder_result: bfloat16 [8192, 768], P(('dp', 'tensor'))
- decoder_result: bfloat16 [4096, 768], P(('dp', 'tensor'))
- encoder_rows_gradient: float32 [8192, 768], P(('dp', 'tensor'))
- decoder_rows_gradient: float32 [4096, 768], P(('dp', 'tensor'))
- norm_gains_gradient: float32 [6, 768], replicated
- encoder_attention_in_gradient: float32 [768, 3, 768], P(None, None, 'tensor')
- encoder_attention_out_gradient: float32 [768, 768], P('tensor')
- encoder_gate_up_gradient: float32 [768, 2, 2048], P(None, None, 'tensor')
- encoder_down_gradient: float32 [2048, 768], P('tensor')
- decoder_attention_in_gradient: float32 [768, 3, 768], P(None, None, 'tensor')
- decoder_attention_out_gradient: float32 [768, 768], P('tensor')
- cross_queries_gradient: float32 [768, 768], P(None, 'tensor')
- cross_keys_values_gradient: float32 [768, 2, 768], P(None, None, 'tensor')
- cross_output_gradient: float32 [768, 768], P('tensor')
- decoder_gate_up_gradient: float32 [768, 2, 2048], P(None, None, 'tensor')
- decoder_down_gradient: float32 [2048, 768], P('tensor')
- position_tables_gradient: float32 [2, 32, 12], P(None, None, 'tensor')
Inputs may be any that keep to these rules, and one draw needn't show every extreme that they name: `encoder_segments`: each row holds 4 segments numbered 0 to 3 in order, each of 2 or more positions. `decoder_segments`: each row holds 4 segments numbered 0 to 3 in order, each of 2 or more positions; segment k of a decoder row belongs to segment k of the same encoder row.
All inputs are finite; a program needn't handle non-finite values.
Results may differ from a plain program's by a relative error of at most 0.025.
The roundings to bfloat16 on the way count: a program that leaves them out, or rounds other values in their place, can miss the bound.
Values may be sent and summed in bfloat16 or wider, within the bound.
A program may use at most 512 MiB of HBM per device.

v0:
```python
import math

import jax
import jax.numpy as jnp
from jax import lax
from jax.sharding import PartitionSpec as P

BUCKETS = 32


EPS = 1e-06
NEG = -1e30


def bucket_limits(exact_range, far_range, bucket_count):
    limits = []
    for level_index in range(1, bucket_count - exact_range):
        candidate = exact_range
        while (
            int(
                math.log(candidate / exact_range)
                / math.log(far_range / exact_range)
                * (bucket_count - exact_range)
            )
            < level_index
        ):
            candidate += 1
        limits.append(candidate)
    return limits


def relative_buckets(offsets, both_sides):
    if both_sides:
        bucket_count = BUCKETS // 2
        direction_base = jnp.where(offsets > 0, bucket_count, 0).astype(jnp.int32)
        distance = jnp.abs(offsets)
    else:
        bucket_count = BUCKETS
        direction_base = jnp.zeros_like(offsets)
        distance = jnp.maximum(-offsets, 0)
    exact_range = bucket_count // 2
    far_bucket = jnp.full_like(distance, exact_range)
    for limit_value in bucket_limits(exact_range, 128, bucket_count):
        far_bucket = far_bucket + (distance >= limit_value).astype(jnp.int32)
    return direction_base + jnp.where(distance < exact_range, distance, far_bucket)


def normalize(residual, gain_row):
    scale_row = lax.rsqrt(jnp.mean(residual * residual, axis=-1, keepdims=True) + EPS)
    return (residual * scale_row * gain_row, scale_row)


def normalize_backward(residual, scale_row, gain_row, normed_grad):
    weighted = normed_grad * gain_row
    inner_mean = jnp.mean(residual * weighted, axis=-1, keepdims=True)
    input_grad = scale_row * weighted - residual * scale_row**3 * inner_mean
    gain_grad = jnp.sum(normed_grad * residual * scale_row, axis=0)
    return (input_grad, gain_grad)


def offset_buckets(key_count, attention_kind):
    offsets_all = jnp.arange(2 * key_count - 1, dtype=jnp.int32) - (key_count - 1)
    return relative_buckets(offsets_all, attention_kind == "encoder")


def block_scores(
    query_block, key_rows, row_start, query_segments, key_segments, bias_table, attention_kind
):
    scores = jnp.einsum("bhd,lhd->hbl", query_block, key_rows, preferred_element_type=jnp.float32)
    key_count = key_rows.shape[0]
    rows_here = row_start + jnp.arange(query_block.shape[0], dtype=jnp.int32)
    columns = jnp.arange(key_count, dtype=jnp.int32)
    allowed = query_segments[:, None] == key_segments[None, :]
    bucket_line = None
    if attention_kind != "cross":
        bucket_line = offset_buckets(key_count, attention_kind)
        bias_line = jnp.transpose(jnp.take(bias_table, bucket_line, axis=0))
        offset_index = columns[None, :] - rows_here[:, None] + (key_count - 1)
        scores = scores + jnp.take(bias_line, offset_index, axis=1)
    if attention_kind == "decoder":
        allowed = allowed & (columns[None, :] <= rows_here[:, None])
    return (scores, allowed[None], bucket_line)


def table_gradient(score_grad, bucket_line, row_start):
    heads_local, block_rows, key_count = score_grad.shape
    width = block_rows + key_count
    padded = jnp.pad(score_grad, ((0, 0), (0, 0), (block_rows, 0)))
    flat = jnp.pad(padded.reshape(heads_local, block_rows * width), ((0, 0), (0, block_rows)))
    skewed = flat.reshape(heads_local, block_rows, width + 1)
    diagonal_sums = jnp.sum(skewed, axis=1, dtype=jnp.float32)
    offset_index = jnp.arange(width + 1, dtype=jnp.int32) - block_rows - row_start + (key_count - 1)
    offset_index = jnp.clip(offset_index, 0, 2 * key_count - 2)
    bucket_here = jnp.take(bucket_line, offset_index)
    one_hot = (bucket_here[:, None] == jnp.arange(BUCKETS, dtype=jnp.int32)[None, :]).astype(
        jnp.float32
    )
    return jnp.einsum("hc,ck->kh", diagonal_sums, one_hot, preferred_element_type=jnp.float32)


def attend_forward(
    query_rows, key_rows, value_rows, query_segments, key_segments, bias_table, attention_kind
):
    block_rows = min(512, query_rows.shape[0])
    outputs = []
    log_totals = []
    for block_index in range(query_rows.shape[0] // block_rows):
        row_start = block_index * block_rows
        row_end = row_start + block_rows
        scores, allowed, bucket_line = block_scores(
            query_rows[row_start:row_end],
            key_rows,
            row_start,
            query_segments[row_start:row_end],
            key_segments,
            bias_table,
            attention_kind,
        )
        masked = jnp.where(allowed, scores, NEG)
        row_peak = jnp.max(masked, axis=-1, keepdims=True)
        exponent = jnp.exp(masked - row_peak)
        row_total = jnp.sum(exponent, axis=-1, keepdims=True)
        probabilities = (exponent / row_total).astype(jnp.bfloat16)
        outputs.append(
            jnp.einsum(
                "hbl,lhd->bhd", probabilities, value_rows, preferred_element_type=jnp.float32
            )
        )
        log_totals.append((row_peak + jnp.log(row_total))[..., 0])
    return (jnp.concatenate(outputs, axis=0), jnp.concatenate(log_totals, axis=1))


def attend_backward(
    query_rows,
    key_rows,
    value_rows,
    out_grad,
    log_totals,
    query_segments,
    key_segments,
    bias_table,
    attention_kind,
):
    block_rows = min(512, query_rows.shape[0])
    heads_local = query_rows.shape[1]
    key_grad = jnp.zeros(key_rows.shape, jnp.float32)
    value_grad = jnp.zeros(value_rows.shape, jnp.float32)
    table_grad = jnp.zeros((BUCKETS, heads_local), jnp.float32)
    query_grads = []
    for block_index in range(query_rows.shape[0] // block_rows):
        row_start = block_index * block_rows
        row_end = row_start + block_rows
        query_block = query_rows[row_start:row_end]
        scores, allowed, bucket_line = block_scores(
            query_block,
            key_rows,
            row_start,
            query_segments[row_start:row_end],
            key_segments,
            bias_table,
            attention_kind,
        )
        probabilities = jnp.where(
            allowed, jnp.exp(scores - log_totals[:, row_start:row_end, None]), 0.0
        )
        grad_block = out_grad[row_start:row_end]
        prob_grad = jnp.einsum(
            "bhd,lhd->hbl", grad_block, value_rows, preferred_element_type=jnp.float32
        )
        row_delta = jnp.sum(probabilities * prob_grad, axis=-1, keepdims=True)
        score_grad = (probabilities * (prob_grad - row_delta)).astype(jnp.bfloat16)
        query_grads.append(
            jnp.einsum("hbl,lhd->bhd", score_grad, key_rows, preferred_element_type=jnp.float32)
        )
        key_grad = key_grad + jnp.einsum(
            "hbl,bhd->lhd", score_grad, query_block, preferred_element_type=jnp.float32
        )
        value_grad = value_grad + jnp.einsum(
            "hbl,bhd->lhd",
            probabilities.astype(jnp.bfloat16),
            grad_block,
            preferred_element_type=jnp.float32,
        )
        if bucket_line is not None:
            table_grad = table_grad + table_gradient(score_grad, bucket_line, row_start)
    return (jnp.concatenate(query_grads, axis=0), key_grad, value_grad, table_grad)


def self_forward(normalized_everything, input_weight, segments, bias_table, attention_kind):
    seq_count, length = segments.shape
    heads_local = bias_table.shape[1]
    projected_rows = jnp.einsum(
        "ux,xhj->uhj", normalized_everything, input_weight, preferred_element_type=jnp.float32
    ).astype(jnp.bfloat16)
    split_rows = projected_rows.reshape(seq_count, length, 3, heads_local, -1)

    def one_sequence(sequence_items):
        triple, segment_row = sequence_items
        return attend_forward(
            triple[:, 0],
            triple[:, 1],
            triple[:, 2],
            segment_row,
            segment_row,
            bias_table,
            attention_kind,
        )

    attended, log_totals = lax.map(one_sequence, (split_rows, segments))
    return (
        attended.reshape(seq_count * length, -1).astype(jnp.bfloat16),
        projected_rows,
        log_totals,
    )


def self_backward(
    normalized_everything,
    input_weight,
    weight_out,
    projected_rows,
    attended,
    log_totals,
    segments,
    bias_table,
    attention_kind,
    grad_rows,
):
    seq_count, length = segments.shape
    heads_local = bias_table.shape[1]
    attended_grad = jnp.einsum(
        "gd,id->gi", grad_rows, weight_out, preferred_element_type=jnp.float32
    ).astype(jnp.bfloat16)
    weight_out_grad = jnp.einsum(
        "gi,gd->id", attended, grad_rows, preferred_element_type=jnp.float32
    )
    split_rows = projected_rows.reshape(seq_count, length, 3, heads_local, -1)
    grad_split = attended_grad.reshape(seq_count, length, heads_local, -1)

    def one_sequence(sequence_items):
        triple, out_grad, totals_row, segment_row = sequence_items
        query_grad, key_grad, value_grad, table_grad = attend_backward(
            triple[:, 0],
            triple[:, 1],
            triple[:, 2],
            out_grad,
            totals_row,
            segment_row,
            segment_row,
            bias_table,
            attention_kind,
        )
        return (
            jnp.stack([query_grad, key_grad, value_grad], axis=1).astype(jnp.bfloat16),
            table_grad,
        )

    projected_gradient, table_grads = lax.map(
        one_sequence, (split_rows, grad_split, log_totals, segments)
    )
    projected_gradient = projected_gradient.reshape(seq_count * length, 3, -1)
    weight_in_grad = jnp.einsum(
        "tn,tfq->nfq", normalized_everything, projected_gradient, preferred_element_type=jnp.float32
    )
    normed_grad = jnp.einsum(
        "vte,xte->vx", projected_gradient, input_weight, preferred_element_type=jnp.float32
    )
    return (normed_grad, weight_in_grad, weight_out_grad, jnp.sum(table_grads, axis=0))


def feed_forward(normalized_everything, gate_up_matrix, down_weight):
    gate_up_rows = jnp.einsum(
        "ux,xhj->uhj", normalized_everything, gate_up_matrix, preferred_element_type=jnp.float32
    )
    hidden = (jax.nn.gelu(gate_up_rows[:, 0]) * gate_up_rows[:, 1]).astype(jnp.bfloat16)
    return (jnp.dot(hidden, down_weight, preferred_element_type=jnp.float32), gate_up_rows, hidden)


def feed_backward(
    normalized_everything, gate_up_matrix, down_weight, gate_up_rows, hidden, grad_rows
):
    hidden_grad = jnp.einsum(
        "gd,fd->gf", grad_rows, down_weight, preferred_element_type=jnp.float32
    )
    down_grad = jnp.einsum("gf,gd->fd", hidden, grad_rows, preferred_element_type=jnp.float32)
    activated, gelu_pullback = jax.vjp(jax.nn.gelu, gate_up_rows[:, 0])
    gate_grad = gelu_pullback(hidden_grad * gate_up_rows[:, 1])[0]
    up_grad = hidden_grad * activated
    stacked_rows = jnp.stack([gate_grad, up_grad], axis=1).astype(jnp.bfloat16)
    gate_up_grad = jnp.einsum(
        "tn,tfq->nfq", normalized_everything, stacked_rows, preferred_element_type=jnp.float32
    )
    normed_grad = jnp.einsum(
        "vte,xte->vx", stacked_rows, gate_up_matrix, preferred_element_type=jnp.float32
    )
    return (normed_grad, gate_up_grad, down_grad)


def gather_rows(local_rows):
    return lax.all_gather(local_rows, "tensor", axis=0, tiled=True)


def scatter_rows(partial_rows):
    return lax.psum_scatter(partial_rows, "tensor", scatter_dimension=0, tiled=True)


def gather_grads(local_grads):
    return lax.all_gather(local_grads.astype(jnp.bfloat16), "tensor", axis=0, tiled=True)


def scatter_grads(partial_grads):
    return lax.psum_scatter(partial_grads, "tensor", scatter_dimension=0, tiled=True)


def local(
    encoder_rows,
    decoder_rows,
    encoder_segments,
    decoder_segments,
    norm_gains,
    encoder_attention_in,
    encoder_attention_out,
    encoder_gate_up,
    encoder_down,
    decoder_attention_in,
    decoder_attention_out,
    cross_queries,
    cross_key_value_rows,
    cross_output,
    decoder_gate_up,
    decoder_down,
    position_tables,
    encoder_cotangent,
    decoder_cotangent,
):
    seq_count, enc_length = encoder_segments.shape
    dec_length = decoder_segments.shape[1]
    heads_local = position_tables.shape[2]
    inner_local = cross_output.shape[0]
    head_size = inner_local // heads_local
    encoder_input = encoder_rows.astype(jnp.float32)
    normed_value, scale_attention = normalize(encoder_input, norm_gains[0])
    encoder_attention_rows = gather_rows(normed_value.astype(jnp.bfloat16))
    attended_one, projected_one, totals_one = self_forward(
        encoder_attention_rows,
        encoder_attention_in,
        encoder_segments,
        position_tables[0],
        "encoder",
    )
    encoder_middle = encoder_input + scatter_rows(
        jnp.dot(attended_one, encoder_attention_out, preferred_element_type=jnp.float32)
    )
    normed_value, scale_feed = normalize(encoder_middle, norm_gains[1])
    encoder_feed_rows = gather_rows(normed_value.astype(jnp.bfloat16))
    feed_part, gate_up_one, hidden_one = feed_forward(
        encoder_feed_rows, encoder_gate_up, encoder_down
    )
    encoder_last = encoder_middle + scatter_rows(feed_part)
    final_value, scale_final = normalize(encoder_last, norm_gains[2])
    encoder_result = final_value.astype(jnp.bfloat16)
    encoder_closing_rows = gather_rows(encoder_result)
    cross_pairs = jnp.einsum(
        "ux,xhj->uhj",
        encoder_closing_rows,
        cross_key_value_rows,
        preferred_element_type=jnp.float32,
    ).astype(jnp.bfloat16)
    decoder_input = decoder_rows.astype(jnp.float32)
    normed_value, scale_self = normalize(decoder_input, norm_gains[3])
    decoder_self_rows = gather_rows(normed_value.astype(jnp.bfloat16))
    attended_two, projected_two, totals_two = self_forward(
        decoder_self_rows, decoder_attention_in, decoder_segments, position_tables[1], "decoder"
    )
    decoder_middle = decoder_input + scatter_rows(
        jnp.dot(attended_two, decoder_attention_out, preferred_element_type=jnp.float32)
    )
    normed_value, scale_cross = normalize(decoder_middle, norm_gains[4])
    decoder_cross_rows = gather_rows(normed_value.astype(jnp.bfloat16))
    cross_query_rows = jnp.dot(
        decoder_cross_rows, cross_queries, preferred_element_type=jnp.float32
    ).astype(jnp.bfloat16)
    query_split = cross_query_rows.reshape(seq_count, dec_length, heads_local, head_size)
    pair_split = cross_pairs.reshape(seq_count, enc_length, 2, heads_local, head_size)

    def cross_sequence(sequence_items):
        query_seq, pair_seq, query_segs, key_segs = sequence_items
        return attend_forward(
            query_seq, pair_seq[:, 0], pair_seq[:, 1], query_segs, key_segs, None, "cross"
        )

    cross_attended, cross_totals = lax.map(
        cross_sequence, (query_split, pair_split, decoder_segments, encoder_segments)
    )
    cross_attended = cross_attended.reshape(seq_count * dec_length, inner_local).astype(
        jnp.bfloat16
    )
    decoder_later = decoder_middle + scatter_rows(
        jnp.dot(cross_attended, cross_output, preferred_element_type=jnp.float32)
    )
    normed_value, scale_last = normalize(decoder_later, norm_gains[5])
    decoder_feed_rows = gather_rows(normed_value.astype(jnp.bfloat16))
    feed_two, gate_up_two, hidden_two = feed_forward(
        decoder_feed_rows, decoder_gate_up, decoder_down
    )
    decoder_result = (decoder_later + scatter_rows(feed_two)).astype(jnp.bfloat16)
    result_grad = decoder_cotangent.astype(jnp.float32)
    normed_grad, gate_up_grad_two, down_grad_two = feed_backward(
        decoder_feed_rows,
        decoder_gate_up,
        decoder_down,
        gate_up_two,
        hidden_two,
        gather_grads(result_grad),
    )
    input_part, gain_five = normalize_backward(
        decoder_later, scale_last, norm_gains[5], scatter_grads(normed_grad)
    )
    later_grad = result_grad + input_part
    branch_grad = gather_grads(later_grad)
    cross_attended_grad = jnp.einsum(
        "gd,id->gi", branch_grad, cross_output, preferred_element_type=jnp.float32
    ).astype(jnp.bfloat16)
    cross_output_grad = jnp.einsum(
        "gi,gd->id", cross_attended, branch_grad, preferred_element_type=jnp.float32
    )

    def cross_back(sequence_items):
        query_seq, pair_seq, out_grad, totals_row, query_segs, key_segs = sequence_items
        query_grad, key_grad, value_grad, unused_table = attend_backward(
            query_seq,
            pair_seq[:, 0],
            pair_seq[:, 1],
            out_grad,
            totals_row,
            query_segs,
            key_segs,
            None,
            "cross",
        )
        return (
            query_grad.astype(jnp.bfloat16),
            jnp.stack([key_grad, value_grad], axis=1).astype(jnp.bfloat16),
        )

    query_grads, key_value_gradients = lax.map(
        cross_back,
        (
            query_split,
            pair_split,
            cross_attended_grad.reshape(seq_count, dec_length, heads_local, head_size),
            cross_totals,
            decoder_segments,
            encoder_segments,
        ),
    )
    query_grads = query_grads.reshape(seq_count * dec_length, inner_local)
    key_value_gradients = key_value_gradients.reshape(seq_count * enc_length, 2, inner_local)
    cross_queries_grad = jnp.einsum(
        "gd,gi->di", decoder_cross_rows, query_grads, preferred_element_type=jnp.float32
    )
    cross_pairs_grad = jnp.einsum(
        "tn,tfq->nfq", encoder_closing_rows, key_value_gradients, preferred_element_type=jnp.float32
    )
    input_part, gain_four = normalize_backward(
        decoder_middle,
        scale_cross,
        norm_gains[4],
        scatter_grads(
            jnp.einsum("gi,di->gd", query_grads, cross_queries, preferred_element_type=jnp.float32)
        ),
    )
    middle_grad = later_grad + input_part
    final_grad = encoder_cotangent.astype(jnp.float32) + lax.psum_scatter(
        jnp.einsum(
            "vte,xte->vx",
            key_value_gradients,
            cross_key_value_rows,
            preferred_element_type=jnp.float32,
        ),
        "tensor",
        scatter_dimension=0,
        tiled=True,
    )
    normed_grad, self_in_grad, self_out_grad, table_two = self_backward(
        decoder_self_rows,
        decoder_attention_in,
        decoder_attention_out,
        projected_two,
        attended_two,
        totals_two,
        decoder_segments,
        position_tables[1],
        "decoder",
        gather_grads(middle_grad),
    )
    input_part, gain_three = normalize_backward(
        decoder_input, scale_self, norm_gains[3], scatter_grads(normed_grad)
    )
    decoder_rows_gradient = middle_grad + input_part
    last_grad, gain_two = normalize_backward(encoder_last, scale_final, norm_gains[2], final_grad)
    normed_grad, gate_up_grad_one, down_grad_one = feed_backward(
        encoder_feed_rows,
        encoder_gate_up,
        encoder_down,
        gate_up_one,
        hidden_one,
        gather_grads(last_grad),
    )
    input_part, gain_one = normalize_backward(
        encoder_middle, scale_feed, norm_gains[1], scatter_grads(normed_grad)
    )
    middle_enc_grad = last_grad + input_part
    normed_grad, enc_in_grad, enc_out_grad, table_one = self_backward(
        encoder_attention_rows,
        encoder_attention_in,
        encoder_attention_out,
        projected_one,
        attended_one,
        totals_one,
        encoder_segments,
        position_tables[0],
        "encoder",
        gather_grads(middle_enc_grad),
    )
    input_part, gain_zero = normalize_backward(
        encoder_input, scale_attention, norm_gains[0], scatter_grads(normed_grad)
    )
    encoder_rows_gradient = middle_enc_grad + input_part
    gains_local = jnp.stack([gain_zero, gain_one, gain_two, gain_three, gain_four, gain_five])
    gains_total = lax.psum(gains_local, ("dp", "tensor"))
    every_sum = lax.psum(
        (
            enc_in_grad,
            enc_out_grad,
            gate_up_grad_one,
            down_grad_one,
            table_one,
            self_in_grad,
            self_out_grad,
            cross_queries_grad,
            cross_pairs_grad,
            cross_output_grad,
            gate_up_grad_two,
            down_grad_two,
            table_two,
        ),
        "dp",
    )
    encoder_sums = every_sum[:5]
    decoder_sums = every_sum[5:]
    return (
        encoder_result,
        decoder_result,
        encoder_rows_gradient,
        decoder_rows_gradient,
        gains_total,
        encoder_sums[0],
        encoder_sums[1],
        encoder_sums[2],
        encoder_sums[3],
        decoder_sums[0],
        decoder_sums[1],
        decoder_sums[2],
        decoder_sums[3],
        decoder_sums[4],
        decoder_sums[5],
        decoder_sums[6],
        jnp.stack([encoder_sums[4], decoder_sums[7]]),
    )


def solution(mesh):
    return jax.shard_map(
        local,
        mesh=mesh,
        in_specs=(
            P(("dp", "tensor"), None),
            P(("dp", "tensor"), None),
            P("dp", None),
            P("dp", None),
            P(),
            P(None, None, "tensor"),
            P("tensor", None),
            P(None, None, "tensor"),
            P("tensor", None),
            P(None, None, "tensor"),
            P("tensor", None),
            P(None, "tensor"),
            P(None, None, "tensor"),
            P("tensor", None),
            P(None, None, "tensor"),
            P("tensor", None),
            P(None, None, "tensor"),
            P(("dp", "tensor"), None),
            P(("dp", "tensor"), None),
        ),
        out_specs=(
            P(("dp", "tensor"), None),
            P(("dp", "tensor"), None),
            P(("dp", "tensor"), None),
            P(("dp", "tensor"), None),
            P(),
            P(None, None, "tensor"),
            P("tensor", None),
            P(None, None, "tensor"),
            P("tensor", None),
            P(None, None, "tensor"),
            P("tensor", None),
            P(None, "tensor"),
            P(None, None, "tensor"),
            P("tensor", None),
            P(None, None, "tensor"),
            P("tensor", None),
            P(None, None, "tensor"),
        ),
        check_vma=False,
    )
```

profile of v0, /device:TPU:0, one launch (start us, length us, event | category | flops | bytes accessed | tf_op | source)
XLA Modules:
  0.0 6254.5 jit_solution(10414866356194300201)
XLA Ops:
  18.9 7.9 gather_fusion.1
  28.4 1897.3 %gather_fusion.3 = f32[524288,3]{1,0:T(8,128)} fusion(f32[3,2047]{0,1:T(8,128)S(1)} %select_bitcast_fusion, s32[524288]{0:T(1024)} %broadcast_clamp_fusion), kind=kCustom, calls=%fused_computation.5.clone | custom fusion | bytes 14680064 | tf_op jit(solution)/shard_map/while/body/eval_jaxpr/jit(_take)/gather | solution.py:79
  1925.7 140.0 %copy.82 = f32[512,1024,3]{1,0,2:T(8,128)} copy(f32[512,1024,3]{2,1,0:T(8,128)} %bitcast.15) | data formatting | bytes 12582912 | tf_op jit(solution)/shard_map/while/body/eval_jaxpr/jit(_take)/gather | solution.py:79
  2065.8 1897.3 %gather_fusion.2 = f32[524288,3]{1,0:T(8,128)} fusion(f32[3,2047]{0,1:T(8,128)S(1)} %select_bitcast_fusion, s32[524288]{0:T(1024)} %broadcast_clamp_fusion.1), kind=kCustom, calls=%fused_computation.1.clone | custom fusion | bytes 14680064 | tf_op jit(solution)/shard_map/while/body/eval_jaxpr/jit(_take)/gather | solution.py:79
  3963.1 140.1 %copy.81 = f32[512,1024,3]{1,0,2:T(8,128)} copy(f32[512,1024,3]{2,1,0:T(8,128)} %bitcast.10) | data formatting | bytes 12582912 | tf_op jit(solution)/shard_map/while/body/eval_jaxpr/jit(_take)/gather | solution.py:79
  4106.7 3.1 fusion.174
  4128.5 40.7 reduce-scatter.12.cloned.1.call-done
  4174.9 8.3 all_gather.35
  4187.7 4.0 gather_fusion.4
  4193.1 3.2 fusion.45
  4205.0 949.1 %gather_fusion.5 = f32[262144,3]{1,0:T(8,128)} fusion(f32[3,1023]{0,1:T(8,128)S(1)} %select_bitcast_fusion.1, s32[262144]{0:T(1024)} %broadcast_clamp_fusion.2), kind=kCustom, calls=%fused_computation.3.clone | custom fusion | bytes 7340032 | tf_op jit(solution)/shard_map/while/body/eval_jaxpr/jit(_take)/gather | solution.py:79
  5154.0 71.3 %copy.60 = f32[512,512,3]{0,1,2:T(8,128)} copy(f32[512,512,3]{2,1,0:T(8,128)} %bitcast.31) | data formatting | bytes 6291456 | tf_op jit(solution)/shard_map/while/body/eval_jaxpr/jit(_take)/gather | solution.py:79
  5226.0 3.3 select_reduce_fusion.3
  5238.7 26.1 reduce-scatter.16.cloned.1.call-done
  5266.6 8.2 all_gather.37
  5277.0 9.5 all-gather.10.cloned.1.call-done
  5297.2 9.0 all_gather.39
  5306.2 19.2 reduce-scatter.18.cloned.1.call-done
  5326.7 8.3 all_gather.38
  5343.6 3.0 fusion.181
  5346.7 25.5 reduce-scatter.22.cloned.1.call-done
  5374.0 29.8 reduce-scatter.20.cloned.1.call-done
  5405.9 8.4 all_gather.40
  5416.1 4.6 multiply_reduce_fusion.2
  5429.8 38.5 reduce-scatter.24.cloned.1.call-done
  5472.9 3.0 convolution_convert_fusion.4
  5478.2 14.5 all-gather.12.cloned.1.call-done
  5492.7 5.0 fusion.91
  5499.0 3.5 convolution_bitcast_fusion.1
  5502.6 8.8 gather_fusion.6
  5511.5 8.8 gather_fusion.7
  5520.4 4.4 gather_fusion
  5528.1 9.0 all_gather.43
  5545.7 3.0 fusion.187
  5548.8 4.3 fusion.102
  5560.7 4.8 copy.94
  5569.3 7.3 pad_convert_fusion.2
  5576.6 14.7 reshape.495
  5591.4 3.5 reduce_sum.308
  5602.9 3.6 fusion.184
  5606.6 4.0 fusion.43
  5610.5 7.6 all-gather.14.cloned.1.call-done
  5620.3 6.0 multiply_reduce_fusion.1
  5626.5 4.2 multiply_reduce_fusion
  5630.7 8.0 multiply_convert_fusion
  5638.7 4.6 pad_bitcast_fusion.1
  5648.9 9.0 copy.92
  5657.9 3.1 fusion.76
  5664.6 3.1 convolution_bitcast_fusion
  5667.8 8.4 pad_convert_fusion.1
  5676.6 6.7 copy.93
  5683.5 2.8 fusion.183
  5688.6 8.0 pad_convert_fusion
  5696.6 13.3 reshape.618
  5709.9 17.6 reshape.493
  5727.5 4.5 reduce_sum.306
  5732.0 13.3 reshape.620
  5745.3 16.9 reshape.494
  5762.2 4.6 reduce_sum.307
  5767.6 22.2 all-reduce.6
  5791.9 44.4 psum.98
  5838.7 389.6 %all-reduce.10.cloned.1.call-done = (f32[768,3,192]{0,2,1:T(8,128)}, f32[192,768]{1,0:T(8,128)}, f32[768,2,512]{2,0,1:T(8,128)}, f32[512,768]{1,0:T(8,128)}, f32...) async-done(((f32[768,3,192]{0,2,1:T(8,128)}, ...) | async-done | bytes 16515088 | tf_op jit(solution)/shard_map/psum | solution.py:532
  6228.3 6.1 copy.71
  6234.4 4.1 copy.72
  (501 shorter events, 172.1 us)
Async XLA Ops:
  7.2 4185.9 %copy-start = (bf16[768,2,512]{2,1,0:T(2,128)(2,1)S(1)}, bf16[768,2,512]{2,1,0:T(2,128)(2,1)}, u32[]{:S(2)}) copy-start(bf16[768,2,512]{2,1,0:T(2,128)(2,1)} %param.36) | copy-start | bytes 4718596
  7.2 4099.5 %all-gather.6.cloned.1.call-start = ((), (), s32[]{:S(2)}) async-start(), calls=%async_computation.11 | async-start | bytes 1966080 | tf_op jit(solution)/shard_map/all_gather | solution.py:300
  13.0 4156.2 %reduce-scatter.12.cloned.1.call-start = ((), (), s32[]{:S(2)}) async-start(), calls=%async_computation.12 | async-start | bytes 3932160 | tf_op jit(solution)/shard_map/reduce_scatter | solution.py:304
  3963.1 141.0 %copy-start.120 = (s32[1,1024]{1,0:T(1,128)S(1)}, s32[1,1024]{1,0:T(1,128)}, u32[]{:S(2)}) copy-start(s32[1,1024]{1,0:T(1,128)} %param.31) | copy-start | bytes 12292
  3963.1 141.0 %copy-start.114 = (s32[512]{0:T(512)S(1)}, s32[512]{0:T(512)}, u32[]{:S(2)}) copy-start(s32[512]{0:T(512)} %copy-done.113) | copy-start | bytes 6148
  3963.1 142.6 %copy-start.112 = (s32[1,512]{1,0:T(1,128)S(1)}, s32[1,512]{1,0:T(1,128)}, u32[]{:S(2)}) copy-start(s32[1,512]{1,0:T(1,128)} %param.32) | copy-start | bytes 6148
  4106.7 8.4 copy-start.15
  4106.7 16.8 copy-start.13
  4110.1 13.4 copy-start.17
  4126.1 43.1 copy-start.21
  4128.4 42.8 copy-start.104
  4128.4 45.4 copy-start.98
  4128.5 64.6 %all-gather.8.cloned.1.call-start = ((), (), s32[]{:S(2)}) async-start(), calls=%async_computation.13 | async-start | bytes 1966080 | tf_op jit(solution)/shard_map/all_gather | solution.py:300
  4170.6 1064.9 %copy-start.11 = (f32[256,768]{1,0:T(8,128)}, f32[256,768]{1,0:T(8,128)S(1)}, u32[]{:S(2)}) copy-start(f32[256,768]{1,0:T(8,128)S(1)} %get-tuple-element.234) | copy-start | bytes 2359300
  4171.2 15.0 copy-start.121
  4172.1 14.1 copy-start.123
  4172.1 1063.4 %reduce-scatter.14.cloned.1.call-start = ((), (), s32[]{:S(2)}) async-start(), calls=%async_computation.14 | async-start | bytes 3932160 | tf_op jit(solution)/shard_map/reduce_scatter | solution.py:304
  4173.8 12.6 copy-start.124
  4202.6 1062.2 %reduce-scatter.16.cloned.1.call-start = ((), (), s32[]{:S(2)}) async-start(), calls=%async_computation.15 | async-start | bytes 1966080 | tf_op jit(solution)/shard_map/reduce_scatter | solution.py:304
  5235.2 29.6 copy-start.38
  5235.2 31.2 copy-start.100
  5235.3 51.3 all-gather.10.cloned.1.call-start
  5237.4 51.5 copy-start.115
  5238.6 86.8 %reduce-scatter.18.cloned.1.call-start = ((), (), s32[]{:S(2)}) async-start(), calls=%async_computation.17 | async-start | bytes 1966080 | tf_op jit(solution)/shard_map/reduce_scatter | solution.py:304
  5266.4 22.5 copy-start.126
  5294.9 31.7 copy-start.103
  5297.1 75.2 %reduce-scatter.22.cloned.1.call-start = ((), (), s32[]{:S(2)}) async-start(), calls=%async_computation.19 | async-start | bytes 1966080 | tf_op jit(solution)/shard_map/reduce_scatter | solution.py:312
  5326.5 11.7 copy-start.45
  5326.5 11.7 copy-start.73
  5343.6 60.2 reduce-scatter.20.cloned.1.call-start
  5346.6 121.6 %reduce-scatter.24.cloned.1.call-start = ((), (), s32[]{:S(2)}) async-start(), calls=%async_computation.20 | async-start | bytes 3932160 | tf_op jit(solution)/shard_map/reduce_scatter | solution.py:474
  5403.7 12.3 copy-start.36
  5414.3 6.3 slice-start.4
  5429.7 38.6 copy-start.20
  5429.7 43.2 copy-start.37
  5429.7 63.0 %all-gather.12.cloned.1.call-start = ((), (), s32[]{:S(2)}) async-start(), calls=%async_computation.21 | async-start | bytes 1966080 | tf_op jit(solution)/shard_map/all_gather | solution.py:308
  5472.9 52.0 reduce-scatter.30.cloned.1.call-start
  5475.9 16.8 copy-start.84
  5478.2 87.3 %reduce-scatter.26.cloned.1.call-start = ((), (), s32[]{:S(2)}) async-start(), calls=%async_computation.22 | async-start | bytes 3932160 | tf_op jit(solution)/shard_map/reduce_scatter | solution.py:312
  5502.6 96.8 %reduce-scatter.32.cloned.1.call-start = ((), (), s32[]{:S(2)}) async-start(), calls=%async_computation.26 | async-start | bytes 1966080 | tf_op jit(solution)/shard_map/reduce_scatter | solution.py:312
  5524.8 12.3 copy-start.66
  5524.8 13.2 copy-start.34
  5524.9 13.1 copy-start.8
  5545.5 72.6 %all-gather.14.cloned.1.call-start = ((), (), s32[]{:S(2)}) async-start(), calls=%async_computation.23 | async-start | bytes 1966080 | tf_op jit(solution)/shard_map/all_gather | solution.py:308
  5560.6 6.2 copy-start.47
  5560.6 6.2 copy-start.129
  5569.3 221.2 %reduce-scatter.28.cloned.1.call-start = ((), (), s32[]{:S(2)}) async-start(), calls=%async_computation.24 | async-start | bytes 3932160 | tf_op jit(solution)/shard_map/reduce_scatter | solution.py:312
  5595.4 7.6 copy-start.24
  5600.6 5.9 copy-start.61
  5610.5 9.8 copy-start.14
  5610.5 9.8 copy-start.18
  5620.3 6.1 slice-start.2
  5620.3 6.1 slice-start.3
  5620.3 6.2 copy-start.16
  5667.7 560.6 %all-reduce.10.cloned.1.call-start = ((), (), s32[]{:S(2)}) async-start(), calls=%async_computation.27 | async-start | bytes 33030144 | tf_op jit(solution)/shard_map/psum | solution.py:532
  5667.8 8.4 copy-start.5
  5676.6 6.7 copy-start.55
  5676.6 6.9 copy-start.42
  5762.2 28.2 copy-start.22
  5762.2 28.2 copy-start.97
  5762.2 28.2 copy-start.117
  5762.2 74.1 %copy-start.46 = (f32[256,768]{1,0:T(8,128)S(1)}, f32[256,768]{1,0:T(8,128)}, u32[]{:S(2)}) copy-start(f32[256,768]{1,0:T(8,128)} %get-tuple-element.222) | copy-start | bytes 2359300
  5762.2 74.1 %copy-start.128 = (f32[256]{0:T(256)S(1)}, f32[256]{0:T(256)}, u32[]{:S(2)}) copy-start(f32[256]{0:T(256)} %get-tuple-element.250) | copy-start | bytes 3076
  6228.3 6.1 copy-start.44
  (101 other events, 291.6 us)
Sparse Core Ops, SparseCore 0:
  13.1 22.3 all-gather.5
  4128.6 40.6 reduce-scatter.11
  4172.2 19.8 all-gather.7
  4202.7 39.1 reduce-scatter.13
  5235.4 29.3 reduce-scatter.15
  5266.9 19.6 all-gather.9
  5297.2 28.1 reduce-scatter.17
  5343.7 28.5 reduce-scatter.21
  5375.5 28.1 reduce-scatter.19
  5429.8 38.3 reduce-scatter.23
  5473.0 19.6 all-gather.11
  5495.8 28.1 reduce-scatter.29
  5527.1 37.9 reduce-scatter.25
  5568.2 28.1 reduce-scatter.31
  5598.4 19.6 all-gather.13
  5667.8 37.9 reduce-scatter.27
  5714.3 513.9 all-reduce.9
where the time goes:
time: 6360 us; the launch traced here: 6250 us
  local copies, waits for them, and re-layouts  5280 us (83%)
  waiting for transfers between devices  601 us (9%)
  matrix products  134 us (2%)
  blocking collectives  118 us (2%)
  other arithmetic  106 us (2%)
    gather x6, local copies, waits for them, and re-layouts, block_scores(): scores = scores + jnp.take(bias_line, offset_index, axis=1)  5100 us
    psum x1, waiting for transfers between devices, local(): lax.psum((enc_in_grad, enc_out_grad, gate_up_grad_one, down_grad_one, tab...  390 us
  transfers between devices with their start and end apart: 17, of which 10 were waited for; matrix products, arithmetic and copies ran while one was open for 86% of the time, Pallas kernels for 0%

commit v1 on v0

v1 whole, which is shorter than its diff:
```python
import functools, math
import jax
import jax.numpy as jnp
from jax import lax
from jax.experimental import pallas as pl
from jax.experimental.pallas import tpu as pltpu
from jax.sharding import PartitionSpec as P

BUCKETS = 32
EPS = 1e-06
NEG = -1e30
VMEM_BYTES = 56 * 2**20


def bucket_limits(exact_range, far_range, bucket_count):
    limits = []
    for level_index in range(1, bucket_count - exact_range):
        candidate = exact_range
        while (int(math.log(candidate / exact_range) / math.log(far_range / exact_range) * (bucket_count - exact_range)) < level_index):
            candidate += 1
        limits.append(candidate)
    return limits

def side_starts(count):
    exact = count // 2
    return list(range(exact + 1)) + bucket_limits(exact, 128, count)

def bucket_ranges(kind):
    far = 1 << 20
    if kind == "encoder":
        starts = side_starts(BUCKETS // 2)
        ends = [s - 1 for s in starts[1:]] + [far]
        left = [(b, -ends[b], -starts[b]) for b in range(len(starts))][::-1]
        right = [(BUCKETS // 2 + b, starts[b], ends[b]) for b in range(1, len(starts))]
        return left + right
    starts = side_starts(BUCKETS)
    ends = [s - 1 for s in starts[1:]] + [far]
    return [(b, -ends[b], -starts[b]) for b in range(len(starts))][::-1]

def head_mask(shape, head, size):
    lane = lax.broadcasted_iota(jnp.int32, shape, 1)
    return (lane >= head * size) & (lane < (head + 1) * size)

def fill_strip(strip, table, kind, block, length):
    heads = strip.shape[0]
    offset = length - block
    ranges = bucket_ranges(kind)
    low, high = offset - 128, offset + block + 128
    width = strip.shape[2]
    lo, hi = max(low, 0), min(high, width)
    r = (lax.broadcasted_iota(jnp.int32, (block, hi - lo), 1) + (lo - offset)
         - lax.broadcasted_iota(jnp.int32, (block, hi - lo), 0))
    masks = [r >= first for _, first, _ in ranges[1:]]
    for head in range(heads):
        value = jnp.full((block, hi - lo), table[ranges[0][0], head], jnp.float32)
        for mask, (bucket, _, _) in zip(masks, ranges[1:]):
            value = jnp.where(mask, table[bucket, head], value)
        if kind == "decoder":
            value = jnp.where(r > 0, NEG, value)
        strip[head, :, lo:hi] = value
        if lo > 0:
            strip[head, :, 0:lo] = jnp.full((block, lo), table[ranges[0][0], head], jnp.float32)
        if hi < width:
            strip[head, :, hi:] = jnp.full((block, width - hi), NEG if kind == "decoder" else table[ranges[-1][0], head], jnp.float32)

def nt(a, b):
    return lax.dot_general(a, b, (((1,), (1,)), ((), ())), preferred_element_type=jnp.float32)
def tn(a, b):
    return lax.dot_general(a, b, (((0,), (0,)), ((), ())), preferred_element_type=jnp.float32)
def nn(a, b):
    return lax.dot_general(a, b, (((1,), (0,)), ((), ())), preferred_element_type=jnp.float32)

def strip_slice(place, block, length):
    return pl.ds(pl.multiple_of((length - block) - place * block, 128), length)

def forward_kernel(kind, heads, size, chunk, places, q, k, v, seg_q, seg_k, *rest):
    if kind == "cross":
        table = strip = None
        out, totals, scores, probs = rest
    else:
        table, out, totals, scores, probs, strip = rest
    block, length = q.shape[0], k.shape[0]
    step = pl.program_id(0)
    if strip is not None:
        @pl.when(step == 0)
        def _():
            fill_strip(strip, table, kind, block, length)
        window = strip_slice(places[step], block, length)
    total = jnp.zeros((block, heads * size), jnp.float32)
    queries = q[...]
    for head in range(heads):
        mask = head_mask(queries.shape, head, size)
        scores[head] = nt(jnp.where(mask, queries, 0).astype(jnp.bfloat16), k[...])

        def rows_step(index, carry):
            rows = pl.ds(index * chunk, chunk)
            s = scores[head, rows, :]
            if strip is not None:
                s = s + strip[head, rows, window]
            s = jnp.where(seg_q[rows, :] == seg_k[...], s, NEG)
            peak = jnp.max(s, axis=-1, keepdims=True)
            e = jnp.exp(s - peak)
            weight = jnp.sum(e, axis=-1, keepdims=True)
            probs[head, rows, :] = (e * (1.0 / weight)).astype(jnp.bfloat16)
            lane = lax.broadcasted_iota(jnp.int32, (chunk, 128), 1)
            here = peak + jnp.log(weight)
            if head == 0:
                totals[rows, :] = jnp.broadcast_to(here, (chunk, 128))
            else:
                totals[rows, :] = jnp.where(lane == head, here, totals[rows, :])
            return carry
        [rows_step(index, 0) for index in range(block // chunk)]
        total += jnp.where(mask, nn(probs[head], v[...]), 0.0)
    out[...] = total.astype(jnp.bfloat16)

def backward_kernel(kind, heads, size, chunk, key_block, places, q, k, v, seg_q, seg_k, dout, totals, *rest):
    if kind == "cross":
        table = strip = gsum = table_grad = None
        dq, dk, dv, scores, dprobs, probs, dscores, dk_sum, dv_sum = rest
    else:
        table, dq, dk, dv, table_grad, scores, dprobs, probs, dscores, dk_sum, dv_sum, strip, gsum = rest
    block, length = q.shape[0], k.shape[0]
    step = pl.program_id(0)
    steps = pl.num_programs(0)

    @pl.when(step == 0)
    def _():
        dk_sum[...] = jnp.zeros_like(dk_sum)
        dv_sum[...] = jnp.zeros_like(dv_sum)
        if strip is not None:
            gsum[...] = jnp.zeros_like(gsum)
            fill_strip(strip, table, kind, block, length)
    if strip is not None:
        window = strip_slice(places[step], block, length)
    total = jnp.zeros((block, heads * size), jnp.float32)
    queries = q[...]
    grads = dout[...]
    for head in range(heads):
        mask = head_mask(queries.shape, head, size)
        query = jnp.where(mask, queries, 0).astype(jnp.bfloat16)
        grad = jnp.where(mask, grads, 0).astype(jnp.bfloat16)
        scores[head] = nt(query, k[...])
        dprobs[head] = nt(grad, v[...])

        def rows_step(index, carry):
            rows = pl.ds(index * chunk, chunk)
            s = scores[head, rows, :]
            if strip is not None:
                s = s + strip[head, rows, window]
            s = jnp.where(seg_q[rows, :] == seg_k[...], s, NEG)
            p = jnp.exp(s - totals[rows, head:head + 1])
            probs[head, rows, :] = p.astype(jnp.bfloat16)
            dp = dprobs[head, rows, :]
            delta = jnp.sum(p * dp, axis=-1, keepdims=True)
            ds = (p * (dp - delta)).astype(jnp.bfloat16)
            dscores[head, rows, :] = ds
            if strip is not None:
                gsum[head, rows, window] += ds.astype(jnp.float32)
            return carry
        [rows_step(index, 0) for index in range(block // chunk)]
        ds = dscores[head]
        total += jnp.where(mask, nn(ds, k[...]), 0.0)
        dk_sum[...] += tn(ds, query)
        dv_sum[...] += tn(probs[head], grad)
    dq[...] = total.astype(jnp.bfloat16)

    @pl.when(step == steps - 1)
    def _():
        for index in range(length // key_block):
            rows = pl.ds(pl.multiple_of(places[index] * key_block, key_block), key_block)
            to = pl.ds(index * key_block, key_block)
            dk[to, :] = dk_sum[rows, :].astype(jnp.bfloat16)
            dv[to, :] = dv_sum[rows, :].astype(jnp.bfloat16)
        if strip is not None:
            table_grad[...] = bucket_sums(gsum, kind, block, length)

def bucket_sums(gsum, kind, block, length):
    heads, _, width = gsum.shape
    offset = length - block
    lo, hi = offset - 128, min(offset + block + 128, width)
    wide = block + 512
    lines = []
    for head in range(heads):
        left = None
        if lo < 0:
            g = jnp.concatenate([jnp.zeros((block, -lo), jnp.float32), gsum[head, :, 0:hi]], axis=1)
        else:
            g = gsum[head, :, lo:hi]
            if lo > 0:
                left = jnp.sum(jnp.sum(gsum[head, :, 0:lo], axis=0, keepdims=True), axis=1, keepdims=True)
        right = None
        if hi < width:
            right = jnp.sum(jnp.sum(gsum[head, :, hi:], axis=0, keepdims=True), axis=1, keepdims=True)
        g = jnp.concatenate([g, jnp.zeros((block, wide - g.shape[1]), jnp.float32)], axis=1)
        half = block // 2
        while half >= 1:
            g = g[:half] + pltpu.roll(g[half:], wide - half, 1)
            half //= 2
        lane = lax.broadcasted_iota(jnp.int32, (1, wide), 1)
        if left is not None:
            g = g + jnp.where(lane == 0, left, 0.0)
        if right is not None:
            g = g + jnp.where(lane == 256, right, 0.0)
        lines.append(g)
    line = jnp.concatenate(lines + [jnp.zeros((8 - heads, wide), jnp.float32)], axis=0)
    at = lax.broadcasted_iota(jnp.int32, (wide, 128), 0)
    r = jnp.where(at > block + 255, at - wide, at) - 128
    lane = lax.broadcasted_iota(jnp.int32, (1, 128), 1)
    first = jnp.full((1, 128), 1 << 24, jnp.int32)
    last = jnp.full((1, 128), -(1 << 24), jnp.int32)
    for bucket, a, b in bucket_ranges(kind):
        first = jnp.where(lane == bucket, a, first)
        last = jnp.where(lane == bucket, b, last)
    member = jnp.where((r >= first) & (r <= last), 1.0, 0.0)
    return lax.dot_general(line, member, (((1,), (0,)), ((), ())), precision=lax.Precision.HIGHEST, preferred_element_type=jnp.float32)

def attention_forward(kind, heads, places, q, k, v, seg_q, seg_k, table, block, chunk=32):
    n = places.shape[0]
    length, inner = k.shape
    size = inner // heads
    full = lambda shape: pl.BlockSpec(shape, lambda i, p: (0, 0))
    at = lambda cols: pl.BlockSpec((block, cols), lambda i, p: (p[i], 0))
    put = lambda cols: pl.BlockSpec((block, cols), lambda i, p: (i, 0))
    ins = [at(inner), full((length, inner)), full((length, inner)), at(1), full((1, length))]
    args = [q, k, v, seg_q, seg_k]
    scratch = [pltpu.VMEM((heads, block, length), jnp.float32), pltpu.VMEM((heads, block, length), jnp.bfloat16)]
    if kind != "cross":
        ins.append(pl.BlockSpec(memory_space=pltpu.SMEM)); args.append(table)
        scratch.append(pltpu.VMEM((heads, block, 2 * length - block), jnp.float32))
    return pl.pallas_call(
        functools.partial(forward_kernel, kind, heads, size, chunk),
        grid_spec=pltpu.PrefetchScalarGridSpec(num_scalar_prefetch=1, grid=(n,), in_specs=ins,
            out_specs=[put(inner), put(128)], scratch_shapes=scratch),
        out_shape=[jax.ShapeDtypeStruct((n * block, inner), jnp.bfloat16), jax.ShapeDtypeStruct((n * block, 128), jnp.float32)],
        cost_estimate=pl.CostEstimate(flops=n * block * length * heads * 64 * 4 * 4, bytes_accessed=n * block * inner * 8, transcendentals=n * block * length * heads),
        compiler_params=pltpu.CompilerParams(dimension_semantics=("arbitrary",), vmem_limit_bytes=VMEM_BYTES),
        name="attention_forward_" + kind,
    )(places, *args)

def attention_backward(kind, heads, places, q, k, v, seg_q, seg_k, dout, totals, table, block, key_block, chunk=32):
    n = places.shape[0]
    length, inner = k.shape
    size = inner // heads
    full = lambda shape: pl.BlockSpec(shape, lambda i, p: (0, 0))
    at = lambda cols: pl.BlockSpec((block, cols), lambda i, p: (p[i], 0))
    put = lambda cols: pl.BlockSpec((block, cols), lambda i, p: (i, 0))
    ins = [at(inner), full((length, inner)), full((length, inner)), at(1), full((1, length)), put(inner), put(128)]
    args = [q, k, v, seg_q, seg_k, dout, totals]
    outs = [put(inner), full((length, inner)), full((length, inner))]
    shapes = [jax.ShapeDtypeStruct((n * block, inner), jnp.bfloat16), jax.ShapeDtypeStruct((length, inner), jnp.bfloat16), jax.ShapeDtypeStruct((length, inner), jnp.bfloat16)]
    scratch = [pltpu.VMEM((heads, block, length), jnp.float32)] * 2 + [pltpu.VMEM((heads, block, length), jnp.bfloat16)] * 2 + [pltpu.VMEM((length, inner), jnp.float32)] * 2
    if kind != "cross":
        ins.append(pl.BlockSpec(memory_space=pltpu.SMEM)); args.append(table)
        outs.append(full((8, 128))); shapes.append(jax.ShapeDtypeStruct((8, 128), jnp.float32))
        scratch += [pltpu.VMEM((heads, block, 2 * length - block), jnp.float32)] * 2
    return pl.pallas_call(
        functools.partial(backward_kernel, kind, heads, size, chunk, key_block),
        grid_spec=pltpu.PrefetchScalarGridSpec(num_scalar_prefetch=1, grid=(n,), in_specs=ins, out_specs=outs, scratch_shapes=scratch),
        out_shape=shapes,
        cost_estimate=pl.CostEstimate(flops=n * block * length * heads * 64 * 4 * 10, bytes_accessed=n * block * inner * 16, transcendentals=n * block * length * heads),
        compiler_params=pltpu.CompilerParams(dimension_semantics=("arbitrary",), vmem_limit_bytes=VMEM_BYTES),
        name="attention_backward_" + kind,
    )(places, *args)


def normalize(residual, gain_row):
    scale_row = lax.rsqrt(jnp.mean(residual * residual, axis=-1, keepdims=True) + EPS)
    return (residual * scale_row * gain_row, scale_row)


def normalize_backward(residual, scale_row, gain_row, normed_grad):
    weighted = normed_grad * gain_row
    inner_mean = jnp.mean(residual * weighted, axis=-1, keepdims=True)
    input_grad = scale_row * weighted - residual * scale_row**3 * inner_mean
    gain_grad = jnp.sum(normed_grad * residual * scale_row, axis=0)
    return (input_grad, gain_grad)


CORE = [(0, 1), (1, 0), (2, 3), (3, 2)]
CHIP = [(0, 2), (2, 0), (1, 3), (3, 1)]


def swap_core(value):
    return lax.ppermute(value, "tensor", CORE)


def swap_chip(value):
    return lax.ppermute(value, "tensor", CHIP)


def gather_rows(rows):
    across = swap_chip(rows)
    near = jnp.concatenate([rows, swap_core(rows)], axis=0)
    far = jnp.concatenate([across, swap_core(across)], axis=0)
    return near, far


def scatter_rows(near, far):
    half = near.shape[0] // 2
    sent = far[:half] + swap_core(far[half:])
    across = swap_chip(sent.astype(jnp.bfloat16))
    return near[:half] + swap_core(near[half:]) + across.astype(jnp.float32)


def reduce_pieces(grad, size):
    place = lax.axis_index("dp")
    bits = [1 << bit for bit in range(size.bit_length() - 1)]
    current = grad
    for bit in bits:
        upper = (place // bit) % 2
        half = current.shape[0] // 2
        send = lax.dynamic_slice_in_dim(current, (1 - upper) * half, half, 0)
        keep = lax.dynamic_slice_in_dim(current, upper * half, half, 0)
        came = lax.ppermute(send, "dp", [(i, i ^ bit) for i in range(size)])
        current = (keep.astype(jnp.float32) + came.astype(jnp.float32)).astype(jnp.bfloat16)
    for bit in bits[::-1]:
        upper = (place // bit) % 2 == 1
        came = lax.ppermute(current, "dp", [(i, i ^ bit) for i in range(size)])
        current = jnp.concatenate([jnp.where(upper, came, current), jnp.where(upper, current, came)], axis=0)
    return current


def sum_all(value, size, axes):
    for axis, count in axes:
        bit = 1
        while bit < count:
            value = value + lax.ppermute(value, axis, [(i, i ^ bit) for i in range(count)])
            bit *= 2
    return value


def dot_nt(a, b):
    return lax.dot_general(a, b, (((1,), (1,)), ((), ())), preferred_element_type=jnp.float32)


def dot_nn(a, b):
    return lax.dot_general(a, b, (((1,), (0,)), ((), ())), preferred_element_type=jnp.float32)


def dot_tn(a, b):
    return lax.dot_general(a, b, (((0,), (0,)), ((), ())), preferred_element_type=jnp.float32)


def both(pair, function):
    return function(pair[0]), function(pair[1])


def to_order(value, places, block):
    out = jnp.zeros_like(value)
    for index in range(4):
        out = lax.dynamic_update_slice_in_dim(out, value[index * block:(index + 1) * block], places[index] * block, 0)
    return out


def low(value):
    return value.astype(jnp.bfloat16)


def feed_forward(normed, gate_up, down):
    gu = both(normed, lambda a: dot_nn(a, gate_up))
    hidden = both(gu, lambda x: low(jax.nn.gelu(x[:, :x.shape[1] // 2]) * x[:, x.shape[1] // 2:]))
    part = both(hidden, lambda h: dot_nn(h, down))
    return scatter_rows(*part), gu, hidden


def feed_backward(normed, gate_up, down, gu, hidden, grads):
    def one(index):
        hidden_grad = dot_nt(grads[index], down)
        gate, up = jnp.split(gu[index], 2, axis=1)
        activated, pullback = jax.vjp(jax.nn.gelu, gate)
        gate_grad = pullback(hidden_grad * up)[0]
        return low(jnp.concatenate([gate_grad, hidden_grad * activated], axis=1))
    stacked = one(0), one(1)
    normed_grad = scatter_rows(*both(stacked, lambda s: dot_nt(s, gate_up)))
    join = lambda pair: jnp.concatenate(pair, axis=0)
    rows, cols = join(normed), join(stacked)
    gate_up_grad = low(dot_tn(rows, cols))
    down_grad = low(dot_tn(join(hidden), join(grads)))
    return normed_grad, gate_up_grad, down_grad


def local(
    sizes,
    encoder_rows,
    decoder_rows,
    encoder_segments,
    decoder_segments,
    norm_gains,
    encoder_attention_in,
    encoder_attention_out,
    encoder_gate_up,
    encoder_down,
    decoder_attention_in,
    decoder_attention_out,
    cross_queries,
    cross_key_value_rows,
    cross_output,
    decoder_gate_up,
    decoder_down,
    position_tables,
    encoder_cotangent,
    decoder_cotangent,
):
    dp = sizes["dp"]
    heads = position_tables.shape[2]
    inner = cross_output.shape[0]
    width = encoder_rows.shape[1]
    eb, db = encoder_rows.shape[0], decoder_rows.shape[0]
    t = lax.axis_index("tensor").astype(jnp.int32)
    places = jnp.bitwise_xor(t, jnp.arange(4, dtype=jnp.int32))
    weight_in = lambda w: jnp.transpose(w, (1, 2, 0)).reshape(-1, width)
    enc_in, dec_in, kv_in = weight_in(encoder_attention_in), weight_in(decoder_attention_in), weight_in(cross_key_value_rows)
    q_in = jnp.transpose(cross_queries)
    enc_gu = encoder_gate_up.reshape(width, -1)
    dec_gu = decoder_gate_up.reshape(width, -1)
    enc_seg_k, dec_seg_k = encoder_segments, decoder_segments
    enc_seg_q, dec_seg_q = jnp.transpose(encoder_segments), jnp.transpose(decoder_segments)
    join = lambda pair: jnp.concatenate(pair, axis=0)

    def project(pair, weight, block):
        rows = join(pair)
        return [to_order(low(dot_nt(rows, weight[i:i + inner])), places, block) for i in range(0, weight.shape[0], inner)]

    def out_part(attended, weight):
        half = attended.shape[0] // 2
        return scatter_rows(dot_nn(attended[:half], weight), dot_nn(attended[half:], weight))

    x = encoder_rows.astype(jnp.float32)
    y = decoder_rows.astype(jnp.float32)
    normed, enc_s0 = normalize(x, norm_gains[0])
    enc_a0 = gather_rows(low(normed))
    normed, dec_s3 = normalize(y, norm_gains[3])
    dec_a3 = gather_rows(low(normed))
    qkv1 = project(enc_a0, enc_in, eb)
    att1, tot1 = attention_forward("encoder", heads, places, *qkv1, enc_seg_q, enc_seg_k, position_tables[0], eb, chunk=64)
    h = x + out_part(att1, encoder_attention_out)
    normed, enc_s1 = normalize(h, norm_gains[1])
    enc_a1 = gather_rows(low(normed))
    qkv2 = project(dec_a3, dec_in, db)
    att2, tot2 = attention_forward("decoder", heads, places, *qkv2, dec_seg_q, dec_seg_k, position_tables[1], db, chunk=db)
    part, gu1, hid1 = feed_forward(enc_a1, enc_gu, encoder_down)
    e = h + part
    normed, enc_s2 = normalize(e, norm_gains[2])
    encoder_result = low(normed)
    enc_r = gather_rows(encoder_result)
    m = y + out_part(att2, decoder_attention_out)
    normed, dec_s4 = normalize(m, norm_gains[4])
    dec_a4 = gather_rows(low(normed))
    cq = project(dec_a4, q_in, db)[0]
    ck, cv = project(enc_r, kv_in, eb)
    att3, tot3 = attention_forward("cross", heads, places, cq, ck, cv, dec_seg_q, enc_seg_k, None, db, chunk=db)
    n = m + out_part(att3, cross_output)
    normed, dec_s5 = normalize(n, norm_gains[5])
    dec_a5 = gather_rows(low(normed))
    part, gu2, hid2 = feed_forward(dec_a5, dec_gu, decoder_down)
    decoder_result = low(n + part)

    result_grad = decoder_cotangent.astype(jnp.float32)
    grads = gather_rows(decoder_cotangent)
    normed_grad, dec_gu_grad, dec_down_grad = feed_backward(dec_a5, dec_gu, decoder_down, gu2, hid2, grads)
    part, gain5 = normalize_backward(n, dec_s5, norm_gains[5], normed_grad)
    later_grad = result_grad + part
    grads = gather_rows(low(later_grad))
    co_grad = low(dot_nt(join(grads), cross_output))
    cross_output_grad = low(dot_tn(att3, join(grads)))
    dcq, dck, dcv = attention_backward("cross", heads, places, cq, ck, cv, dec_seg_q, enc_seg_k, co_grad, tot3, None, db, eb, chunk=db)
    half = 2 * eb
    kv_grad = jnp.concatenate([dck, dcv], axis=1)
    kv_normed = scatter_rows(dot_nn(kv_grad[:half], kv_in), dot_nn(kv_grad[half:], kv_in))
    q_normed = scatter_rows(dot_nn(dcq[:2 * db], q_in), dot_nn(dcq[2 * db:], q_in))
    cross_queries_grad = low(dot_tn(dcq, join(dec_a4)))
    cross_kv_grad = low(dot_tn(kv_grad, join(enc_r)))
    part, gain2 = normalize_backward(e, enc_s2, norm_gains[2], encoder_cotangent.astype(jnp.float32) + kv_normed)
    last_grad = part
    grads = gather_rows(low(last_grad))
    normed_grad, enc_gu_grad, enc_down_grad = feed_backward(enc_a1, enc_gu, encoder_down, gu1, hid1, grads)
    part, gain4 = normalize_backward(m, dec_s4, norm_gains[4], q_normed)
    middle_grad = later_grad + part
    dec_grads = gather_rows(low(middle_grad))

    def self_backward(kind, grads, weight_in, weight_out, qkv, attended, totals, seg_q, seg_k, table, block, normed, chunk):
        rows = join(grads)
        out_grad = low(dot_nt(rows, weight_out))
        dq, dk, dv, table_grad = attention_backward(kind, heads, places, *qkv, seg_q, seg_k, out_grad, totals, table, block, block, chunk=chunk)
        dqkv = jnp.concatenate([dq, dk, dv], axis=1)
        normed_grad = scatter_rows(dot_nn(dqkv[:2 * block], weight_in), dot_nn(dqkv[2 * block:], weight_in))
        return normed_grad, low(dot_tn(dqkv, join(normed))), low(dot_tn(attended, rows)), table_grad[:heads, :BUCKETS]

    part, gain1 = normalize_backward(h, enc_s1, norm_gains[1], normed_grad)
    h_grad = last_grad + part
    grads = gather_rows(low(h_grad))
    normed_grad, dec_in_grad, dec_out_grad, dec_table = self_backward(
        "decoder", dec_grads, dec_in, decoder_attention_out, qkv2, att2, tot2, dec_seg_q, dec_seg_k, position_tables[1], db, dec_a3, db)
    part, gain3 = normalize_backward(y, dec_s3, norm_gains[3], normed_grad)
    decoder_rows_gradient = middle_grad + part
    normed_grad, enc_in_grad, enc_out_grad, enc_table = self_backward(
        "encoder", grads, enc_in, encoder_attention_out, qkv1, att1, tot1, enc_seg_q, enc_seg_k, position_tables[0], eb, enc_a0, 64)
    part, gain0 = normalize_backward(x, enc_s0, norm_gains[0], normed_grad)
    encoder_rows_gradient = h_grad + part

    wide = lambda a: a.astype(jnp.float32)
    total = functools.partial(reduce_pieces, size=dp)
    dec_gu_sum, dec_down_sum = wide(total(dec_gu_grad)), wide(total(dec_down_grad))
    cross = total(jnp.concatenate([cross_output_grad, cross_queries_grad, cross_kv_grad], axis=0))
    enc_gu_sum, enc_down_sum = wide(total(enc_gu_grad)), wide(total(enc_down_grad))
    dec_att = total(jnp.concatenate([dec_out_grad, dec_in_grad], axis=0))
    enc_att = total(jnp.concatenate([enc_out_grad, enc_in_grad], axis=0))
    gains = jnp.stack([gain0, gain1, gain2, gain3, gain4, gain5])
    gains = sum_all(gains, None, [("tensor", 4)])
    tables = jnp.stack([enc_table, dec_table])
    small = jnp.concatenate([gains.reshape(-1), tables.reshape(-1)])
    small = sum_all(small, None, [("dp", dp)])
    gains = small[:gains.size].reshape(gains.shape)
    tables = small[gains.size:].reshape(tables.shape)
    unfold = lambda g, parts: jnp.transpose(wide(g).reshape(parts, inner, width), (2, 0, 1))
    return (
        encoder_result,
        decoder_result,
        encoder_rows_gradient,
        decoder_rows_gradient,
        gains,
        unfold(enc_att[inner:], 3),
        wide(enc_att[:inner]),
        enc_gu_sum.reshape(encoder_gate_up.shape),
        enc_down_sum,
        unfold(dec_att[inner:], 3),
        wide(dec_att[:inner]),
        jnp.transpose(wide(cross[inner:2 * inner])),
        unfold(cross[2 * inner:], 2),
        wide(cross[:inner]),
        dec_gu_sum.reshape(decoder_gate_up.shape),
        dec_down_sum,
        jnp.transpose(tables, (0, 2, 1)),
    )


def solution(mesh):
    return jax.shard_map(
        functools.partial(local, dict(mesh.shape)),
        mesh=mesh,
        in_specs=(
            P(("dp", "tensor"), None),
            P(("dp", "tensor"), None),
            P("dp", None),
            P("dp", None),
            P(),
            P(None, None, "tensor"),
            P("tensor", None),
            P(None, None, "tensor"),
            P("tensor", None),
            P(None, None, "tensor"),
            P("tensor", None),
            P(None, "tensor"),
            P(None, None, "tensor"),
            P("tensor", None),
            P(None, None, "tensor"),
            P("tensor", None),
            P(None, None, "tensor"),
            P(("dp", "tensor"), None),
            P(("dp", "tensor"), None),
        ),
        out_specs=(
            P(("dp", "tensor"), None),
            P(("dp", "tensor"), None),
            P(("dp", "tensor"), None),
            P(("dp", "tensor"), None),
            P(),
            P(None, None, "tensor"),
            P("tensor", None),
            P(None, None, "tensor"),
            P("tensor", None),
            P(None, None, "tensor"),
            P("tensor", None),
            P(None, "tensor"),
            P(None, None, "tensor"),
            P("tensor", None),
            P(None, None, "tensor"),
            P("tensor", None),
            P(None, None, "tensor"),
        ),
        check_vma=False,
    )
```

time: 6360 us -> 560 us (0.09); the launches traced: 6250 us -> 552 us
  local copies, waits for them, and re-layouts: 5280 us -> 55.7 us
  waiting for transfers between devices: 601 us -> 190 us
  blocking collectives: 118 us -> 0 us
  starting transfers between devices: 0.88 us -> 92.8 us
  matrix products: 134 us -> 51.7 us
  Pallas kernels: 0 us -> 78.6 us
    gather x11 -> x0, local copies, waits for them, and re-layouts: 5130 us -> none  [the longest x6 5100 us: block_scores(): scores = scores + jnp.take(bias_line, offset_index, axis=1)]
    psum x1 -> x0, waiting for transfers between devices: 390 us -> none  [local(): lax.psum((enc_in_grad, enc_out_grad, gate_up_grad_one, down_grad_one, tab...]
    ppermute x0 -> x113, waiting for transfers between devices: none -> 190 us  [the longest x21 69.2 us: reduce_pieces(): came = lax.ppermute(send, 'dp', [(i, i ^ bit) for i in range(size)])]
    reduce_scatter x11 -> x0, waiting for transfers between devices: 180 us -> none  [the longest x5 116 us: scatter_rows(): lax.psum_scatter(partial_rows, 'tensor', scatter_dimension=0, tiled=True)]
    ppermute x0 -> x113, starting transfers between devices: none -> 92.8 us  [the longest x21 29.3 us: reduce_pieces(): came = lax.ppermute(send, 'dp', [(i, i ^ bit) for i in range(size)])]
    pallas_call x0 -> x6, Pallas kernels: none -> 78.6 us  [the longest x3 47.3 us: attention_backward(): pl.pallas_call(functools.partial(backward_kernel, kind, heads, size, chun...]
    unnamed x320 -> x344, local copies, waits for them, and re-layouts: 97.3 us -> 24.1 us
    dot_general x54 -> x53, matrix products: 120 us -> 51.7 us  [the longest x20 23.1 us: dot_nt(): lax.dot_general(a, b, (((1,), (1,)), ((), ())), preferred_element_type=jn...]
  transfers between devices with their start and end apart: 17 -> 113, of which waited for: 10 -> 44; matrix products, arithmetic and copies ran while one was open for 86% -> 26% of each run, Pallas kernels for 0% -> 10%
where the time goes in v1:
time: 560 us; the launch traced here: 552 us
  waiting for transfers between devices  190 us (34%)
  starting transfers between devices  92.8 us (17%)
  Pallas kernels  78.6 us (14%)
  other arithmetic  73.5 us (13%)
  local copies, waits for them, and re-layouts  55.7 us (10%)
  matrix products  51.7 us (9%)
  between operations  9.32 us (2%)
    ppermute x21, waiting for transfers between devices, reduce_pieces(): came = lax.ppermute(send, 'dp', [(i, i ^ bit) for i in range(size)])  69.2 us
    ppermute x22, waiting for transfers between devices, swap_chip(): return lax.ppermute(value, 'tensor', CHIP)  62.5 us
    ppermute x21, waiting for transfers between devices, reduce_pieces(): came = lax.ppermute(current, 'dp', [(i, i ^ bit) for i in range(size)])  50 us
    pallas_call x3, Pallas kernels, attention_backward(): pl.pallas_call(functools.partial(backward_kernel, kind, heads, size, chun...  47.3 us
    pallas_call x3, Pallas kernels, attention_forward(): pl.pallas_call(functools.partial(forward_kernel, kind, heads, size, chunk...  31.4 us
    ppermute x21, starting transfers between devices, reduce_pieces(): came = lax.ppermute(send, 'dp', [(i, i ^ bit) for i in range(size)])  29.3 us
    ppermute x22, starting transfers between devices, swap_chip(): return lax.ppermute(value, 'tensor', CHIP)  25.4 us
    unnamed x344, local copies, waits for them, and re-layouts  24.1 us
  transfers between devices with their start and end apart: 113, of which 44 were waited for; matrix products, arithmetic and copies ran while one was open for 26% of the time, Pallas kernels for 10%

profile of v1, /device:TPU:0, one launch (start us, length us, event | category | flops | bytes accessed | tf_op | source)
XLA Modules:
  0.0 551.8 jit_solution(5868296395114271162)
XLA Ops:
  5.3 3.0 collective-permute-start.1
  17.5 4.1 collective-permute-done.13
  34.3 2.0 convolution_convert_fusion.7
  37.3 12.4 %attention_forward_encoder.1 = (bf16[1024,192]{1,0:T(8,128)(2,1)}, f32[1024,128]{1,0:T(8,128)}) custom-call(s32[4]{0:T(128)} %copy-done.99, bf16[1024,192]{1,0:T(8,128)(2,1)} %copy-done.53, bf16[1024,192]{1,0:T(8,128)(2,1)} %copy-done.54, bf16[1024,192]{1,0:T(8,128)(2,1)} %copy-done.55, s32[1024,1]{1,0:T(8,128)} %copy.86.seg_q, s32[1,1024]{1,0:T(1,128)} %seg_k.10, ...), custom_call_target="tpu_custom_call" | custom-call | flops 3221225472 | bytes 1572864 | tf_op jit(solution)/shard_map/attention_forward_encoder/pallas_call | solution.py:230
  52.2 8.7 %attention_forward_decoder.1 = (bf16[512,192]{1,0:T(8,128)(2,1)}, f32[512,128]{1,0:T(8,128)}) custom-call(s32[4]{0:T(128)} %copy-done.99, bf16[512,192]{1,0:T(8,128)(2,1)} %copy-done.74, bf16[512,192]{1,0:T(8,128)(2,1)} %copy-done.76, bf16[512,192]{1,0:T(8,128)(2,1)} %copy-done.75, s32[512,1]{1,0:T(8,128)} %copy.91.seg_q, s32[1,512]{1,0:T(1,128)} %seg_k.11, ...), custom_call_target="tpu_custom_call" | custom-call | flops 805306368 | bytes 786432 | tf_op jit(solution)/shard_map/attention_forward_decoder/pallas_call | solution.py:230
  66.2 8.4 %collective-permute-done.5 = bf16[256,768]{1,0:T(8,128)(2,1)S(1)} collective-permute-done((bf16[256,768]{1,0:T(8,128)(2,1)S(1)}, bf16[256,768]{1,0:T(8,128)(2,1)S(1)}, u32[]{:S(2)}, u32[]{:S(2)}) %collective-permute-start.5) | collective-permute-done | bytes 393248 | tf_op jit(solution)/shard_map/ppermute | solution.py:288
  79.0 7.7 %collective-permute-done.8 = bf16[256,768]{1,0:T(8,128)(2,1)S(1)} collective-permute-done((bf16[256,768]{1,0:T(8,128)(2,1)S(1)}, bf16[256,768]{1,0:T(8,128)(2,1)S(1)}, u32[]{:S(2)}, u32[]{:S(2)}) %collective-permute-start.8) | collective-permute-done | bytes 393248 | tf_op jit(solution)/shard_map/ppermute | solution.py:288
  101.1 8.7 %collective-permute-done.11 = bf16[256,768]{1,0:T(8,128)(2,1)S(1)} collective-permute-done((bf16[256,768]{1,0:T(8,128)(2,1)S(1)}, bf16[256,768]{1,0:T(8,128)(2,1)S(1)}, u32[]{:S(2)}, u32[]{:S(2)}) %collective-permute-start.11) | collective-permute-done | bytes 393248 | tf_op jit(solution)/shard_map/ppermute | solution.py:288
  111.5 9.8 %collective-permute-done.22 = bf16[256,768]{1,0:T(8,128)(2,1)S(1)} collective-permute-done((bf16[256,768]{1,0:T(8,128)(2,1)S(1)}, bf16[256,768]{1,0:T(8,128)(2,1)S(1)}, u32[]{:S(2)}, u32[]{:S(2)}) %collective-permute-start.22) | collective-permute-done | bytes 393248 | tf_op jit(solution)/shard_map/ppermute | solution.py:288
  126.2 10.3 %attention_forward_cross.1 = (bf16[512,192]{1,0:T(8,128)(2,1)}, f32[512,128]{1,0:T(8,128)}) custom-call(s32[4]{0:T(128)} %copy-done.99, bf16[512,192]{1,0:T(8,128)(2,1)} %copy-done.73, bf16[1024,192]{1,0:T(8,128)(2,1)} %copy-done.52, bf16[1024,192]{1,0:T(8,128)(2,1)} %copy-done.56, s32[512,1]{1,0:T(8,128)} %copy.91.seg_q, s32[1,1024]{1,0:T(1,128)} %seg_k.10), custom_call_target="tpu_custom_call" | custom-call | flops 1610612736 | bytes 786432 | tf_op jit(solution)/shard_map/attention_forward_cross/pallas_call | solution.py:230
  141.6 5.7 %collective-permute-done.26 = bf16[128,768]{1,0:T(8,128)(2,1)S(1)} collective-permute-done((bf16[128,768]{1,0:T(8,128)(2,1)S(1)}, bf16[128,768]{1,0:T(8,128)(2,1)S(1)}, u32[]{:S(2)}, u32[]{:S(2)}) %collective-permute-start.26) | collective-permute-done | bytes 196640 | tf_op jit(solution)/shard_map/ppermute | solution.py:288
  149.3 3.0 copy.124
  152.7 2.2 fusion.175
  157.7 2.1 collective-permute-done.29
  168.6 2.0 convolution_convert_fusion
  171.3 7.7 %collective-permute-done.107 = bf16[256,768]{1,0:T(8,128)(2,1)S(1)} collective-permute-done((bf16[256,768]{1,0:T(8,128)(2,1)S(1)}, bf16[256,768]{1,0:T(8,128)(2,1)S(1)}, u32[]{:S(2)}, u32[]{:S(2)}) %collective-permute-start.107) | collective-permute-done | bytes 393248 | tf_op jit(solution)/shard_map/ppermute | solution.py:314
  181.2 4.0 collective-permute-done.108
  187.0 2.7 collective-permute-start.109
  190.9 2.0 fusion.246
  195.2 2.7 collective-permute-start.110
  201.4 2.1 collective-permute-done.110
  207.6 15.4 %attention_backward_cross.1 = (bf16[512,192]{1,0:T(8,128)(2,1)}, bf16[1024,192]{1,0:T(8,128)(2,1)}, bf16[1024,192]{1,0:T(8,128)(2,1)}) custom-call(s32[4]{0:T(128)} %copy-done.99, bf16[512,192]{1,0:T(8,128)(2,1)} %copy-done.73, bf16[1024,192]{1,0:T(8,128)(2,1)} %copy-done.52, bf16[1024,192]{1,0:T(8,128)(2,1)} %copy-done.56, s32[512,1]{1,0:T(8,128)} %copy.91.seg_q, ...), custom_call_target="tpu_custom_call" | custom-call | flops 4026531840 | bytes 1572864 | tf_op jit(solution)/shard_map/attention_backward_cross/pallas_call | solution.py:256
  235.3 4.7 collective-permute-done.112
  241.7 3.5 collective-permute-start.103
  246.5 7.0 %collective-permute-done.103 = bf16[96,1024]{1,0:T(8,128)(2,1)S(1)} collective-permute-done((bf16[96,1024]{1,0:T(8,128)(2,1)S(1)}, bf16[96,1024]{1,0:T(8,128)(2,1)S(1)}, u32[]{:S(2)}, u32[]{:S(2)}) %collective-permute-start.103) | collective-permute-done | bytes 196640 | tf_op jit(solution)/shard_map/ppermute | solution.py:314
  254.0 6.3 %collective-permute-done.59 = bf16[128,768]{1,0:T(8,128)(2,1)S(1)} collective-permute-done((bf16[128,768]{1,0:T(8,128)(2,1)S(1)}, bf16[128,768]{1,0:T(8,128)(2,1)S(1)}, u32[]{:S(2)}, u32[]{:S(2)}) %collective-permute-start.59) | collective-permute-done | bytes 196640 | tf_op jit(solution)/shard_map/ppermute | solution.py:288
  265.0 2.0 collective-permute-start.105
  269.6 4.0 collective-permute-done.96
  279.1 11.4 %attention_backward_decoder.1 = (bf16[512,192]{1,0:T(8,128)(2,1)}, bf16[512,192]{1,0:T(8,128)(2,1)}, bf16[512,192]{1,0:T(8,128)(2,1)}, f32[8,128]{1,0:T(8,128)}) custom-call(s32[4]{0:T(128)} %copy-done.99, bf16[512,192]{1,0:T(8,128)(2,1)} %copy-done.74, bf16[512,192]{1,0:T(8,128)(2,1)} %copy-done.76, bf16[512,192]{1,0:T(8,128)(2,1)} %copy-done.75, ...), custom_call_target="tpu_custom_call" | custom-call | flops 2013265920 | bytes 1572864 | tf_op jit(solution)/shard_map/attention_backward_decoder/pallas_call | solution.py:256
  300.7 8.0 %collective-permute-done.98 = bf16[96,768]{1,0:T(8,128)(2,1)S(1)} collective-permute-done((bf16[96,768]{1,0:T(8,128)(2,1)S(1)}, bf16[96,768]{1,0:T(8,128)(2,1)S(1)}, u32[]{:S(2)}, u32[]{:S(2)}) %collective-permute-start.98) | collective-permute-done | bytes 147488 | tf_op jit(solution)/shard_map/ppermute | solution.py:318
  313.5 5.2 collective-permute-done.99
  325.5 6.3 %collective-permute-done.65 = bf16[128,768]{1,0:T(8,128)(2,1)S(1)} collective-permute-done((bf16[128,768]{1,0:T(8,128)(2,1)S(1)}, bf16[128,768]{1,0:T(8,128)(2,1)S(1)}, u32[]{:S(2)}, u32[]{:S(2)}) %collective-permute-start.65) | collective-permute-done | bytes 196640 | tf_op jit(solution)/shard_map/ppermute | solution.py:288
  335.6 6.2 %collective-permute-done.106 = bf16[384,1024]{1,0:T(8,128)(2,1)S(1)} collective-permute-done((bf16[384,1024]{1,0:T(8,128)(2,1)S(1)}, bf16[384,1024]{1,0:T(8,128)(2,1)S(1)}, u32[]{:S(2)}, u32[]{:S(2)}) %collective-permute-start.106) | collective-permute-done | bytes 786464 | tf_op jit(solution)/shard_map/ppermute | solution.py:318
  343.3 3.3 concatenate.256
  346.6 3.6 concatenate.255
  350.2 4.8 maximum_convert_fusion.1
  356.2 2.5 fusion.42
  364.3 2.1 fusion.26
  367.5 2.9 collective-permute-start.92
  373.8 16.5 %collective-permute-done.83 = bf16[256,768]{1,0:T(8,128)(2,1)S(1)} collective-permute-done((bf16[256,768]{1,0:T(8,128)(2,1)S(1)}, bf16[256,768]{1,0:T(8,128)(2,1)S(1)}, u32[]{:S(2)}, u32[]{:S(2)}) %collective-permute-start.83) | collective-permute-done | bytes 393248 | tf_op jit(solution)/shard_map/ppermute | solution.py:314
  390.5 2.6 collective-permute-start.84
  393.3 6.7 %collective-permute-done.84 = bf16[128,768]{1,0:T(8,128)(2,1)S(1)} collective-permute-done((bf16[128,768]{1,0:T(8,128)(2,1)S(1)}, bf16[128,768]{1,0:T(8,128)(2,1)S(1)}, u32[]{:S(2)}, u32[]{:S(2)}) %collective-permute-start.84) | collective-permute-done | bytes 196640 | tf_op jit(solution)/shard_map/ppermute | solution.py:314
  401.3 2.7 collective-permute-done.93
  404.1 2.8 collective-permute-done.85
  408.5 4.7 collective-permute-done.86
  415.7 2.0 collective-permute-start.78
  417.7 3.2 collective-permute-done.87
  432.0 3.9 collective-permute-done.79
  438.8 5.8 %collective-permute-done.80 = bf16[96,1024]{1,0:T(8,128)(2,1)S(1)} collective-permute-done((bf16[96,1024]{1,0:T(8,128)(2,1)S(1)}, bf16[96,1024]{1,0:T(8,128)(2,1)S(1)}, u32[]{:S(2)}, u32[]{:S(2)}) %collective-permute-start.80) | collective-permute-done | bytes 196640 | tf_op jit(solution)/shard_map/ppermute | solution.py:318
  448.0 20.5 %attention_backward_encoder.1 = (bf16[1024,192]{1,0:T(8,128)(2,1)}, bf16[1024,192]{1,0:T(8,128)(2,1)}, bf16[1024,192]{1,0:T(8,128)(2,1)}, f32[8,128]{1,0:T(8,128)}) custom-call(s32[4]{0:T(128)} %copy-done.99, bf16[1024,192]{1,0:T(8,128)(2,1)} %copy-done.53, bf16[1024,192]{1,0:T(8,128)(2,1)} %copy-done.54, bf16[1024,192]{1,0:T(8,128)(2,1)} %copy-done.55, ...), custom_call_target="tpu_custom_call" | custom-call | flops 8053063680 | bytes 3145728 | tf_op jit(solution)/shard_map/attention_backward_encoder/pallas_call | solution.py:256
  471.6 2.3 convolution_convert_fusion.2
  478.2 10.2 %collective-permute-done.71 = bf16[384,768]{1,0:T(8,128)(2,1)S(1)} collective-permute-done((bf16[384,768]{1,0:T(8,128)(2,1)S(1)}, bf16[384,768]{1,0:T(8,128)(2,1)S(1)}, u32[]{:S(2)}, u32[]{:S(2)}) %collective-permute-start.71) | collective-permute-done | bytes 589856 | tf_op jit(solution)/shard_map/ppermute | solution.py:314
  492.6 3.1 collective-permute-done.72
  495.9 4.4 collective-permute-start.73
  501.1 3.2 collective-permute-done.73
  505.0 2.0 collective-permute-start.74
  507.7 3.9 collective-permute-done.74
  513.3 3.0 fusion.69
  519.4 4.1 collective-permute-start.67
  523.5 2.4 broadcast_select_fusion.3
  526.5 2.6 concatenate.236
  534.1 3.3 maximum_convert_fusion
  537.4 2.1 collective-permute-start.69
  541.3 2.6 collective-permute-start.70
  (808 shorter events, 211.5 us)
Async XLA Ops:
  5.3 23.0 %collective-permute-start.1 = (bf16[256,768]{1,0:T(8,128)(2,1)S(1)}, bf16[256,768]{1,0:T(8,128)(2,1)}, u32[]{:S(2)}, u32[]{:S(2)}) collective-permute-start(bf16[256,768]{1,0:T(8,128)(2,1)S(1)} %fusion.63), channel_id=1, source_target_pairs={{0,2},{2,0},{1,3},{3,1},{4,6},{6,4},{5,7},{7,5},{8,10},{10,8},{9,1... | collective-permute-start | bytes 1179656 | tf_op jit(solution)/shard_map/ppermute | solution.py:288
  8.3 20.6 %collective-permute-start = (bf16[256,768]{1,0:T(8,128)(2,1)S(1)}, bf16[256,768]{1,0:T(8,128)(2,1)}, u32[]{:S(2)}, u32[]{:S(2)}) collective-permute-start(bf16[256,768]{1,0:T(8,128)(2,1)S(1)} %fusion.63), channel_id=1, source_target_pairs={{0,1},{1,0},{2,3},{3,2},{4,5},{5,4},{6,7},{7,6},{8,9},{9,8},{10,11... | collective-permute-start | bytes 1179656 | tf_op jit(solution)/shard_map/ppermute | solution.py:284
  10.0 11.6 %collective-permute-start.13 = (bf16[128,768]{1,0:T(8,128)(2,1)S(1)}, bf16[128,768]{1,0:T(8,128)(2,1)S(1)}, u32[]{:S(2)}, u32[]{:S(2)}) collective-permute-start(bf16[128,768]{1,0:T(8,128)(2,1)S(1)} %fusion.153), channel_id=1, source_target_pairs={{0,2},{2,0},{1,3},{3,1},{4,6},{6,4},{5,7},{7,5},{8,10},{10,8},{9,1... | collective-permute-start | bytes 589832 | tf_op jit(solution)/shard_map/ppermute | solution.py:288
  10.2 13.7 %collective-permute-start.12 = (bf16[128,768]{1,0:T(8,128)(2,1)S(1)}, bf16[128,768]{1,0:T(8,128)(2,1)S(1)}, u32[]{:S(2)}, u32[]{:S(2)}) collective-permute-start(bf16[128,768]{1,0:T(8,128)(2,1)S(1)} %fusion.153), channel_id=1, source_target_pairs={{0,1},{1,0},{2,3},{3,2},{4,5},{5,4},{6,7},{7,6},{8,9},{9,8},{10,11... | collective-permute-start | bytes 589832 | tf_op jit(solution)/shard_map/ppermute | solution.py:284
  51.1 11.5 %collective-permute-start.4 = (f32[256,768]{1,0:T(8,128)S(1)}, f32[256,768]{1,0:T(8,128)S(1)}, u32[]{:S(2)}, u32[]{:S(2)}) collective-permute-start(f32[256,768]{1,0:T(8,128)S(1)} %slice.629), channel_id=1, source_target_pairs={{0,1},{1,0},{2,3},{3,2},{4,5},{5,4},{6,7},{7,6},{8,9},{9,8},{10,11... | collective-permute-start | bytes 2359304 | tf_op jit(solution)/shard_map/ppermute | solution.py:284
  62.7 12.0 %collective-permute-start.5 = (bf16[256,768]{1,0:T(8,128)(2,1)S(1)}, bf16[256,768]{1,0:T(8,128)(2,1)S(1)}, u32[]{:S(2)}, u32[]{:S(2)}) collective-permute-start(bf16[256,768]{1,0:T(8,128)(2,1)S(1)} %fusion.80), channel_id=1, source_target_pairs={{0,2},{2,0},{1,3},{3,1},{4,6},{6,4},{5,7},{7,5},{8,10},{10,8},{9,1... | collective-permute-start | bytes 1179656 | tf_op jit(solution)/shard_map/ppermute | solution.py:288
  64.7 13.2 %collective-permute-start.15 = (f32[128,768]{1,0:T(8,128)S(1)}, f32[128,768]{1,0:T(8,128)S(1)}, u32[]{:S(2)}, u32[]{:S(2)}) collective-permute-start(f32[128,768]{1,0:T(8,128)S(1)} %slice.654), channel_id=1, source_target_pairs={{0,1},{1,0},{2,3},{3,2},{4,5},{5,4},{6,7},{7,6},{8,9},{9,8},{10,11... | collective-permute-start | bytes 1179656 | tf_op jit(solution)/shard_map/ppermute | solution.py:284
  65.0 13.9 %collective-permute-start.17 = (bf16[128,768]{1,0:T(8,128)(2,1)S(1)}, bf16[128,768]{1,0:T(8,128)(2,1)S(1)}, u32[]{:S(2)}, u32[]{:S(2)}) collective-permute-start(bf16[128,768]{1,0:T(8,128)(2,1)S(1)} %fusion.173), channel_id=1, source_target_pairs={{0,2},{2,0},{1,3},{3,1},{4,6},{6,4},{5,7},{7,5},{8,10},{10,8},{9,1... | collective-permute-start | bytes 589832 | tf_op jit(solution)/shard_map/ppermute | solution.py:288
  75.7 11.0 %collective-permute-start.8 = (bf16[256,768]{1,0:T(8,128)(2,1)S(1)}, bf16[256,768]{1,0:T(8,128)(2,1)S(1)}, u32[]{:S(2)}, u32[]{:S(2)}) collective-permute-start(bf16[256,768]{1,0:T(8,128)(2,1)S(1)} %multiply_convert_fusion.5), channel_id=1, source_target_pairs={{0,2},{2,0},{1,3},{3,1},{4,6},{6,4},{5,7},{7,5},{8,10},{10,8},{9,1... | collective-permute-start | bytes 1179656 | tf_op jit(solution)/shard_map/ppermute | solution.py:288
  87.4 10.6 %collective-permute-start.19 = (bf16[128,768]{1,0:T(8,128)(2,1)S(1)}, bf16[128,768]{1,0:T(8,128)(2,1)S(1)}, u32[]{:S(2)}, u32[]{:S(2)}) collective-permute-start(bf16[128,768]{1,0:T(8,128)(2,1)S(1)} %multiply_convert_fusion.11), channel_id=1, source_target_pairs={{0,2},{2,0},{1,3},{3,1},{4,6},{6,4},{5,7},{7,5},{8,10},{10,8},{9,1... | collective-permute-start | bytes 589832 | tf_op jit(solution)/shard_map/ppermute | solution.py:288
  98.3 11.4 %collective-permute-start.11 = (bf16[256,768]{1,0:T(8,128)(2,1)S(1)}, bf16[256,768]{1,0:T(8,128)(2,1)S(1)}, u32[]{:S(2)}, u32[]{:S(2)}) collective-permute-start(bf16[256,768]{1,0:T(8,128)(2,1)S(1)} %fusion.77), channel_id=1, source_target_pairs={{0,2},{2,0},{1,3},{3,1},{4,6},{6,4},{5,7},{7,5},{8,10},{10,8},{9,1... | collective-permute-start | bytes 1179656 | tf_op jit(solution)/shard_map/ppermute | solution.py:288
  110.7 10.6 %collective-permute-start.22 = (bf16[256,768]{1,0:T(8,128)(2,1)S(1)}, bf16[256,768]{1,0:T(8,128)(2,1)S(1)}, u32[]{:S(2)}, u32[]{:S(2)}) collective-permute-start(bf16[256,768]{1,0:T(8,128)(2,1)S(1)} %multiply_convert_fusion.4), channel_id=1, source_target_pairs={{0,2},{2,0},{1,3},{3,1},{4,6},{6,4},{5,7},{7,5},{8,10},{10,8},{9,1... | collective-permute-start | bytes 1179656 | tf_op jit(solution)/shard_map/ppermute | solution.py:288
  111.4 10.0 %collective-permute-start.21 = (bf16[256,768]{1,0:T(8,128)(2,1)S(1)}, bf16[256,768]{1,0:T(8,128)(2,1)S(1)}, u32[]{:S(2)}, u32[]{:S(2)}) collective-permute-start(bf16[256,768]{1,0:T(8,128)(2,1)S(1)} %multiply_convert_fusion.4), channel_id=1, source_target_pairs={{0,1},{1,0},{2,3},{3,2},{4,5},{5,4},{6,7},{7,6},{8,9},{9,8},{10,11... | collective-permute-start | bytes 1179656 | tf_op jit(solution)/shard_map/ppermute | solution.py:284
  140.0 12.4 %collective-permute-start.35 = (bf16[128,768]{1,0:T(8,128)(2,1)}, bf16[128,768]{1,0:T(8,128)(2,1)}, u32[]{:S(2)}, u32[]{:S(2)}) collective-permute-start(bf16[128,768]{1,0:T(8,128)(2,1)} %param.37), channel_id=1, source_target_pairs={{0,2},{2,0},{1,3},{3,1},{4,6},{6,4},{5,7},{7,5},{8,10},{10,8},{9,1... | collective-permute-start | bytes 589832 | tf_op jit(solution)/shard_map/ppermute | solution.py:288
  157.5 29.5 %collective-permute-start.34 = (f32[128,768]{1,0:T(8,128)S(1)}, f32[128,768]{1,0:T(8,128)S(1)}, u32[]{:S(2)}, u32[]{:S(2)}) collective-permute-start(f32[128,768]{1,0:T(8,128)S(1)} %slice.684), channel_id=1, source_target_pairs={{0,1},{1,0},{2,3},{3,2},{4,5},{5,4},{6,7},{7,6},{8,9},{9,8},{10,11... | collective-permute-start | bytes 1179656 | tf_op jit(solution)/shard_map/ppermute | solution.py:284
  160.2 29.7 %collective-permute-start.28 = (f32[128,768]{1,0:T(8,128)S(1)}, f32[128,768]{1,0:T(8,128)S(1)}, u32[]{:S(2)}, u32[]{:S(2)}) collective-permute-start(f32[128,768]{1,0:T(8,128)S(1)} %slice.678), channel_id=1, source_target_pairs={{0,1},{1,0},{2,3},{3,2},{4,5},{5,4},{6,7},{7,6},{8,9},{9,8},{10,11... | collective-permute-start | bytes 1179656 | tf_op jit(solution)/shard_map/ppermute | solution.py:284
  164.8 14.7 %collective-permute-start.31 = (f32[128,768]{1,0:T(8,128)S(1)}, f32[128,768]{1,0:T(8,128)S(1)}, u32[]{:S(2)}, u32[]{:S(2)}) collective-permute-start(f32[128,768]{1,0:T(8,128)S(1)} %slice.682), channel_id=1, source_target_pairs={{0,1},{1,0},{2,3},{3,2},{4,5},{5,4},{6,7},{7,6},{8,9},{9,8},{10,11... | collective-permute-start | bytes 1179656 | tf_op jit(solution)/shard_map/ppermute | solution.py:284
  167.0 12.0 %collective-permute-start.107 = (bf16[256,768]{1,0:T(8,128)(2,1)S(1)}, bf16[256,768]{1,0:T(8,128)(2,1)S(1)}, u32[]{:S(2)}, u32[]{:S(2)}) collective-permute-start(bf16[256,768]{1,0:T(8,128)(2,1)S(1)} %constant_dynamic-slice_fusion.2), channel_id=1, source_target_pairs={{0,4},{4,0},{8,12},{12,8},{16,20},{20,16},{24,28},{28,24},{1,5},{5... | collective-permute-start | bytes 1179656 | tf_op jit(solution)/shard_map/ppermute | solution.py:314
  170.7 27.2 %collective-permute-start.101 = (bf16[384,1024]{1,0:T(8,128)(2,1)S(1)}, bf16[384,1024]{1,0:T(8,128)(2,1)S(1)}, u32[]{:S(2)}, u32[]{:S(2)}) collective-permute-start(bf16[384,1024]{1,0:T(8,128)(2,1)S(1)} %constant_dynamic-slice_fusion.5), channel_id=1, source_target_pairs={{0,4},{4,0},{8,12},{12,8},{16,20},{20,16},{24,28},{28,24},{1,5},{5... | collective-permute-start | bytes 2359304 | tf_op jit(solution)/shard_map/ppermute | solution.py:314
  179.0 10.7 %collective-permute-start.38 = (bf16[128,768]{1,0:T(8,128)(2,1)S(1)}, bf16[128,768]{1,0:T(8,128)(2,1)S(1)}, u32[]{:S(2)}, u32[]{:S(2)}) collective-permute-start(bf16[128,768]{1,0:T(8,128)(2,1)S(1)} %fusion.164), channel_id=1, source_target_pairs={{0,2},{2,0},{1,3},{3,1},{4,6},{6,4},{5,7},{7,5},{8,10},{10,8},{9,1... | collective-permute-start | bytes 589832 | tf_op jit(solution)/shard_map/ppermute | solution.py:288
  194.6 10.4 %collective-permute-start.39 = (bf16[128,768]{1,0:T(8,128)(2,1)S(1)}, bf16[128,768]{1,0:T(8,128)(2,1)S(1)}, u32[]{:S(2)}, u32[]{:S(2)}) collective-permute-start(bf16[128,768]{1,0:T(8,128)(2,1)S(1)} %get-tuple-element.112), channel_id=1, source_target_pairs={{0,1},{1,0},{2,3},{3,2},{4,5},{5,4},{6,7},{7,6},{8,9},{9,8},{10,11... | collective-permute-start | bytes 589832 | tf_op jit(solution)/shard_map/ppermute | solution.py:284
  199.8 33.5 %collective-permute-start.102 = (bf16[192,1024]{1,0:T(8,128)(2,1)}, bf16[192,1024]{1,0:T(8,128)(2,1)}, u32[]{:S(2)}, u32[]{:S(2)}) collective-permute-start(bf16[192,1024]{1,0:T(8,128)(2,1)} %constant_dynamic-slice_fusion.4), channel_id=1, source_target_pairs={{0,8},{4,12},{8,0},{12,4},{16,24},{20,28},{24,16},{28,20},{1,9},{5... | collective-permute-start | bytes 1179656 | tf_op jit(solution)/shard_map/ppermute | solution.py:314
  204.3 23.4 %collective-permute-start.111 = (bf16[128,768]{1,0:T(8,128)(2,1)}, bf16[128,768]{1,0:T(8,128)(2,1)}, u32[]{:S(2)}, u32[]{:S(2)}) collective-permute-start(bf16[128,768]{1,0:T(8,128)(2,1)} %pad_maximum_fusion.29), channel_id=1, source_target_pairs={{0,8},{4,12},{8,0},{12,4},{16,24},{20,28},{24,16},{28,20},{1,9},{5... | collective-permute-start | bytes 589832 | tf_op jit(solution)/shard_map/ppermute | solution.py:318
  225.5 39.5 %collective-permute-start.43 = (f32[256,768]{1,0:T(8,128)S(1)}, f32[256,768]{1,0:T(8,128)S(1)}, u32[]{:S(2)}, u32[]{:S(2)}) collective-permute-start(f32[256,768]{1,0:T(8,128)S(1)} %slice.694), channel_id=1, source_target_pairs={{0,1},{1,0},{2,3},{3,2},{4,5},{5,4},{6,7},{7,6},{8,9},{9,8},{10,11... | collective-permute-start | bytes 2359304 | tf_op jit(solution)/shard_map/ppermute | solution.py:284
  226.8 82.5 %collective-permute-start.42 = (f32[256,768]{1,0:T(8,128)}, f32[256,768]{1,0:T(8,128)}, u32[]{:S(2)}, u32[]{:S(2)}) collective-permute-start(f32[256,768]{1,0:T(8,128)} %slice.690), channel_id=1, source_target_pairs={{0,1},{1,0},{2,3},{3,2},{4,5},{5,4},{6,7},{7,6},{8,9},{9,8},{10,11... | collective-permute-start | bytes 2359304 | tf_op jit(solution)/shard_map/ppermute | solution.py:284
  227.3 14.4 %collective-permute-start.58 = (f32[128,768]{1,0:T(8,128)S(1)}, f32[128,768]{1,0:T(8,128)S(1)}, u32[]{:S(2)}, u32[]{:S(2)}) collective-permute-start(f32[128,768]{1,0:T(8,128)S(1)} %slice.708), channel_id=1, source_target_pairs={{0,1},{1,0},{2,3},{3,2},{4,5},{5,4},{6,7},{7,6},{8,9},{9,8},{10,11... | collective-permute-start | bytes 1179656 | tf_op jit(solution)/shard_map/ppermute | solution.py:284
  228.8 11.3 %collective-permute-start.112 = (bf16[256,768]{1,0:T(8,128)(2,1)S(1)}, bf16[256,768]{1,0:T(8,128)(2,1)S(1)}, u32[]{:S(2)}, u32[]{:S(2)}) collective-permute-start(bf16[256,768]{1,0:T(8,128)(2,1)S(1)} %pad_maximum_fusion.22), channel_id=1, source_target_pairs={{0,4},{4,0},{8,12},{12,8},{16,20},{20,16},{24,28},{28,24},{1,5},{5... | collective-permute-start | bytes 1179656 | tf_op jit(solution)/shard_map/ppermute | solution.py:318
  233.4 20.6 %collective-permute-start.57 = (f32[128,768]{1,0:T(8,128)S(1)}, f32[128,768]{1,0:T(8,128)S(1)}, u32[]{:S(2)}, u32[]{:S(2)}) collective-permute-start(f32[128,768]{1,0:T(8,128)S(1)} %slice.706), channel_id=1, source_target_pairs={{0,1},{1,0},{2,3},{3,2},{4,5},{5,4},{6,7},{7,6},{8,9},{9,8},{10,11... | collective-permute-start | bytes 1179656 | tf_op jit(solution)/shard_map/ppermute | solution.py:284
  240.1 21.8 %collective-permute-start.95 = (bf16[384,768]{1,0:T(8,128)(2,1)S(1)}, bf16[384,768]{1,0:T(8,128)(2,1)S(1)}, u32[]{:S(2)}, u32[]{:S(2)}) collective-permute-start(bf16[384,768]{1,0:T(8,128)(2,1)S(1)} %constant_dynamic-slice_fusion.8), channel_id=1, source_target_pairs={{0,4},{4,0},{8,12},{12,8},{16,20},{20,16},{24,28},{28,24},{1,5},{5... | collective-permute-start | bytes 1769480 | tf_op jit(solution)/shard_map/ppermute | solution.py:314
  241.7 11.9 %collective-permute-start.103 = (bf16[96,1024]{1,0:T(8,128)(2,1)S(1)}, bf16[96,1024]{1,0:T(8,128)(2,1)S(1)}, u32[]{:S(2)}, u32[]{:S(2)}) collective-permute-start(bf16[96,1024]{1,0:T(8,128)(2,1)S(1)} %constant_dynamic-slice_fusion.3), channel_id=1, source_target_pairs={{0,16},{4,20},{8,24},{12,28},{16,0},{20,4},{24,8},{28,12},{1,17},{... | collective-permute-start | bytes 589832 | tf_op jit(solution)/shard_map/ppermute | solution.py:314
  261.8 12.5 %collective-permute-start.60 = (bf16[128,768]{1,0:T(8,128)(2,1)S(1)}, bf16[128,768]{1,0:T(8,128)(2,1)S(1)}, u32[]{:S(2)}, u32[]{:S(2)}) collective-permute-start(bf16[128,768]{1,0:T(8,128)(2,1)S(1)} %get-tuple-element.104), channel_id=1, source_target_pairs={{0,1},{1,0},{2,3},{3,2},{4,5},{5,4},{6,7},{7,6},{8,9},{9,8},{10,11... | collective-permute-start | bytes 589832 | tf_op jit(solution)/shard_map/ppermute | solution.py:284
  265.0 30.5 %collective-permute-start.105 = (bf16[192,1024]{1,0:T(8,128)(2,1)}, bf16[192,1024]{1,0:T(8,128)(2,1)}, u32[]{:S(2)}, u32[]{:S(2)}) collective-permute-start(bf16[192,1024]{1,0:T(8,128)(2,1)} %pad_maximum_fusion.21), channel_id=1, source_target_pairs={{0,8},{4,12},{8,0},{12,4},{16,24},{20,28},{24,16},{28,20},{1,9},{5... | collective-permute-start | bytes 1179656 | tf_op jit(solution)/shard_map/ppermute | solution.py:318
  267.9 43.0 %collective-permute-start.44 = (bf16[256,768]{1,0:T(8,128)(2,1)}, bf16[256,768]{1,0:T(8,128)(2,1)}, u32[]{:S(2)}, u32[]{:S(2)}) collective-permute-start(bf16[256,768]{1,0:T(8,128)(2,1)} %fusion.74), channel_id=1, source_target_pairs={{0,2},{2,0},{1,3},{3,1},{4,6},{6,4},{5,7},{7,5},{8,10},{10,8},{9,1... | collective-permute-start | bytes 1179656 | tf_op jit(solution)/shard_map/ppermute | solution.py:288
  274.3 23.3 %collective-permute-start.97 = (bf16[96,768]{1,0:T(8,128)(2,1)}, bf16[96,768]{1,0:T(8,128)(2,1)}, u32[]{:S(2)}, u32[]{:S(2)}) collective-permute-start(bf16[96,768]{1,0:T(8,128)(2,1)} %constant_dynamic-slice_fusion.6), channel_id=1, source_target_pairs={{0,16},{4,20},{8,24},{12,28},{16,0},{20,4},{24,8},{28,12},{1,17},{... | collective-permute-start | bytes 442376 | tf_op jit(solution)/shard_map/ppermute | solution.py:314
  292.9 20.5 %collective-permute-start.64 = (f32[128,768]{1,0:T(8,128)S(1)}, f32[128,768]{1,0:T(8,128)S(1)}, u32[]{:S(2)}, u32[]{:S(2)}) collective-permute-start(f32[128,768]{1,0:T(8,128)S(1)} %slice.714), channel_id=1, source_target_pairs={{0,1},{1,0},{2,3},{3,2},{4,5},{5,4},{6,7},{7,6},{8,9},{9,8},{10,11... | collective-permute-start | bytes 1179656 | tf_op jit(solution)/shard_map/ppermute | solution.py:284
  295.5 29.5 %collective-permute-start.63 = (f32[128,768]{1,0:T(8,128)S(1)}, f32[128,768]{1,0:T(8,128)S(1)}, u32[]{:S(2)}, u32[]{:S(2)}) collective-permute-start(f32[128,768]{1,0:T(8,128)S(1)} %slice.711), channel_id=1, source_target_pairs={{0,1},{1,0},{2,3},{3,2},{4,5},{5,4},{6,7},{7,6},{8,9},{9,8},{10,11... | collective-permute-start | bytes 1179656 | tf_op jit(solution)/shard_map/ppermute | solution.py:284
  298.5 10.2 %collective-permute-start.98 = (bf16[96,768]{1,0:T(8,128)(2,1)S(1)}, bf16[96,768]{1,0:T(8,128)(2,1)S(1)}, u32[]{:S(2)}, u32[]{:S(2)}) collective-permute-start(bf16[96,768]{1,0:T(8,128)(2,1)S(1)} %add_convert_fusion.16), channel_id=1, source_target_pairs={{0,16},{4,20},{8,24},{12,28},{16,0},{20,4},{24,8},{28,12},{1,17},{... | collective-permute-start | bytes 442376 | tf_op jit(solution)/shard_map/ppermute | solution.py:318
  308.7 24.0 %collective-permute-start.89 = (bf16[384,768]{1,0:T(8,128)(2,1)S(1)}, bf16[384,768]{1,0:T(8,128)(2,1)S(1)}, u32[]{:S(2)}, u32[]{:S(2)}) collective-permute-start(bf16[384,768]{1,0:T(8,128)(2,1)S(1)} %fusion.116), channel_id=1, source_target_pairs={{0,4},{4,0},{8,12},{12,8},{16,20},{20,16},{24,28},{28,24},{1,5},{5... | collective-permute-start | bytes 1769480 | tf_op jit(solution)/shard_map/ppermute | solution.py:314
  309.3 32.5 %collective-permute-start.106 = (bf16[384,1024]{1,0:T(8,128)(2,1)S(1)}, bf16[384,1024]{1,0:T(8,128)(2,1)S(1)}, u32[]{:S(2)}, u32[]{:S(2)}) collective-permute-start(bf16[384,1024]{1,0:T(8,128)(2,1)S(1)} %pad_maximum_fusion.14), channel_id=1, source_target_pairs={{0,4},{4,0},{8,12},{12,8},{16,20},{20,16},{24,28},{28,24},{1,5},{5... | collective-permute-start | bytes 2359304 | tf_op jit(solution)/shard_map/ppermute | solution.py:318
  318.7 15.8 %collective-permute-start.47 = (bf16[256,768]{1,0:T(8,128)(2,1)S(1)}, bf16[256,768]{1,0:T(8,128)(2,1)}, u32[]{:S(2)}, u32[]{:S(2)}) collective-permute-start(bf16[256,768]{1,0:T(8,128)(2,1)S(1)} %fusion.238), channel_id=1, source_target_pairs={{0,2},{2,0},{1,3},{3,1},{4,6},{6,4},{5,7},{7,5},{8,10},{10,8},{9,1... | collective-permute-start | bytes 1179656 | tf_op jit(solution)/shard_map/ppermute | solution.py:288
  321.3 10.5 %collective-permute-start.65 = (bf16[128,768]{1,0:T(8,128)(2,1)S(1)}, bf16[128,768]{1,0:T(8,128)(2,1)S(1)}, u32[]{:S(2)}, u32[]{:S(2)}) collective-permute-start(bf16[128,768]{1,0:T(8,128)(2,1)S(1)} %fusion.160), channel_id=1, source_target_pairs={{0,2},{2,0},{1,3},{3,1},{4,6},{6,4},{5,7},{7,5},{8,10},{10,8},{9,1... | collective-permute-start | bytes 589832 | tf_op jit(solution)/shard_map/ppermute | solution.py:288
  325.0 42.5 %collective-permute-start.100 = (bf16[384,768]{1,0:T(8,128)(2,1)}, bf16[384,768]{1,0:T(8,128)(2,1)}, u32[]{:S(2)}, u32[]{:S(2)}) collective-permute-start(bf16[384,768]{1,0:T(8,128)(2,1)} %pad_maximum_fusion.18), channel_id=1, source_target_pairs={{0,4},{4,0},{8,12},{12,8},{16,20},{20,16},{24,28},{28,24},{1,5},{5... | collective-permute-start | bytes 1769480 | tf_op jit(solution)/shard_map/ppermute | solution.py:318
  331.9 93.3 %collective-permute-start.46 = (f32[256,768]{1,0:T(8,128)}, f32[256,768]{1,0:T(8,128)}, u32[]{:S(2)}, u32[]{:S(2)}) collective-permute-start(f32[256,768]{1,0:T(8,128)} %slice.696), channel_id=1, source_target_pairs={{0,1},{1,0},{2,3},{3,2},{4,5},{5,4},{6,7},{7,6},{8,9},{9,8},{10,11... | collective-permute-start | bytes 2359304 | tf_op jit(solution)/shard_map/ppermute | solution.py:284
  333.9 21.2 %collective-permute-start.90 = (bf16[192,768]{1,0:T(8,128)(2,1)}, bf16[192,768]{1,0:T(8,128)(2,1)}, u32[]{:S(2)}, u32[]{:S(2)}) collective-permute-start(bf16[192,768]{1,0:T(8,128)(2,1)} %constant_dynamic-slice_fusion.10), channel_id=1, source_target_pairs={{0,8},{4,12},{8,0},{12,4},{16,24},{20,28},{24,16},{28,20},{1,9},{5... | collective-permute-start | bytes 884744 | tf_op jit(solution)/shard_map/ppermute | solution.py:314
  334.5 21.8 %collective-permute-start.48 = (bf16[256,768]{1,0:T(8,128)(2,1)}, bf16[256,768]{1,0:T(8,128)(2,1)}, u32[]{:S(2)}, u32[]{:S(2)}) collective-permute-start(bf16[256,768]{1,0:T(8,128)(2,1)} %collective-permute-done.47), channel_id=1, source_target_pairs={{0,1},{1,0},{2,3},{3,2},{4,5},{5,4},{6,7},{7,6},{8,9},{9,8},{10,11... | collective-permute-start | bytes 1179656 | tf_op jit(solution)/shard_map/ppermute | solution.py:284
  356.1 10.4 %collective-permute-start.91 = (bf16[96,768]{1,0:T(8,128)(2,1)S(1)}, bf16[96,768]{1,0:T(8,128)(2,1)S(1)}, u32[]{:S(2)}, u32[]{:S(2)}) collective-permute-start(bf16[96,768]{1,0:T(8,128)(2,1)S(1)} %constant_dynamic-slice_fusion.9), channel_id=1, source_target_pairs={{0,16},{4,20},{8,24},{12,28},{16,0},{20,4},{24,8},{28,12},{1,17},{... | collective-permute-start | bytes 442376 | tf_op jit(solution)/shard_map/ppermute | solution.py:314
  359.9 53.6 %collective-permute-start.49 = (f32[256,768]{1,0:T(8,128)S(1)}, f32[256,768]{1,0:T(8,128)S(1)}, u32[]{:S(2)}, u32[]{:S(2)}) collective-permute-start(f32[256,768]{1,0:T(8,128)S(1)} %slice.698), channel_id=1, source_target_pairs={{0,1},{1,0},{2,3},{3,2},{4,5},{5,4},{6,7},{7,6},{8,9},{9,8},{10,11... | collective-permute-start | bytes 2359304 | tf_op jit(solution)/shard_map/ppermute | solution.py:284
  363.1 52.2 %collective-permute-start.77 = (bf16[384,1024]{1,0:T(8,128)(2,1)S(1)}, bf16[384,1024]{1,0:T(8,128)(2,1)S(1)}, u32[]{:S(2)}, u32[]{:S(2)}) collective-permute-start(bf16[384,1024]{1,0:T(8,128)(2,1)S(1)} %constant_dynamic-slice_fusion.16), channel_id=1, source_target_pairs={{0,4},{4,0},{8,12},{12,8},{16,20},{20,16},{24,28},{28,24},{1,5},{5... | collective-permute-start | bytes 2359304 | tf_op jit(solution)/shard_map/ppermute | solution.py:314
  366.5 23.9 %collective-permute-start.83 = (bf16[256,768]{1,0:T(8,128)(2,1)S(1)}, bf16[256,768]{1,0:T(8,128)(2,1)S(1)}, u32[]{:S(2)}, u32[]{:S(2)}) collective-permute-start(bf16[256,768]{1,0:T(8,128)(2,1)S(1)} %constant_dynamic-slice_fusion.13), channel_id=1, source_target_pairs={{0,4},{4,0},{8,12},{12,8},{16,20},{20,16},{24,28},{28,24},{1,5},{5... | collective-permute-start | bytes 1179656 | tf_op jit(solution)/shard_map/ppermute | solution.py:314
  367.5 25.6 %collective-permute-start.92 = (bf16[96,768]{1,0:T(8,128)(2,1)S(1)}, bf16[96,768]{1,0:T(8,128)(2,1)S(1)}, u32[]{:S(2)}, u32[]{:S(2)}) collective-permute-start(bf16[96,768]{1,0:T(8,128)(2,1)S(1)} %add_convert_fusion.17), channel_id=1, source_target_pairs={{0,16},{4,20},{8,24},{12,28},{16,0},{20,4},{24,8},{28,12},{1,17},{... | collective-permute-start | bytes 442376 | tf_op jit(solution)/shard_map/ppermute | solution.py:318
  393.2 10.8 %collective-permute-start.93 = (bf16[192,768]{1,0:T(8,128)(2,1)S(1)}, bf16[192,768]{1,0:T(8,128)(2,1)S(1)}, u32[]{:S(2)}, u32[]{:S(2)}) collective-permute-start(bf16[192,768]{1,0:T(8,128)(2,1)S(1)} %pad_maximum_fusion.24), channel_id=1, source_target_pairs={{0,8},{4,12},{8,0},{12,4},{16,24},{20,28},{24,16},{28,20},{1,9},{5... | collective-permute-start | bytes 884744 | tf_op jit(solution)/shard_map/ppermute | solution.py:318
  407.9 14.7 %collective-permute-start.94 = (bf16[384,768]{1,0:T(8,128)(2,1)S(1)}, bf16[384,768]{1,0:T(8,128)(2,1)S(1)}, u32[]{:S(2)}, u32[]{:S(2)}) collective-permute-start(bf16[384,768]{1,0:T(8,128)(2,1)S(1)} %pad_maximum_fusion.17), channel_id=1, source_target_pairs={{0,4},{4,0},{8,12},{12,8},{16,20},{20,16},{24,28},{28,24},{1,5},{5... | collective-permute-start | bytes 1769480 | tf_op jit(solution)/shard_map/ppermute | solution.py:318
  413.6 11.6 %collective-permute-start.50 = (bf16[256,768]{1,0:T(8,128)(2,1)S(1)}, bf16[256,768]{1,0:T(8,128)(2,1)S(1)}, u32[]{:S(2)}, u32[]{:S(2)}) collective-permute-start(bf16[256,768]{1,0:T(8,128)(2,1)S(1)} %fusion.72), channel_id=1, source_target_pairs={{0,2},{2,0},{1,3},{3,1},{4,6},{6,4},{5,7},{7,5},{8,10},{10,8},{9,1... | collective-permute-start | bytes 1179656 | tf_op jit(solution)/shard_map/ppermute | solution.py:288
  415.7 11.7 %collective-permute-start.78 = (bf16[192,1024]{1,0:T(8,128)(2,1)S(1)}, bf16[192,1024]{1,0:T(8,128)(2,1)S(1)}, u32[]{:S(2)}, u32[]{:S(2)}) collective-permute-start(bf16[192,1024]{1,0:T(8,128)(2,1)S(1)} %constant_dynamic-slice_fusion.15), channel_id=1, source_target_pairs={{0,8},{4,12},{8,0},{12,4},{16,24},{20,28},{24,16},{28,20},{1,9},{5... | collective-permute-start | bytes 1179656 | tf_op jit(solution)/shard_map/ppermute | solution.py:314
  420.9 15.1 %collective-permute-start.88 = (bf16[256,768]{1,0:T(8,128)(2,1)S(1)}, bf16[256,768]{1,0:T(8,128)(2,1)S(1)}, u32[]{:S(2)}, u32[]{:S(2)}) collective-permute-start(bf16[256,768]{1,0:T(8,128)(2,1)S(1)} %pad_maximum_fusion.20), channel_id=1, source_target_pairs={{0,4},{4,0},{8,12},{12,8},{16,20},{20,16},{24,28},{28,24},{1,5},{5... | collective-permute-start | bytes 1179656 | tf_op jit(solution)/shard_map/ppermute | solution.py:318
  431.4 13.3 %collective-permute-start.51 = (bf16[256,768]{1,0:T(8,128)(2,1)S(1)}, bf16[256,768]{1,0:T(8,128)(2,1)S(1)}, u32[]{:S(2)}, u32[]{:S(2)}) collective-permute-start(bf16[256,768]{1,0:T(8,128)(2,1)S(1)} %get-tuple-element.108), channel_id=1, source_target_pairs={{0,1},{1,0},{2,3},{3,2},{4,5},{5,4},{6,7},{7,6},{8,9},{9,8},{10,11... | collective-permute-start | bytes 1179656 | tf_op jit(solution)/shard_map/ppermute | solution.py:284
  444.6 45.3 %collective-permute-start.81 = (bf16[192,1024]{1,0:T(8,128)(2,1)S(1)}, bf16[192,1024]{1,0:T(8,128)(2,1)}, u32[]{:S(2)}, u32[]{:S(2)}) collective-permute-start(bf16[192,1024]{1,0:T(8,128)(2,1)S(1)} %pad_maximum_fusion.19), channel_id=1, source_target_pairs={{0,8},{4,12},{8,0},{12,4},{16,24},{20,28},{24,16},{28,20},{1,9},{5... | collective-permute-start | bytes 1179656 | tf_op jit(solution)/shard_map/ppermute | solution.py:318
  474.2 14.2 %collective-permute-start.71 = (bf16[384,768]{1,0:T(8,128)(2,1)S(1)}, bf16[384,768]{1,0:T(8,128)(2,1)S(1)}, u32[]{:S(2)}, u32[]{:S(2)}) collective-permute-start(bf16[384,768]{1,0:T(8,128)(2,1)S(1)} %fusion.118), channel_id=1, source_target_pairs={{0,4},{4,0},{8,12},{12,8},{16,20},{20,16},{24,28},{28,24},{1,5},{5... | collective-permute-start | bytes 1769480 | tf_op jit(solution)/shard_map/ppermute | solution.py:314
  476.7 23.6 %collective-permute-start.55 = (f32[256,768]{1,0:T(8,128)S(1)}, f32[256,768]{1,0:T(8,128)S(1)}, u32[]{:S(2)}, u32[]{:S(2)}) collective-permute-start(f32[256,768]{1,0:T(8,128)S(1)} %slice.704), channel_id=1, source_target_pairs={{0,1},{1,0},{2,3},{3,2},{4,5},{5,4},{6,7},{7,6},{8,9},{9,8},{10,11... | collective-permute-start | bytes 2359304 | tf_op jit(solution)/shard_map/ppermute | solution.py:284
  477.7 35.6 %collective-permute-start.54 = (f32[256,768]{1,0:T(8,128)}, f32[256,768]{1,0:T(8,128)}, u32[]{:S(2)}, u32[]{:S(2)}) collective-permute-start(f32[256,768]{1,0:T(8,128)} %slice.701), channel_id=1, source_target_pairs={{0,1},{1,0},{2,3},{3,2},{4,5},{5,4},{6,7},{7,6},{8,9},{9,8},{10,11... | collective-permute-start | bytes 2359304 | tf_op jit(solution)/shard_map/ppermute | solution.py:284
  492.1 31.4 %collective-permute-start.82 = (bf16[384,1024]{1,0:T(8,128)(2,1)}, bf16[384,1024]{1,0:T(8,128)(2,1)}, u32[]{:S(2)}, u32[]{:S(2)}) collective-permute-start(bf16[384,1024]{1,0:T(8,128)(2,1)} %pad_maximum_fusion.13), channel_id=1, source_target_pairs={{0,4},{4,0},{8,12},{12,8},{16,20},{20,16},{24,28},{28,24},{1,5},{5... | collective-permute-start | bytes 2359304 | tf_op jit(solution)/shard_map/ppermute | solution.py:318
  501.1 12.2 %collective-permute-start.56 = (bf16[256,768]{1,0:T(8,128)(2,1)}, bf16[256,768]{1,0:T(8,128)(2,1)}, u32[]{:S(2)}, u32[]{:S(2)}) collective-permute-start(bf16[256,768]{1,0:T(8,128)(2,1)} %fusion.70), channel_id=1, source_target_pairs={{0,2},{2,0},{1,3},{3,1},{4,6},{6,4},{5,7},{7,5},{8,10},{10,8},{9,1... | collective-permute-start | bytes 1179656 | tf_op jit(solution)/shard_map/ppermute | solution.py:288
  518.8 11.7 %collective-permute-start.75 = (bf16[192,768]{1,0:T(8,128)(2,1)}, bf16[192,768]{1,0:T(8,128)(2,1)}, u32[]{:S(2)}, u32[]{:S(2)}) collective-permute-start(bf16[192,768]{1,0:T(8,128)(2,1)} %pad_maximum_fusion.23), channel_id=1, source_target_pairs={{0,8},{4,12},{8,0},{12,4},{16,24},{20,28},{24,16},{28,20},{1,9},{5... | collective-permute-start | bytes 884744 | tf_op jit(solution)/shard_map/ppermute | solution.py:318
  532.6 15.5 %collective-permute-start.76 = (bf16[384,768]{1,0:T(8,128)(2,1)}, bf16[384,768]{1,0:T(8,128)(2,1)}, u32[]{:S(2)}, u32[]{:S(2)}) collective-permute-start(bf16[384,768]{1,0:T(8,128)(2,1)} %pad_maximum_fusion.16), channel_id=1, source_target_pairs={{0,4},{4,0},{8,12},{12,8},{16,20},{20,16},{24,28},{28,24},{1,5},{5... | collective-permute-start | bytes 1769480 | tf_op jit(solution)/shard_map/ppermute | solution.py:318
  (219 other events, 1381.0 us)

commit v2 on v1

--- a/solution.py
+++ b/solution.py
@@ -262,44 +262,411 @@
         name="attention_backward_" + kind,
     )(places, *args)
 
-
-def normalize(residual, gain_row):
-    scale_row = lax.rsqrt(jnp.mean(residual * residual, axis=-1, keepdims=True) + EPS)
-    return (residual * scale_row * gain_row, scale_row)
-
-
-def normalize_backward(residual, scale_row, gain_row, normed_grad):
-    weighted = normed_grad * gain_row
-    inner_mean = jnp.mean(residual * weighted, axis=-1, keepdims=True)
-    input_grad = scale_row * weighted - residual * scale_row**3 * inner_mean
-    gain_grad = jnp.sum(normed_grad * residual * scale_row, axis=0)
-    return (input_grad, gain_grad)
-
-
-CORE = [(0, 1), (1, 0), (2, 3), (3, 2)]
-CHIP = [(0, 2), (2, 0), (1, 3), (3, 1)]
-
-
-def swap_core(value):
-    return lax.ppermute(value, "tensor", CORE)
-
-
-def swap_chip(value):
-    return lax.ppermute(value, "tensor", CHIP)
-
-
-def gather_rows(rows):
-    across = swap_chip(rows)
-    near = jnp.concatenate([rows, swap_core(rows)], axis=0)
-    far = jnp.concatenate([across, swap_core(across)], axis=0)
-    return near, far
-
-
-def scatter_rows(near, far):
-    half = near.shape[0] // 2
-    sent = far[:half] + swap_core(far[half:])
-    across = swap_chip(sent.astype(jnp.bfloat16))
-    return near[:half] + swap_core(near[half:]) + across.astype(jnp.float32)
+MESH = pl.DeviceIdType.MESH
+
+
+def low(value):
+    return value.astype(jnp.bfloat16)
+
+
+def wide(value):
+    return value.astype(jnp.float32)
+
+
+def root_scale(rows):
+    return lax.rsqrt(jnp.mean(rows * rows, axis=-1, keepdims=True) + EPS)
+
+
+def normalize(rows, gain):
+    return rows * root_scale(rows) * gain
+
+
+def normalize_backward(rows, gain, grad):
+    scale = root_scale(rows)
+    weighted = grad * gain
+    inner = jnp.mean(rows * weighted, axis=-1, keepdims=True)
+    gain_grad = jnp.sum(grad * rows * scale, axis=0, keepdims=True)
+    return scale * weighted - rows * (scale * scale * scale) * inner, gain_grad
+
+
+def gelu_parts(x):
+    c = math.sqrt(2.0 / math.pi)
+    square = x * x
+    th = jnp.tanh(c * (x + 0.044715 * (square * x)))
+    half = 0.5 * (1.0 + th)
+    slope = half + 0.5 * x * (1.0 - th * th) * (c * (1.0 + 3 * 0.044715 * square))
+    return x * half, slope
+
+
+class Links:
+    def __init__(self, send, recv):
+        self.send, self.recv, self.used, self.open = send, recv, 0, []
+        self.t = lax.axis_index("tensor")
+        self.core = {"tensor": self.t + 1 - 2 * lax.rem(self.t, 2)}
+        self.chip = {"tensor": lax.rem(self.t + 2, 4)}
+
+    def enter(self):
+        barrier = pltpu.get_barrier_semaphore()
+        for peer in (self.core, self.chip):
+            pl.semaphore_signal(barrier, inc=1, device_id=peer, device_id_type=MESH)
+        pl.semaphore_wait(barrier, 2)
+
+    def copy(self, source, target, peer):
+        index = self.used
+        self.used += 1
+        made = pltpu.make_async_remote_copy(
+            src_ref=source, dst_ref=target, send_sem=self.send.at[index], recv_sem=self.recv.at[index],
+            device_id=peer, device_id_type=MESH)
+        made.start()
+        self.open.append(made)
+        return made
+
+    def close(self):
+        for made in self.open:
+            made.wait_send()
+
+    def place(self, index):
+        low_bit = lax.rem(self.t, 2)
+        high_bit = lax.div(self.t, 2)
+        if index % 2:
+            low_bit = 1 - low_bit
+        if index // 2:
+            high_bit = 1 - high_bit
+        return 2 * high_bit + low_bit
+
+
+def gather(links, buf, on_near=None, on_far=None):
+    block = buf.shape[0] // 4
+    slot = lambda i: buf.at[pl.ds(i * block, block)]
+    across = links.copy(slot(0), slot(2), links.chip)
+    beside = links.copy(slot(0), slot(1), links.core)
+    yield
+    beside.wait_recv()
+    if on_near is not None:
+        on_near()
+    yield
+    across.wait_recv()
+    passed = links.copy(slot(2), slot(3), links.core)
+    yield
+    passed.wait_recv()
+    if on_far is not None:
+        on_far()
+
+
+def scatter(links, bufs, on_far, on_near, value_near=None):
+    partial, came, sent, landed = bufs
+    block = sent.shape[0]
+    partial[2 * block:] = on_far()
+    first = links.copy(partial.at[pl.ds(3 * block, block)], came.at[0], links.core)
+    partial[:2 * block] = on_near()
+    second = links.copy(partial.at[pl.ds(block, block)], came.at[1], links.core)
+    yield
+    first.wait_recv()
+    sent[...] = low(partial[2 * block:3 * block] + came[0])
+    across = links.copy(sent, landed, links.chip)
+    yield
+    second.wait_recv()
+    mine = partial[:block] + came[1]
+    yield
+    across.wait_recv()
+    return mine + wide(landed[...])
+
+
+def scatter_bufs(block, width):
+    return [
+        pltpu.VMEM((4 * block, width), jnp.float32),
+        pltpu.VMEM((2, block, width), jnp.float32),
+        pltpu.VMEM((block, width), jnp.bfloat16),
+        pltpu.VMEM((block, width), jnp.bfloat16),
+    ]
+
+
+def run(*chains):
+    chains = list(chains)
+    while chains:
+        for chain in list(chains):
+            try:
+                next(chain)
+            except StopIteration:
+                chains.remove(chain)
+
+
+def call(name, number, body, ins, outs, scratch, copies):
+    n_in, n_out, n_scratch = len(ins), len(outs), len(scratch)
+
+    def kernel(*refs):
+        in_refs, refs = refs[:n_in], refs[n_in:]
+        out_refs, refs = refs[:n_out], refs[n_out:]
+        scratch_refs, (send, recv) = refs[:n_scratch], refs[n_scratch:]
+        links = Links(send, recv)
+        links.enter()
+        body(links, in_refs, out_refs, scratch_refs)
+        links.close()
+        assert links.used == copies, links.used
+
+    vmem = pl.BlockSpec(memory_space=pltpu.VMEM)
+    return pl.pallas_call(
+        kernel,
+        in_specs=[vmem] * n_in,
+        out_specs=[vmem] * n_out,
+        out_shape=[jax.ShapeDtypeStruct(shape, dtype) for shape, dtype in outs],
+        scratch_shapes=[*scratch, pltpu.SemaphoreType.DMA((copies,)), pltpu.SemaphoreType.DMA((copies,))],
+        compiler_params=pltpu.CompilerParams(collective_id=number, has_side_effects=True, vmem_limit_bytes=VMEM_BYTES),
+        name=name,
+    )(*ins)
+
+
+BF, F32 = jnp.bfloat16, jnp.float32
+
+
+def project(links, rows_ref, weight, targets, first, block, inner):
+    for index in (first, first + 1):
+        rows = rows_ref[index * block:(index + 1) * block, :]
+        at = pl.ds(pl.multiple_of(links.place(index) * block, block), block)
+        for number, target in enumerate(targets):
+            target[at, :] = low(nt(rows, weight[number * inner:(number + 1) * inner, :]))
+
+
+def first_kernel(x, y, gains, enc_in, dec_in):
+    (eb, width), db, inner = x.shape, y.shape[0], enc_in.shape[0] // 3
+
+    def body(links, ins, outs, scratch):
+        x, y, gains, enc_in, dec_in = ins
+        a0, a3, q1, k1, v1, q2, k2, v2 = outs
+        a0[:eb] = low(normalize(wide(x[...]), gains[0:1, :]))
+
+        def enc():
+            step = lambda first: lambda: project(links, a0, enc_in, (q1, k1, v1), first, eb, inner)
+            yield from gather(links, a0, step(0), step(2))
+
+        def dec():
+            a3[:db] = low(normalize(wide(y[...]), gains[3:4, :]))
+            step = lambda first: lambda: project(links, a3, dec_in, (q2, k2, v2), first, db, inner)
+            yield from gather(links, a3, step(0), step(2))
+        run(enc(), dec())
+
+    outs = [((4 * eb, width), BF), ((4 * db, width), BF)] + [((4 * eb, inner), BF)] * 3 + [((4 * db, inner), BF)] * 3
+    return call("rows_in", 1, body, (x, y, gains, enc_in, dec_in), outs, [], 6)
+
+
+def second_kernel(att1, att2, enc_out, dec_out, x, y, gains, enc_gu, enc_down, kv_in, q_in, cot):
+    (eb, width), db, inner, ff = x.shape, y.shape[0], enc_out.shape[0], enc_down.shape[0]
+
+    def body(links, ins, outs, scratch):
+        att1, att2, enc_out, dec_out, x, y, gains, enc_gu, enc_down, kv_in, q_in, cot = ins
+        h_out, e_out, m_out, result, a1, gu1, hid1, closing, ck, cv, a4, cq, cot_all = outs
+
+        def feed(first):
+            for index in (first, first + 1):
+                rows = slice(index * eb, (index + 1) * eb)
+                gu = nn(a1[rows, :], enc_gu[...])
+                gu1[rows, :] = gu
+                gate, up = gu[:, :ff], gu[:, ff:]
+                hid1[rows, :] = low(gelu_parts(gate)[0] * up)
+
+        def enc():
+            h = wide(x[...]) + (yield from scatter(
+                links, scratch[0:4], lambda: nn(att1[2 * eb:, :], enc_out[...]), lambda: nn(att1[:2 * eb, :], enc_out[...])))
+            h_out[...] = h
+            a1[:eb] = low(normalize(h, gains[1:2, :]))
+            yield from gather(links, a1, lambda: feed(0), lambda: feed(2))
+            e = h_out[...] + (yield from scatter(
+                links, scratch[4:8], lambda: nn(hid1[2 * eb:, :], enc_down[...]), lambda: nn(hid1[:2 * eb, :], enc_down[...])))
+            e_out[...] = e
+            closed = low(normalize(e, gains[2:3, :]))
+            result[...] = closed
+            closing[:eb] = closed
+            step = lambda first: lambda: project(links, closing, kv_in, (ck, cv), first, eb, inner)
+            yield from gather(links, closing, step(0), step(2))
+
+        def dec():
+            m = wide(y[...]) + (yield from scatter(
+                links, scratch[8:12], lambda: nn(att2[2 * db:, :], dec_out[...]), lambda: nn(att2[:2 * db, :], dec_out[...])))
+            m_out[...] = m
+            a4[:db] = low(normalize(m, gains[4:5, :]))
+            step = lambda first: lambda: project(links, a4, q_in, (cq,), first, db, inner)
+            yield from gather(links, a4, step(0), step(2))
+            cot_all[:db] = cot[...]
+            yield from gather(links, cot_all)
+        run(enc(), dec())
+
+    outs = [((eb, width), F32), ((eb, width), F32), ((db, width), F32), ((eb, width), BF), ((4 * eb, width), BF),
+            ((4 * eb, 2 * ff), F32), ((4 * eb, ff), BF), ((4 * eb, width), BF), ((4 * eb, inner), BF), ((4 * eb, inner), BF),
+            ((4 * db, width), BF), ((4 * db, inner), BF), ((4 * db, width), BF)]
+    scratch = scatter_bufs(eb, width) * 2 + scatter_bufs(db, width)
+    return call("encoder_rows", 2, body, (att1, att2, enc_out, dec_out, x, y, gains, enc_gu, enc_down, kv_in, q_in, cot), outs, scratch, 21)
+
+
+def feed_back(gu, hid, a, grads, gate_up, down, rows, stacked):
+    ff = down.shape[0]
+    hidden_grad = nt(grads[rows, :], down[...])
+    gate, up = gu[rows, :ff], gu[rows, ff:]
+    active, slope = gelu_parts(gate)
+    stacked[rows, :ff] = low(hidden_grad * up * slope)
+    stacked[rows, ff:] = low(hidden_grad * active)
+
+
+def third_kernel(att3, cross_out, m, gains, dec_gu, dec_down, cot, cot_all):
+    (db, width), inner, ff = m.shape, cross_out.shape[0], dec_down.shape[0]
+
+    def body(links, ins, outs, scratch):
+        att3, cross_out, m, gains, dec_gu, dec_down, cot, cot_all = ins
+        result, later_out, do3, gu_grad, down_grad, out_grad, gain5 = outs
+        n_keep, a5, gu, hid, stacked, grads = scratch[12:]
+
+        def feed(first):
+            rows = slice(first * db, (first + 2) * db)
+            here = nn(a5[rows, :], dec_gu[...])
+            gu[rows, :] = here
+            active, slope = gelu_parts(here[:, :ff])
+            up = here[:, ff:]
+            hid[rows, :] = low(active * up)
+            hidden_grad = nt(cot_all[rows, :], dec_down[...])
+            stacked[rows, :ff] = low(hidden_grad * up * slope)
+            stacked[rows, ff:] = low(hidden_grad * active)
+
+        near, far = slice(0, 2 * db), slice(2 * db, 4 * db)
+        started = []
+
+        def back():
+            n = m[...] + (yield from scatter(
+                links, scratch[0:4], lambda: nn(att3[far, :], cross_out[...]), lambda: nn(att3[near, :], cross_out[...])))
+            n_keep[...] = n
+            a5[:db] = low(normalize(n, gains[5:6, :]))
+            yield from gather(links, a5, lambda: feed(0), lambda: feed(2))
+            started.append(True)
+            grad = yield from scatter(
+                links, scratch[4:8], lambda: nt(stacked[far, :], dec_gu[...]), lambda: nt(stacked[near, :], dec_gu[...]))
+            part, gain = normalize_backward(n_keep[...], gains[5:6, :], grad)
+            gain5[...] = jnp.broadcast_to(gain, gain5.shape)
+            later = wide(cot[...]) + part
+            later_out[...] = later
+            grads[:db] = low(later)
+            step = lambda rows: lambda: do3.__setitem__((rows, slice(None)), low(nt(grads[rows, :], cross_out[...])))
+            yield from gather(links, grads, step(near), step(far))
+            out_grad[...] = low(tn(att3[...], grads[...]))
+
+        def rest():
+            while not started:
+                yield
+            yield
+            part = yield from scatter(
+                links, scratch[8:12], lambda: nn(hid[far, :], dec_down[...]), lambda: nn(hid[near, :], dec_down[...]))
+            result[...] = low(n_keep[...] + part)
+
+        def weights():
+            while not started:
+                yield
+            yield
+            down_grad[...] = low(tn(hid[...], cot_all[...]))
+            yield
+            gu_grad[...] = low(tn(a5[...], stacked[...]))
+        run(back(), rest(), weights())
+
+    outs = [((db, width), BF), ((db, width), F32), ((4 * db, inner), BF), ((width, 2 * ff), BF), ((ff, width), BF), ((inner, width), BF), ((8, width), F32)]
+    scratch = scatter_bufs(db, width) * 3 + [
+        pltpu.VMEM((db, width), F32), pltpu.VMEM((4 * db, width), BF), pltpu.VMEM((4 * db, 2 * ff), F32),
+        pltpu.VMEM((4 * db, ff), BF), pltpu.VMEM((4 * db, 2 * ff), BF), pltpu.VMEM((4 * db, width), BF)]
+    return call("decoder_rows", 3, body, (att3, cross_out, m, gains, dec_gu, dec_down, cot, cot_all), outs, scratch, 15)
+
+
+def fourth_kernel(dcq, dck, dcv, kv_in, q_in, e, m, h, gains, enc_cot, later, a1, gu1, hid1, enc_gu, enc_down, closing, a4, enc_out, dec_out, att1, att2):
+    (eb, width), db, inner, ff = e.shape, m.shape[0], enc_out.shape[0], enc_down.shape[0]
+
+    def body(links, ins, outs, scratch):
+        dcq, dck, dcv, kv_in, q_in, e, m, h, gains, enc_cot, later, a1, gu1, hid1, enc_gu, enc_down, closing, a4, enc_out, dec_out, att1, att2 = ins
+        h_grad, middle, do1, do2, kv_grad, q_grad, gu_grad, down_grad, enc_out_grad, dec_out_grad, gain_grads = outs
+        last, grads1, grads0, grads_dec, stacked = scratch[16:]
+        near, far = slice(0, 2 * eb), slice(2 * eb, 4 * eb)
+        dnear, dfar = slice(0, 2 * db), slice(2 * db, 4 * db)
+        marks = {}
+
+        def feed(first):
+            for index in (first, first + 1):
+                feed_back(gu1, hid1, a1, grads1, enc_gu, enc_down, slice(index * eb, (index + 1) * eb), stacked)
+
+        def enc():
+            part = lambda rows: nn(dck[rows, :], kv_in[:inner, :]) + nn(dcv[rows, :], kv_in[inner:, :])
+            grad = wide(enc_cot[...]) + (yield from scatter(links, scratch[0:4], lambda: part(far), lambda: part(near)))
+            back, gain = normalize_backward(e[...], gains[2:3, :], grad)
+            gain_grads[2:3, :] = gain
+            last[...] = back
+            grads1[:eb] = low(back)
+            yield from gather(links, grads1, lambda: feed(0), lambda: feed(2))
+            marks["fed"] = True
+            grad = yield from scatter(links, scratch[4:8], lambda: nt(stacked[far, :], enc_gu[...]), lambda: nt(stacked[near, :], enc_gu[...]))
+            back, gain = normalize_backward(h[...], gains[1:2, :], grad)
+            gain_grads[1:2, :] = gain
+            total = last[...] + back
+            h_grad[...] = total
+            grads0[:eb] = low(total)
+            step = lambda rows: lambda: do1.__setitem__((rows, slice(None)), low(nt(grads0[rows, :], enc_out[...])))
+            yield from gather(links, grads0, step(near), step(far))
+            enc_out_grad[...] = low(tn(att1[...], grads0[...]))
+
+        def dec():
+            grad = yield from scatter(links, scratch[8:12], lambda: nn(dcq[dfar, :], q_in[...]), lambda: nn(dcq[dnear, :], q_in[...]))
+            back, gain = normalize_backward(m[...], gains[4:5, :], grad)
+            gain_grads[4:5, :] = gain
+            total = later[...] + back
+            middle[...] = total
+            grads_dec[:db] = low(total)
+            step = lambda rows: lambda: do2.__setitem__((rows, slice(None)), low(nt(grads_dec[rows, :], dec_out[...])))
+            yield from gather(links, grads_dec, step(dnear), step(dfar))
+            dec_out_grad[...] = low(tn(att2[...], grads_dec[...]))
+
+        def weights():
+            yield
+            kv_grad[:inner, :] = low(tn(dck[...], closing[...]))
+            yield
+            kv_grad[inner:, :] = low(tn(dcv[...], closing[...]))
+            q_grad[...] = low(tn(dcq[...], a4[...]))
+            while "fed" not in marks:
+                yield
+            yield
+            gu_grad[...] = low(tn(a1[...], stacked[...]))
+            yield
+            down_grad[...] = low(tn(hid1[...], grads1[...]))
+        gain_grads[...] = jnp.zeros_like(gain_grads)
+        run(enc(), dec(), weights())
+
+    outs = [((eb, width), F32), ((db, width), F32), ((4 * eb, inner), BF), ((4 * db, inner), BF), ((2 * inner, width), BF), ((inner, width), BF),
+            ((width, 2 * ff), BF), ((ff, width), BF), ((inner, width), BF), ((inner, width), BF), ((8, width), F32)]
+    scratch = scatter_bufs(eb, width) * 2 + scatter_bufs(db, width) + scatter_bufs(8, 128) + [
+        pltpu.VMEM((eb, width), F32), pltpu.VMEM((4 * eb, width), BF), pltpu.VMEM((4 * eb, width), BF), pltpu.VMEM((4 * db, width), BF),
+        pltpu.VMEM((4 * eb, 2 * ff), BF)]
+    ins = (dcq, dck, dcv, kv_in, q_in, e, m, h, gains, enc_cot, later, a1, gu1, hid1, enc_gu, enc_down, closing, a4, enc_out, dec_out, att1, att2)
+    return call("encoder_back", 4, body, ins, outs, scratch, 18)
+
+
+def fifth_kernel(dqkv1, dqkv2, enc_in, dec_in, x, y, gains, h_grad, middle, a0, a3):
+    (eb, width), db, inner = h_grad.shape, middle.shape[0], enc_in.shape[0] // 3
+
+    def body(links, ins, outs, scratch):
+        dq1, dk1, dv1, dq2, dk2, dv2, enc_in, dec_in, x, y, gains, h_grad, middle, a0, a3 = ins
+        enc_rows, dec_rows, enc_in_grad, dec_in_grad, gain_grads = outs
+
+        def side(bufs, triple, weight, rows_in, gain_row, above, out, block):
+            part = lambda rows: sum(nn(d[rows, :], weight[i * inner:(i + 1) * inner, :]) for i, d in enumerate(triple))
+            grad = yield from scatter(links, bufs, lambda: part(slice(2 * block, 4 * block)), lambda: part(slice(0, 2 * block)))
+            back, gain = normalize_backward(wide(rows_in[...]), gains[gain_row:gain_row + 1, :], grad)
+            gain_grads[gain_row:gain_row + 1, :] = gain
+            out[...] = above[...] + back
+
+        def weights():
+            for i, d in enumerate((dq1, dk1, dv1)):
+                enc_in_grad[i * inner:(i + 1) * inner, :] = low(tn(d[...], a0[...]))
+            yield
+            for i, d in enumerate((dq2, dk2, dv2)):
+                dec_in_grad[i * inner:(i + 1) * inner, :] = low(tn(d[...], a3[...]))
+        gain_grads[...] = jnp.zeros_like(gain_grads)
+        run(side(scratch[0:4], (dq1, dk1, dv1), enc_in, x, 0, h_grad, enc_rows, eb),
+            side(scratch[4:8], (dq2, dk2, dv2), dec_in, y, 3, middle, dec_rows, db), weights())
+
+    outs = [((eb, width), F32), ((db, width), F32), ((3 * inner, width), BF), ((3 * inner, width), BF), ((8, width), F32)]
+    scratch = scatter_bufs(eb, width) + scatter_bufs(db, width)
+    ins = (*dqkv1, *dqkv2, enc_in, dec_in, x, y, gains, h_grad, middle, a0, a3)
+    return call("rows_back", 5, body, ins, outs, scratch, 6)
 
 
 def reduce_pieces(grad, size):
@@ -320,63 +687,13 @@
     return current
 
 
-def sum_all(value, size, axes):
+def sum_all(value, axes):
     for axis, count in axes:
         bit = 1
         while bit < count:
             value = value + lax.ppermute(value, axis, [(i, i ^ bit) for i in range(count)])
             bit *= 2
     return value
-
-
-def dot_nt(a, b):
-    return lax.dot_general(a, b, (((1,), (1,)), ((), ())), preferred_element_type=jnp.float32)
-
-
-def dot_nn(a, b):
-    return lax.dot_general(a, b, (((1,), (0,)), ((), ())), preferred_element_type=jnp.float32)
-
-
-def dot_tn(a, b):
-    return lax.dot_general(a, b, (((0,), (0,)), ((), ())), preferred_element_type=jnp.float32)
-
-
-def both(pair, function):
-    return function(pair[0]), function(pair[1])
-
-
-def to_order(value, places, block):
-    out = jnp.zeros_like(value)
-    for index in range(4):
-        out = lax.dynamic_update_slice_in_dim(out, value[index * block:(index + 1) * block], places[index] * block, 0)
-    return out
-
-
-def low(value):
-    return value.astype(jnp.bfloat16)
-
-
-def feed_forward(normed, gate_up, down):
-    gu = both(normed, lambda a: dot_nn(a, gate_up))
-    hidden = both(gu, lambda x: low(jax.nn.gelu(x[:, :x.shape[1] // 2]) * x[:, x.shape[1] // 2:]))
-    part = both(hidden, lambda h: dot_nn(h, down))
-    return scatter_rows(*part), gu, hidden
-
-
-def feed_backward(normed, gate_up, down, gu, hidden, grads):
-    def one(index):
-        hidden_grad = dot_nt(grads[index], down)
-        gate, up = jnp.split(gu[index], 2, axis=1)
-        activated, pullback = jax.vjp(jax.nn.gelu, gate)
-        gate_grad = pullback(hidden_grad * up)[0]
-        return low(jnp.concatenate([gate_grad, hidden_grad * activated], axis=1))
-    stacked = one(0), one(1)
-    normed_grad = scatter_rows(*both(stacked, lambda s: dot_nt(s, gate_up)))
-    join = lambda pair: jnp.concatenate(pair, axis=0)
-    rows, cols = join(normed), join(stacked)
-    gate_up_grad = low(dot_tn(rows, cols))
-    down_grad = low(dot_tn(join(hidden), join(grads)))
-    return normed_grad, gate_up_grad, down_grad
 
 
 def local(
@@ -413,103 +730,41 @@
     q_in = jnp.transpose(cross_queries)
     enc_gu = encoder_gate_up.reshape(width, -1)
     dec_gu = decoder_gate_up.reshape(width, -1)
-    enc_seg_k, dec_seg_k = encoder_segments, decoder_segments
     enc_seg_q, dec_seg_q = jnp.transpose(encoder_segments), jnp.transpose(decoder_segments)
-    join = lambda pair: jnp.concatenate(pair, axis=0)
-
-    def project(pair, weight, block):
-        rows = join(pair)
-        return [to_order(low(dot_nt(rows, weight[i:i + inner])), places, block) for i in range(0, weight.shape[0], inner)]
-
-    def out_part(attended, weight):
-        half = attended.shape[0] // 2
-        return scatter_rows(dot_nn(attended[:half], weight), dot_nn(attended[half:], weight))
-
-    x = encoder_rows.astype(jnp.float32)
-    y = decoder_rows.astype(jnp.float32)
-    normed, enc_s0 = normalize(x, norm_gains[0])
-    enc_a0 = gather_rows(low(normed))
-    normed, dec_s3 = normalize(y, norm_gains[3])
-    dec_a3 = gather_rows(low(normed))
-    qkv1 = project(enc_a0, enc_in, eb)
-    att1, tot1 = attention_forward("encoder", heads, places, *qkv1, enc_seg_q, enc_seg_k, position_tables[0], eb, chunk=64)
-    h = x + out_part(att1, encoder_attention_out)
-    normed, enc_s1 = normalize(h, norm_gains[1])
-    enc_a1 = gather_rows(low(normed))
-    qkv2 = project(dec_a3, dec_in, db)
-    att2, tot2 = attention_forward("decoder", heads, places, *qkv2, dec_seg_q, dec_seg_k, position_tables[1], db, chunk=db)
-    part, gu1, hid1 = feed_forward(enc_a1, enc_gu, encoder_down)
-    e = h + part
-    normed, enc_s2 = normalize(e, norm_gains[2])
-    encoder_result = low(normed)
-    enc_r = gather_rows(encoder_result)
-    m = y + out_part(att2, decoder_attention_out)
-    normed, dec_s4 = normalize(m, norm_gains[4])
-    dec_a4 = gather_rows(low(normed))
-    cq = project(dec_a4, q_in, db)[0]
-    ck, cv = project(enc_r, kv_in, eb)
-    att3, tot3 = attention_forward("cross", heads, places, cq, ck, cv, dec_seg_q, enc_seg_k, None, db, chunk=db)
-    n = m + out_part(att3, cross_output)
-    normed, dec_s5 = normalize(n, norm_gains[5])
-    dec_a5 = gather_rows(low(normed))
-    part, gu2, hid2 = feed_forward(dec_a5, dec_gu, decoder_down)
-    decoder_result = low(n + part)
-
-    result_grad = decoder_cotangent.astype(jnp.float32)
-    grads = gather_rows(decoder_cotangent)
-    normed_grad, dec_gu_grad, dec_down_grad = feed_backward(dec_a5, dec_gu, decoder_down, gu2, hid2, grads)
-    part, gain5 = normalize_backward(n, dec_s5, norm_gains[5], normed_grad)
-    later_grad = result_grad + part
-    grads = gather_rows(low(later_grad))
-    co_grad = low(dot_nt(join(grads), cross_output))
-    cross_output_grad = low(dot_tn(att3, join(grads)))
-    dcq, dck, dcv = attention_backward("cross", heads, places, cq, ck, cv, dec_seg_q, enc_seg_k, co_grad, tot3, None, db, eb, chunk=db)
-    half = 2 * eb
-    kv_grad = jnp.concatenate([dck, dcv], axis=1)
-    kv_normed = scatter_rows(dot_nn(kv_grad[:half], kv_in), dot_nn(kv_grad[half:], kv_in))
-    q_normed = scatter_rows(dot_nn(dcq[:2 * db], q_in), dot_nn(dcq[2 * db:], q_in))
-    cross_queries_grad = low(dot_tn(dcq, join(dec_a4)))
-    cross_kv_grad = low(dot_tn(kv_grad, join(enc_r)))
-    part, gain2 = normalize_backward(e, enc_s2, norm_gains[2], encoder_cotangent.astype(jnp.float32) + kv_normed)
-    last_grad = part
-    grads = gather_rows(low(last_grad))
-    normed_grad, enc_gu_grad, enc_down_grad = feed_backward(enc_a1, enc_gu, encoder_down, gu1, hid1, grads)
-    part, gain4 = normalize_backward(m, dec_s4, norm_gains[4], q_normed)
-    middle_grad = later_grad + part
-    dec_grads = gather_rows(low(middle_grad))
-
-    def self_backward(kind, grads, weight_in, weight_out, qkv, attended, totals, seg_q, seg_k, table, block, normed, chunk):
-        rows = join(grads)
-        out_grad = low(dot_nt(rows, weight_out))
-        dq, dk, dv, table_grad = attention_backward(kind, heads, places, *qkv, seg_q, seg_k, out_grad, totals, table, block, block, chunk=chunk)
-        dqkv = jnp.concatenate([dq, dk, dv], axis=1)
-        normed_grad = scatter_rows(dot_nn(dqkv[:2 * block], weight_in), dot_nn(dqkv[2 * block:], weight_in))
-        return normed_grad, low(dot_tn(dqkv, join(normed))), low(dot_tn(attended, rows)), table_grad[:heads, :BUCKETS]
-
-    part, gain1 = normalize_backward(h, enc_s1, norm_gains[1], normed_grad)
-    h_grad = last_grad + part
-    grads = gather_rows(low(h_grad))
-    normed_grad, dec_in_grad, dec_out_grad, dec_table = self_backward(
-        "decoder", dec_grads, dec_in, decoder_attention_out, qkv2, att2, tot2, dec_seg_q, dec_seg_k, position_tables[1], db, dec_a3, db)
-    part, gain3 = normalize_backward(y, dec_s3, norm_gains[3], normed_grad)
-    decoder_rows_gradient = middle_grad + part
-    normed_grad, enc_in_grad, enc_out_grad, enc_table = self_backward(
-        "encoder", grads, enc_in, encoder_attention_out, qkv1, att1, tot1, enc_seg_q, enc_seg_k, position_tables[0], eb, enc_a0, 64)
-    part, gain0 = normalize_backward(x, enc_s0, norm_gains[0], normed_grad)
-    encoder_rows_gradient = h_grad + part
-
-    wide = lambda a: a.astype(jnp.float32)
+
+    a0, a3, q1, k1, v1, q2, k2, v2 = first_kernel(encoder_rows, decoder_rows, norm_gains, enc_in, dec_in)
+    att1, tot1 = attention_forward("encoder", heads, places, q1, k1, v1, enc_seg_q, encoder_segments, position_tables[0], eb, chunk=64)
+    att2, tot2 = attention_forward("decoder", heads, places, q2, k2, v2, dec_seg_q, decoder_segments, position_tables[1], db, chunk=db)
+    h, e, m, encoder_result, a1, gu1, hid1, closing, ck, cv, a4, cq, cot_all = second_kernel(
+        att1, att2, encoder_attention_out, decoder_attention_out, encoder_rows, decoder_rows, norm_gains, enc_gu, encoder_down,
+        kv_in, q_in, decoder_cotangent)
+    att3, tot3 = attention_forward("cross", heads, places, cq, ck, cv, dec_seg_q, encoder_segments, None, db, chunk=db)
+    decoder_result, later, do3, dec_gu_grad, dec_down_grad, cross_output_grad, gain5 = third_kernel(
+        att3, cross_output, m, norm_gains, dec_gu, decoder_down, decoder_cotangent, cot_all)
+
+    dcq, dck, dcv = attention_backward("cross", heads, places, cq, ck, cv, dec_seg_q, encoder_segments, do3, tot3, None, db, eb, chunk=db)
+    h_grad, middle, do1, do2, cross_kv_grad, cross_queries_grad, enc_gu_grad, enc_down_grad, enc_out_grad, dec_out_grad, gains_mid = fourth_kernel(
+        dcq, dck, dcv, kv_in, q_in, e, m, h, norm_gains, encoder_cotangent, later, a1, gu1, hid1, enc_gu, encoder_down, closing, a4,
+        encoder_attention_out, decoder_attention_out, att1, att2)
+    *dqkv2, dec_table = attention_backward(
+        "decoder", heads, places, q2, k2, v2, dec_seg_q, decoder_segments, do2, tot2, position_tables[1], db, db, chunk=db)
+    *dqkv1, enc_table = attention_backward(
+        "encoder", heads, places, q1, k1, v1, enc_seg_q, encoder_segments, do1, tot1, position_tables[0], eb, eb, chunk=64)
+    encoder_rows_gradient, decoder_rows_gradient, enc_in_grad, dec_in_grad, gains_end = fifth_kernel(
+        dqkv1, dqkv2, enc_in, dec_in, encoder_rows, decoder_rows, norm_gains, h_grad, middle, a0, a3)
+
     total = functools.partial(reduce_pieces, size=dp)
     dec_gu_sum, dec_down_sum = wide(total(dec_gu_grad)), wide(total(dec_down_grad))
     cross = total(jnp.concatenate([cross_output_grad, cross_queries_grad, cross_kv_grad], axis=0))
     enc_gu_sum, enc_down_sum = wide(total(enc_gu_grad)), wide(total(enc_down_grad))
     dec_att = total(jnp.concatenate([dec_out_grad, dec_in_grad], axis=0))
     enc_att = total(jnp.concatenate([enc_out_grad, enc_in_grad], axis=0))
-    gains = jnp.stack([gain0, gain1, gain2, gain3, gain4, gain5])
-    gains = sum_all(gains, None, [("tensor", 4)])
-    tables = jnp.stack([enc_table, dec_table])
+    gains = gains_mid + gains_end
+    gains = jnp.concatenate([gains[:5], gain5[:1]], axis=0)
+    gains = sum_all(gains, [("tensor", 4)])
+    tables = jnp.stack([enc_table[:heads, :BUCKETS], dec_table[:heads, :BUCKETS]])
     small = jnp.concatenate([gains.reshape(-1), tables.reshape(-1)])
-    small = sum_all(small, None, [("dp", dp)])
+    small = sum_all(small, [("dp", dp)])
     gains = small[:gains.size].reshape(gains.shape)
     tables = small[gains.size:].reshape(tables.shape)
     unfold = lambda g, parts: jnp.transpose(wide(g).reshape(parts, inner, width), (2, 0, 1))

time: 560 us -> 632 us (1.13)
  Pallas kernels: 78.6 us -> 300 us
  matrix products: 51.7 us -> 0 us
  starting transfers between devices: 92.8 us -> 53.9 us
  other arithmetic: 73.5 us -> 36.4 us
  local copies, waits for them, and re-layouts: 55.7 us -> 37.2 us
  waiting for transfers between devices: 190 us -> 199 us
  between operations: 9.32 us -> 1.76 us
    pallas_call x0 -> x5, Pallas kernels: none -> 221 us  [call(): pl.pallas_call(kernel, in_specs=[vmem] * n_in, out_specs=[vmem] * n_out,...]
    ppermute x66 -> x0, waiting for transfers between devices: 68.3 us -> none  [the longest x22 62.5 us: swap_chip(): return lax.ppermute(value, 'tensor', CHIP)]
    ppermute x21, waiting for transfers between devices: 50 us -> 110 us  [reduce_pieces(): came = lax.ppermute(current, 'dp', [(i, i ^ bit) for i in range(size)])]
    dot_general x53 -> x0, matrix products: 51.7 us -> none  [the longest x20 23.1 us: dot_nt(): lax.dot_general(a, b, (((1,), (1,)), ((), ())), preferred_element_type=jn...]
    ppermute x66 -> x0, starting transfers between devices: 33.5 us -> none  [the longest x22 25.4 us: swap_chip(): return lax.ppermute(value, 'tensor', CHIP)]
    ppermute x5, waiting for transfers between devices: 2.68 us -> 32.6 us  [sum_all(): lax.ppermute(value, axis, [(i, i ^ bit) for i in range(count)])]
    ppermute x21, waiting for transfers between devices: 69.2 us -> 56.5 us  [reduce_pieces(): came = lax.ppermute(send, 'dp', [(i, i ^ bit) for i in range(size)])]
    convert_element_type x30 -> x7, other arithmetic: 23 us -> 11.9 us  [wide(): return value.astype(jnp.float32)]
  transfers between devices with their start and end apart: 113 -> 47, of which waited for: 44 -> 27; matrix products, arithmetic and copies ran while one was open for 26% -> 7% of each run, Pallas kernels for 10% -> 0%
where the time goes in v2:
time: 632 us; the launch traced here: 628 us
  Pallas kernels  300 us (47%)
  waiting for transfers between devices  199 us (31%)
  starting transfers between devices  53.9 us (9%)
  local copies, waits for them, and re-layouts  37.2 us (6%)
  other arithmetic  36.4 us (6%)
    pallas_call x5, Pallas kernels, call(): pl.pallas_call(kernel, in_specs=[vmem] * n_in, out_specs=[vmem] * n_out,...  221 us
    ppermute x21, waiting for transfers between devices, reduce_pieces(): came = lax.ppermute(current, 'dp', [(i, i ^ bit) for i in range(size)])  110 us
    ppermute x21, waiting for transfers between devices, reduce_pieces(): came = lax.ppermute(send, 'dp', [(i, i ^ bit) for i in range(size)])  56.5 us
    pallas_call x3, Pallas kernels, attention_backward(): pl.pallas_call(functools.partial(backward_kernel, kind, heads, size, chun...  47.1 us
    ppermute x5, waiting for transfers between devices, sum_all(): lax.ppermute(value, axis, [(i, i ^ bit) for i in range(count)])  32.6 us
    pallas_call x3, Pallas kernels, attention_forward(): pl.pallas_call(functools.partial(forward_kernel, kind, heads, size, chunk...  31.2 us
    ppermute x21, starting transfers between devices, reduce_pieces(): came = lax.ppermute(send, 'dp', [(i, i ^ bit) for i in range(size)])  27.6 us
    ppermute x21, starting transfers between devices, reduce_pieces(): came = lax.ppermute(current, 'dp', [(i, i ^ bit) for i in range(size)])  20.4 us
  transfers between devices with their start and end apart: 47, of which 27 were waited for; matrix products, arithmetic and copies ran while one was open for 7% of the time, Pallas kernels for 0%

profile of v2, /device:TPU:0, one launch (start us, length us, event | category | flops | bytes accessed | tf_op | source)
XLA Modules:
  0.0 627.8 jit_solution(15480867053324782140)
XLA Ops:
  1.2 1.7 copy.40.seg_q
  4.3 1.5 copy.42.seg_q
  6.6 3.1 copy.53
  9.6 1.6 copy.54
  11.2 22.8 %rows_in.1 = (bf16[1024,768]{1,0:T(8,128)(2,1)}, bf16[512,768]{1,0:T(8,128)(2,1)}, bf16[1024,192]{1,0:T(8,128)(2,1)}, bf16[1024,192]{1,0:T(8,128)(2,1)}, bf16[10...) custom-call(bf16[256,768]{1,0:T(8,128)(2,1)} %refs_8_.5, ...), custom_call_target="tpu_custom_call" | custom-call | tf_op jit(solution)/shard_map/rows_in/pallas_call | solution.py:408
  34.1 12.4 %attention_forward_encoder.1 = (bf16[1024,192]{1,0:T(8,128)(2,1)}, f32[1024,128]{1,0:T(8,128)}) custom-call(s32[4]{0:T(128)} %iota_xor_fusion.places, bf16[1024,192]{1,0:T(8,128)(2,1)} %get-tuple-element.78.q, bf16[1024,192]{1,0:T(8,128)(2,1)} %get-tuple-element.79.k, bf16[1024,192]{1,0:T(8,128)(2,1)} %get-tuple-element.80.v, s32[1024,1]{1,0:T(8,128)} %copy.40.seg_q, ...), custom_call_target="tpu_custom_call" | custom-call | flops 3221225472 | bytes 1572864 | tf_op jit(solution)/shard_map/attention_forward_encoder/pallas_call | solution.py:230
  46.5 8.6 %attention_forward_decoder.1 = (bf16[512,192]{1,0:T(8,128)(2,1)}, f32[512,128]{1,0:T(8,128)}) custom-call(s32[4]{0:T(128)} %iota_xor_fusion.places, bf16[512,192]{1,0:T(8,128)(2,1)} %get-tuple-element.82.q, bf16[512,192]{1,0:T(8,128)(2,1)} %get-tuple-element.83.k, bf16[512,192]{1,0:T(8,128)(2,1)} %get-tuple-element.84.v, s32[512,1]{1,0:T(8,128)} %copy.42.seg_q, ...), custom_call_target="tpu_custom_call" | custom-call | flops 805306368 | bytes 786432 | tf_op jit(solution)/shard_map/attention_forward_decoder/pallas_call | solution.py:230
  55.1 66.4 %encoder_rows.1 = (f32[256,768]{1,0:T(8,128)}, f32[256,768]{1,0:T(8,128)}, f32[128,768]{1,0:T(8,128)}, bf16[256,768]{1,0:T(8,128)(2,1)}, bf16[1024,768]{1,0:T(8,...) custom-call(bf16[1024,192]{1,0:T(8,128)(2,1)} %get-tuple-element.81., ...), custom_call_target="tpu_custom_call" | custom-call | tf_op jit(solution)/shard_map/encoder_rows/pallas_call | solution.py:408
  121.5 10.1 %attention_forward_cross.1 = (bf16[512,192]{1,0:T(8,128)(2,1)}, f32[512,128]{1,0:T(8,128)}) custom-call(s32[4]{0:T(128)} %iota_xor_fusion.places, bf16[512,192]{1,0:T(8,128)(2,1)} %get-tuple-element.87.q, bf16[1024,192]{1,0:T(8,128)(2,1)} %get-tuple-element.88.k, bf16[1024,192]{1,0:T(8,128)(2,1)} %get-tuple-element.89.v, s32[512,1]{1,0:T(8,128)} %copy.42.seg_q, ...), custom_call_target="tpu_custom_call" | custom-call | flops 1610612736 | bytes 786432 | tf_op jit(solution)/shard_map/attention_forward_cross/pallas_call | solution.py:230
  131.6 38.2 %decoder_rows.1 = (bf16[128,768]{1,0:T(8,128)(2,1)}, f32[128,768]{1,0:T(8,128)}, bf16[512,192]{1,0:T(8,128)(2,1)}, bf16[768,1024]{1,0:T(8,128)(2,1)}, bf16[512,7...) custom-call(bf16[512,192]{1,0:T(8,128)(2,1)} %get-tuple-element.90.refs_0_, bf16[192,768]{1,0:T(8,128)(2,1)} %refs_1_.3, ...), custom_call_target="tpu_custom_call" | custom-call | tf_op jit(solution)/shard_map/decoder_rows/pallas_call | solution.py:408
  170.6 15.2 %attention_backward_cross.1 = (bf16[512,192]{1,0:T(8,128)(2,1)}, bf16[1024,192]{1,0:T(8,128)(2,1)}, bf16[1024,192]{1,0:T(8,128)(2,1)}) custom-call(s32[4]{0:T(128)} %iota_xor_fusion.places, bf16[512,192]{1,0:T(8,128)(2,1)} %get-tuple-element.87.q, bf16[1024,192]{1,0:T(8,128)(2,1)} %get-tuple-element.88.k, bf16[1024,192]{1,0:T(8,128)(2,1)} %get-tuple-element.89.v, ...), custom_call_target="tpu_custom_call" | custom-call | flops 4026531840 | bytes 1572864 | tf_op jit(solution)/shard_map/attention_backward_cross/pallas_call | solution.py:256
  185.8 67.2 %encoder_back.1 = (f32[256,768]{1,0:T(8,128)}, f32[128,768]{1,0:T(8,128)}, bf16[1024,192]{1,0:T(8,128)(2,1)}, bf16[512,192]{1,0:T(8,128)(2,1)}, bf16[384,768]{1,...) custom-call(bf16[512,192]{1,0:T(8,128)(2,1)} %get-tuple-element.96.r, ...), custom_call_target="tpu_custom_call" | custom-call | tf_op jit(solution)/shard_map/encoder_back/pallas_call | solution.py:408
  253.0 20.5 %attention_backward_encoder.1 = (bf16[1024,192]{1,0:T(8,128)(2,1)}, bf16[1024,192]{1,0:T(8,128)(2,1)}, bf16[1024,192]{1,0:T(8,128)(2,1)}, f32[8,128]{1,0:T(8,128)}) custom-call(s32[4]{0:T(128)} %iota_xor_fusion.places, bf16[1024,192]{1,0:T(8,128)(2,1)} %get-tuple-element.78.q, bf16[1024,192]{1,0:T(8,128)(2,1)} %get-tuple-element.79.k, ...), custom_call_target="tpu_custom_call" | custom-call | flops 8053063680 | bytes 3145728 | tf_op jit(solution)/shard_map/attention_backward_encoder/pallas_call | solution.py:256
  273.5 11.4 %attention_backward_decoder.1 = (bf16[512,192]{1,0:T(8,128)(2,1)}, bf16[512,192]{1,0:T(8,128)(2,1)}, bf16[512,192]{1,0:T(8,128)(2,1)}, f32[8,128]{1,0:T(8,128)}) custom-call(s32[4]{0:T(128)} %iota_xor_fusion.places, bf16[512,192]{1,0:T(8,128)(2,1)} %get-tuple-element.82.q, bf16[512,192]{1,0:T(8,128)(2,1)} %get-tuple-element.83.k, ...), custom_call_target="tpu_custom_call" | custom-call | flops 2013265920 | bytes 1572864 | tf_op jit(solution)/shard_map/attention_backward_decoder/pallas_call | solution.py:256
  284.9 26.8 %rows_back.1 = (f32[256,768]{1,0:T(8,128)}, f32[128,768]{1,0:T(8,128)}, bf16[576,768]{1,0:T(8,128)(2,1)}, bf16[576,768]{1,0:T(8,128)(2,1)}, f32[8,768]{1,0:T(8,128)}) custom-call(bf16[1024,192]{1,0:T(8,128)(2,1)} %get-tuple-element.109.refs_0_, bf16[1024,192]{1,0:T(8,128)(2,1)} %get-tuple-element.110.refs_1_, bf16[1024,192]{1,0:T(8,128)(2,1)} %get-tuple-element.111.refs_2_, ...), custom_call_target="tpu_custom_call" | custom-call | tf_op jit(solution)/shard_map/rows_back/pallas_call | solution.py:408
  317.0 2.1 constant_dynamic-slice_fusion.5
  321.9 1.8 constant_dynamic-slice_fusion.14
  328.8 3.0 collective-permute-done.1
  339.5 26.3 %collective-permute-done.2 = f32[4800]{0:T(1024)S(1)} collective-permute-done((f32[4800]{0:T(1024)}, f32[4800]{0:T(1024)S(1)}, u32[]{:S(2)}, u32[]{:S(2)}) %collective-permute-start.2) | collective-permute-done | bytes 19232 | tf_op jit(solution)/shard_map/ppermute | solution.py:694
  368.8 1.5 collective-permute-done.3
  370.9 2.3 collective-permute-start.4
  374.1 1.9 collective-permute-done.4
  385.0 1.6 collective-permute-start.42
  387.8 4.6 collective-permute-done.42
  392.4 1.6 collective-permute-start.18
  394.1 6.1 collective-permute-done.18
  400.2 1.6 collective-permute-start.6
  401.9 7.4 %collective-permute-done.23 = bf16[384,768]{1,0:T(8,128)(2,1)S(1)} collective-permute-done((bf16[384,768]{1,0:T(8,128)(2,1)}, bf16[384,768]{1,0:T(8,128)(2,1)S(1)}, u32[]{:S(2)}, u32[]{:S(2)}) %collective-permute-start.23) | collective-permute-done | bytes 589856 | tf_op jit(solution)/shard_map/ppermute | solution.py:681
  409.3 2.3 collective-permute-start.43
  411.7 6.6 %collective-permute-done.29 = bf16[384,768]{1,0:T(8,128)(2,1)S(1)} collective-permute-done((bf16[384,768]{1,0:T(8,128)(2,1)S(1)}, bf16[384,768]{1,0:T(8,128)(2,1)S(1)}, u32[]{:S(2)}, u32[]{:S(2)}) %collective-permute-start.29) | collective-permute-done | bytes 589856 | tf_op jit(solution)/shard_map/ppermute | solution.py:681
  418.4 2.1 collective-permute-start.19
  420.7 1.7 collective-permute-start.24
  422.5 2.8 collective-permute-done.19
  425.8 3.7 collective-permute-start.44
  432.7 5.3 collective-permute-done.44
  443.3 2.7 collective-permute-start.7
  446.2 19.6 %collective-permute-done.45 = bf16[128,768]{1,0:T(8,128)(2,1)S(1)} collective-permute-done((bf16[128,768]{1,0:T(8,128)(2,1)S(1)}, bf16[128,768]{1,0:T(8,128)(2,1)S(1)}, u32[]{:S(2)}, u32[]{:S(2)}) %collective-permute-start.45) | collective-permute-done | bytes 196640 | tf_op jit(solution)/shard_map/ppermute | solution.py:685
  466.3 1.8 collective-permute-done.21
  468.9 1.5 collective-permute-start.22
  470.4 5.6 collective-permute-done.25
  476.0 1.6 collective-permute-start.46
  477.8 8.0 %collective-permute-done.8 = bf16[96,768]{1,0:T(8,128)(2,1)S(1)} collective-permute-done((bf16[96,768]{1,0:T(8,128)(2,1)S(1)}, bf16[96,768]{1,0:T(8,128)(2,1)S(1)}, u32[]{:S(2)}, u32[]{:S(2)}) %collective-permute-start.8) | collective-permute-done | bytes 147488 | tf_op jit(solution)/shard_map/ppermute | solution.py:685
  485.8 7.5 %collective-permute-done.26 = bf16[96,768]{1,0:T(8,128)(2,1)S(1)} collective-permute-done((bf16[96,768]{1,0:T(8,128)(2,1)S(1)}, bf16[96,768]{1,0:T(8,128)(2,1)S(1)}, u32[]{:S(2)}, u32[]{:S(2)}) %collective-permute-start.26) | collective-permute-done | bytes 147488 | tf_op jit(solution)/shard_map/ppermute | solution.py:685
  493.4 9.5 %collective-permute-done.32 = bf16[96,768]{1,0:T(8,128)(2,1)S(1)} collective-permute-done((bf16[96,768]{1,0:T(8,128)(2,1)S(1)}, bf16[96,768]{1,0:T(8,128)(2,1)S(1)}, u32[]{:S(2)}, u32[]{:S(2)}) %collective-permute-start.32) | collective-permute-done | bytes 147488 | tf_op jit(solution)/shard_map/ppermute | solution.py:685
  503.0 2.1 collective-permute-start.27
  505.6 14.7 %collective-permute-done.37 = bf16[96,1024]{1,0:T(8,128)(2,1)S(1)} collective-permute-done((bf16[96,1024]{1,0:T(8,128)(2,1)S(1)}, bf16[96,1024]{1,0:T(8,128)(2,1)S(1)}, u32[]{:S(2)}, u32[]{:S(2)}) %collective-permute-start.37) | collective-permute-done | bytes 196640 | tf_op jit(solution)/shard_map/ppermute | solution.py:681
  520.2 3.4 collective-permute-start.13
  523.7 8.7 %collective-permute-done.13 = bf16[96,1024]{1,0:T(8,128)(2,1)S(1)} collective-permute-done((bf16[96,1024]{1,0:T(8,128)(2,1)S(1)}, bf16[96,1024]{1,0:T(8,128)(2,1)S(1)}, u32[]{:S(2)}, u32[]{:S(2)}) %collective-permute-start.13) | collective-permute-done | bytes 196640 | tf_op jit(solution)/shard_map/ppermute | solution.py:681
  532.7 2.0 collective-permute-start.38
  538.7 1.7 collective-permute-start.10
  540.4 4.5 collective-permute-done.33
  545.0 5.0 collective-permute-done.38
  550.2 2.0 collective-permute-done.14
  552.4 1.9 collective-permute-start.34
  554.7 7.5 %collective-permute-done.39 = bf16[192,1024]{1,0:T(8,128)(2,1)S(1)} collective-permute-done((bf16[192,1024]{1,0:T(8,128)(2,1)S(1)}, bf16[192,1024]{1,0:T(8,128)(2,1)S(1)}, u32[]{:S(2)}, u32[]{:S(2)}) %collective-permute-start.39) | collective-permute-done | bytes 393248 | tf_op jit(solution)/shard_map/ppermute | solution.py:685
  562.2 4.8 collective-permute-done.15
  567.5 1.9 collective-permute-start.16
  574.5 6.8 %collective-permute-done.28 = bf16[384,768]{1,0:T(8,128)(2,1)S(1)} collective-permute-done((bf16[384,768]{1,0:T(8,128)(2,1)S(1)}, bf16[384,768]{1,0:T(8,128)(2,1)S(1)}, u32[]{:S(2)}, u32[]{:S(2)}) %collective-permute-start.28) | collective-permute-done | bytes 589856 | tf_op jit(solution)/shard_map/ppermute | solution.py:685
  584.7 13.5 %collective-permute-done.16 = bf16[384,1024]{1,0:T(8,128)(2,1)S(1)} collective-permute-done((bf16[384,1024]{1,0:T(8,128)(2,1)S(1)}, bf16[384,1024]{1,0:T(8,128)(2,1)S(1)}, u32[]{:S(2)}, u32[]{:S(2)}) %collective-permute-start.16) | collective-permute-done | bytes 786464 | tf_op jit(solution)/shard_map/ppermute | solution.py:685
  599.8 12.6 %collective-permute-done.40 = bf16[384,1024]{1,0:T(8,128)(2,1)} collective-permute-done((bf16[384,1024]{1,0:T(8,128)(2,1)}, bf16[384,1024]{1,0:T(8,128)(2,1)}, u32[]{:S(2)}, u32[]{:S(2)}) %collective-permute-start.40) | collective-permute-done | bytes 786464 | tf_op jit(solution)/shard_map/ppermute | solution.py:685
  612.3 2.4 broadcast_select_fusion.1
  615.3 2.6 concatenate.108
  617.9 3.3 maximum_convert_fusion
  621.2 3.3 maximum_convert_fusion.1
  (211 shorter events, 69.8 us)
Async XLA Ops:
  6.6 3.1 copy-start
  284.9 26.8 %copy-start.18 = (f32[8,768]{1,0:T(8,128)S(1)}, f32[8,768]{1,0:T(8,128)}, u32[]{:S(2)}) copy-start(f32[8,768]{1,0:T(8,128)} %get-tuple-element.123) | copy-start | bytes 73732
  284.9 28.8 %copy-start.13 = (bf16[192,768]{1,0:T(8,128)(2,1)S(1)}, bf16[192,768]{1,0:T(8,128)(2,1)}, u32[]{:S(2)}) copy-start(bf16[192,768]{1,0:T(8,128)(2,1)} %get-tuple-element.128) | copy-start | bytes 884740
  311.7 3.1 copy-start.5
  313.7 12.6 %collective-permute-start = (f32[6,768]{1,0:T(8,128)}, f32[6,768]{1,0:T(8,128)}, u32[]{:S(2)}, u32[]{:S(2)}) collective-permute-start(f32[6,768]{1,0:T(8,128)} %pad_maximum_fusion.16), channel_id=1, source_target_pairs={{0,1},{1,0},{2,3},{3,2},{4,5},{5,4},{6,7},{7,6},{8,9},{9,8},{10,11... | collective-permute-start | bytes 55304 | tf_op jit(solution)/shard_map/ppermute | solution.py:694
  314.8 5.0 copy-start.7
  315.7 69.3 %collective-permute-start.5 = (bf16[384,768]{1,0:T(8,128)(2,1)}, bf16[384,768]{1,0:T(8,128)(2,1)}, u32[]{:S(2)}, u32[]{:S(2)}) collective-permute-start(bf16[384,768]{1,0:T(8,128)(2,1)} %constant_dynamic-slice_fusion.20), channel_id=1, source_target_pairs={{0,4},{4,0},{8,12},{12,8},{16,20},{20,16},{24,28},{28,24},{1,5},{5... | collective-permute-start | bytes 1769480 | tf_op jit(solution)/shard_map/ppermute | solution.py:681
  319.1 106.7 %collective-permute-start.35 = (bf16[384,1024]{1,0:T(8,128)(2,1)}, bf16[384,1024]{1,0:T(8,128)(2,1)}, u32[]{:S(2)}, u32[]{:S(2)}) collective-permute-start(bf16[384,1024]{1,0:T(8,128)(2,1)} %constant_dynamic-slice_fusion.5), channel_id=1, source_target_pairs={{0,4},{4,0},{8,12},{12,8},{16,20},{20,16},{24,28},{28,24},{1,5},{5... | collective-permute-start | bytes 2359304 | tf_op jit(solution)/shard_map/ppermute | solution.py:681
  319.8 4.6 copy-start.2
  319.8 5.5 copy-start.4
  320.6 59.9 %collective-permute-start.41 = (bf16[256,768]{1,0:T(8,128)(2,1)}, bf16[256,768]{1,0:T(8,128)(2,1)}, u32[]{:S(2)}, u32[]{:S(2)}) collective-permute-start(bf16[256,768]{1,0:T(8,128)(2,1)} %constant_dynamic-slice_fusion.2), channel_id=1, source_target_pairs={{0,4},{4,0},{8,12},{12,8},{16,20},{20,16},{24,28},{28,24},{1,5},{5... | collective-permute-start | bytes 1179656 | tf_op jit(solution)/shard_map/ppermute | solution.py:681
  323.7 58.9 %collective-permute-start.17 = (bf16[256,768]{1,0:T(8,128)(2,1)}, bf16[256,768]{1,0:T(8,128)(2,1)}, u32[]{:S(2)}, u32[]{:S(2)}) collective-permute-start(bf16[256,768]{1,0:T(8,128)(2,1)} %constant_dynamic-slice_fusion.14), channel_id=1, source_target_pairs={{0,4},{4,0},{8,12},{12,8},{16,20},{20,16},{24,28},{28,24},{1,5},{5... | collective-permute-start | bytes 1179656 | tf_op jit(solution)/shard_map/ppermute | solution.py:681
  325.3 1.0 copy-start.12
  325.3 1.0 copy-start.15
  327.7 4.1 collective-permute-start.1
  337.2 28.6 %collective-permute-start.2 = (f32[4800]{0:T(1024)}, f32[4800]{0:T(1024)S(1)}, u32[]{:S(2)}, u32[]{:S(2)}) collective-permute-start(f32[4800]{0:T(1024)} %constant_dynamic-update-slice_fusion.8), channel_id=1, source_target_pairs={{0,4},{4,0},{8,12},{12,8},{16,20},{20,16},{24,28},{28,24},{1,5},{5... | collective-permute-start | bytes 57608 | tf_op jit(solution)/shard_map/ppermute | solution.py:694
  366.5 3.8 collective-permute-start.3
  370.9 5.0 collective-permute-start.4
  375.9 55.1 %collective-permute-start.11 = (bf16[384,1024]{1,0:T(8,128)(2,1)}, bf16[384,1024]{1,0:T(8,128)(2,1)}, u32[]{:S(2)}, u32[]{:S(2)}) collective-permute-start(bf16[384,1024]{1,0:T(8,128)(2,1)} %constant_dynamic-slice_fusion.17), channel_id=1, source_target_pairs={{0,4},{4,0},{8,12},{12,8},{16,20},{20,16},{24,28},{28,24},{1,5},{5... | collective-permute-start | bytes 2359304 | tf_op jit(solution)/shard_map/ppermute | solution.py:681
  379.9 2.7 copy-start.9
  379.9 3.9 copy-start.8
  380.5 28.8 %collective-permute-start.23 = (bf16[384,768]{1,0:T(8,128)(2,1)}, bf16[384,768]{1,0:T(8,128)(2,1)S(1)}, u32[]{:S(2)}, u32[]{:S(2)}) collective-permute-start(bf16[384,768]{1,0:T(8,128)(2,1)} %constant_dynamic-slice_fusion.11), channel_id=1, source_target_pairs={{0,4},{4,0},{8,12},{12,8},{16,20},{20,16},{24,28},{28,24},{1,5},{5... | collective-permute-start | bytes 1769480 | tf_op jit(solution)/shard_map/ppermute | solution.py:681
  382.6 35.8 %collective-permute-start.29 = (bf16[384,768]{1,0:T(8,128)(2,1)S(1)}, bf16[384,768]{1,0:T(8,128)(2,1)S(1)}, u32[]{:S(2)}, u32[]{:S(2)}) collective-permute-start(bf16[384,768]{1,0:T(8,128)(2,1)S(1)} %copy-done.9), channel_id=1, source_target_pairs={{0,4},{4,0},{8,12},{12,8},{16,20},{20,16},{24,28},{28,24},{1,5},{5... | collective-permute-start | bytes 1769480 | tf_op jit(solution)/shard_map/ppermute | solution.py:681
  385.0 7.4 %collective-permute-start.42 = (bf16[128,768]{1,0:T(8,128)(2,1)S(1)}, bf16[128,768]{1,0:T(8,128)(2,1)S(1)}, u32[]{:S(2)}, u32[]{:S(2)}) collective-permute-start(bf16[128,768]{1,0:T(8,128)(2,1)S(1)} %constant_dynamic-slice_fusion.1), channel_id=1, source_target_pairs={{0,8},{4,12},{8,0},{12,4},{16,24},{20,28},{24,16},{28,20},{1,9},{5... | collective-permute-start | bytes 589832 | tf_op jit(solution)/shard_map/ppermute | solution.py:681
  392.4 7.8 %collective-permute-start.18 = (bf16[128,768]{1,0:T(8,128)(2,1)S(1)}, bf16[128,768]{1,0:T(8,128)(2,1)S(1)}, u32[]{:S(2)}, u32[]{:S(2)}) collective-permute-start(bf16[128,768]{1,0:T(8,128)(2,1)S(1)} %constant_dynamic-slice_fusion.13), channel_id=1, source_target_pairs={{0,8},{4,12},{8,0},{12,4},{16,24},{20,28},{24,16},{28,20},{1,9},{5... | collective-permute-start | bytes 589832 | tf_op jit(solution)/shard_map/ppermute | solution.py:681
  400.2 40.7 %collective-permute-start.6 = (bf16[192,768]{1,0:T(8,128)(2,1)S(1)}, bf16[192,768]{1,0:T(8,128)(2,1)S(1)}, u32[]{:S(2)}, u32[]{:S(2)}) collective-permute-start(bf16[192,768]{1,0:T(8,128)(2,1)S(1)} %constant_dynamic-slice_fusion.19), channel_id=1, source_target_pairs={{0,8},{4,12},{8,0},{12,4},{16,24},{20,28},{24,16},{28,20},{1,9},{5... | collective-permute-start | bytes 884744 | tf_op jit(solution)/shard_map/ppermute | solution.py:681
  409.3 11.5 %collective-permute-start.43 = (bf16[64,768]{1,0:T(8,128)(2,1)S(1)}, bf16[64,768]{1,0:T(8,128)(2,1)S(1)}, u32[]{:S(2)}, u32[]{:S(2)}) collective-permute-start(bf16[64,768]{1,0:T(8,128)(2,1)S(1)} %constant_dynamic-slice_fusion), channel_id=1, source_target_pairs={{0,16},{4,20},{8,24},{12,28},{16,0},{20,4},{24,8},{28,12},{1,17},{... | collective-permute-start | bytes 294920 | tf_op jit(solution)/shard_map/ppermute | solution.py:681
  411.7 17.8 %copy-start.1 = (bf16[768,1024]{1,0:T(8,128)(2,1)S(1)}, bf16[768,1024]{1,0:T(8,128)(2,1)}, u32[]{:S(2)}) copy-start(bf16[768,1024]{1,0:T(8,128)(2,1)} %get-tuple-element.137) | copy-start | bytes 4718596
  418.4 6.9 %collective-permute-start.19 = (bf16[64,768]{1,0:T(8,128)(2,1)S(1)}, bf16[64,768]{1,0:T(8,128)(2,1)S(1)}, u32[]{:S(2)}, u32[]{:S(2)}) collective-permute-start(bf16[64,768]{1,0:T(8,128)(2,1)S(1)} %constant_dynamic-slice_fusion.12), channel_id=1, source_target_pairs={{0,16},{4,20},{8,24},{12,28},{16,0},{20,4},{24,8},{28,12},{1,17},{... | collective-permute-start | bytes 294920 | tf_op jit(solution)/shard_map/ppermute | solution.py:681
  420.7 21.6 %collective-permute-start.24 = (bf16[192,768]{1,0:T(8,128)(2,1)S(1)}, bf16[192,768]{1,0:T(8,128)(2,1)S(1)}, u32[]{:S(2)}, u32[]{:S(2)}) collective-permute-start(bf16[192,768]{1,0:T(8,128)(2,1)S(1)} %constant_dynamic-slice_fusion.10), channel_id=1, source_target_pairs={{0,8},{4,12},{8,0},{12,4},{16,24},{20,28},{24,16},{28,20},{1,9},{5... | collective-permute-start | bytes 884744 | tf_op jit(solution)/shard_map/ppermute | solution.py:681
  425.3 18.0 %collective-permute-start.30 = (bf16[192,768]{1,0:T(8,128)(2,1)S(1)}, bf16[192,768]{1,0:T(8,128)(2,1)S(1)}, u32[]{:S(2)}, u32[]{:S(2)}) collective-permute-start(bf16[192,768]{1,0:T(8,128)(2,1)S(1)} %constant_dynamic-slice_fusion.7), channel_id=1, source_target_pairs={{0,8},{4,12},{8,0},{12,4},{16,24},{20,28},{24,16},{28,20},{1,9},{5... | collective-permute-start | bytes 884744 | tf_op jit(solution)/shard_map/ppermute | solution.py:681
  425.8 5.4 copy-start.3
  425.8 12.2 %collective-permute-start.44 = (bf16[64,768]{1,0:T(8,128)(2,1)S(1)}, bf16[64,768]{1,0:T(8,128)(2,1)S(1)}, u32[]{:S(2)}, u32[]{:S(2)}) collective-permute-start(bf16[64,768]{1,0:T(8,128)(2,1)S(1)} %add_convert_fusion.19), channel_id=1, source_target_pairs={{0,16},{4,20},{8,24},{12,28},{16,0},{20,4},{24,8},{28,12},{1,17},{... | collective-permute-start | bytes 294920 | tf_op jit(solution)/shard_map/ppermute | solution.py:685
  431.0 9.1 %collective-permute-start.20 = (bf16[64,768]{1,0:T(8,128)(2,1)S(1)}, bf16[64,768]{1,0:T(8,128)(2,1)S(1)}, u32[]{:S(2)}, u32[]{:S(2)}) collective-permute-start(bf16[64,768]{1,0:T(8,128)(2,1)S(1)} %add_convert_fusion.20), channel_id=1, source_target_pairs={{0,16},{4,20},{8,24},{12,28},{16,0},{20,4},{24,8},{28,12},{1,17},{... | collective-permute-start | bytes 294920 | tf_op jit(solution)/shard_map/ppermute | solution.py:685
  438.0 65.0 %collective-permute-start.36 = (bf16[192,1024]{1,0:T(8,128)(2,1)S(1)}, bf16[192,1024]{1,0:T(8,128)(2,1)S(1)}, u32[]{:S(2)}, u32[]{:S(2)}) collective-permute-start(bf16[192,1024]{1,0:T(8,128)(2,1)S(1)} %constant_dynamic-slice_fusion.4), channel_id=1, source_target_pairs={{0,8},{4,12},{8,0},{12,4},{16,24},{20,28},{24,16},{28,20},{1,9},{5... | collective-permute-start | bytes 1179656 | tf_op jit(solution)/shard_map/ppermute | solution.py:681
  440.1 65.2 %collective-permute-start.12 = (bf16[192,1024]{1,0:T(8,128)(2,1)S(1)}, bf16[192,1024]{1,0:T(8,128)(2,1)S(1)}, u32[]{:S(2)}, u32[]{:S(2)}) collective-permute-start(bf16[192,1024]{1,0:T(8,128)(2,1)S(1)} %constant_dynamic-slice_fusion.16), channel_id=1, source_target_pairs={{0,8},{4,12},{8,0},{12,4},{16,24},{20,28},{24,16},{28,20},{1,9},{5... | collective-permute-start | bytes 1179656 | tf_op jit(solution)/shard_map/ppermute | solution.py:681
  440.9 24.8 %collective-permute-start.45 = (bf16[128,768]{1,0:T(8,128)(2,1)S(1)}, bf16[128,768]{1,0:T(8,128)(2,1)S(1)}, u32[]{:S(2)}, u32[]{:S(2)}) collective-permute-start(bf16[128,768]{1,0:T(8,128)(2,1)S(1)} %pad_maximum_fusion.15), channel_id=1, source_target_pairs={{0,8},{4,12},{8,0},{12,4},{16,24},{20,28},{24,16},{28,20},{1,9},{5... | collective-permute-start | bytes 589832 | tf_op jit(solution)/shard_map/ppermute | solution.py:685
  442.4 25.7 %collective-permute-start.21 = (bf16[128,768]{1,0:T(8,128)(2,1)S(1)}, bf16[128,768]{1,0:T(8,128)(2,1)S(1)}, u32[]{:S(2)}, u32[]{:S(2)}) collective-permute-start(bf16[128,768]{1,0:T(8,128)(2,1)S(1)} %pad_maximum_fusion.14), channel_id=1, source_target_pairs={{0,8},{4,12},{8,0},{12,4},{16,24},{20,28},{24,16},{28,20},{1,9},{5... | collective-permute-start | bytes 589832 | tf_op jit(solution)/shard_map/ppermute | solution.py:685
  443.3 25.6 %collective-permute-start.7 = (bf16[96,768]{1,0:T(8,128)(2,1)S(1)}, bf16[96,768]{1,0:T(8,128)(2,1)S(1)}, u32[]{:S(2)}, u32[]{:S(2)}) collective-permute-start(bf16[96,768]{1,0:T(8,128)(2,1)S(1)} %constant_dynamic-slice_fusion.18), channel_id=1, source_target_pairs={{0,16},{4,20},{8,24},{12,28},{16,0},{20,4},{24,8},{28,12},{1,17},{... | collective-permute-start | bytes 442376 | tf_op jit(solution)/shard_map/ppermute | solution.py:681
  465.8 10.2 %collective-permute-start.25 = (bf16[96,768]{1,0:T(8,128)(2,1)S(1)}, bf16[96,768]{1,0:T(8,128)(2,1)S(1)}, u32[]{:S(2)}, u32[]{:S(2)}) collective-permute-start(bf16[96,768]{1,0:T(8,128)(2,1)S(1)} %constant_dynamic-slice_fusion.9), channel_id=1, source_target_pairs={{0,16},{4,20},{8,24},{12,28},{16,0},{20,4},{24,8},{28,12},{1,17},{... | collective-permute-start | bytes 442376 | tf_op jit(solution)/shard_map/ppermute | solution.py:681
  468.0 9.6 %collective-permute-start.31 = (bf16[96,768]{1,0:T(8,128)(2,1)S(1)}, bf16[96,768]{1,0:T(8,128)(2,1)S(1)}, u32[]{:S(2)}, u32[]{:S(2)}) collective-permute-start(bf16[96,768]{1,0:T(8,128)(2,1)S(1)} %constant_dynamic-slice_fusion.6), channel_id=1, source_target_pairs={{0,16},{4,20},{8,24},{12,28},{16,0},{20,4},{24,8},{28,12},{1,17},{... | collective-permute-start | bytes 442376 | tf_op jit(solution)/shard_map/ppermute | solution.py:681
  468.9 63.8 %collective-permute-start.22 = (bf16[256,768]{1,0:T(8,128)(2,1)S(1)}, bf16[256,768]{1,0:T(8,128)(2,1)S(1)}, u32[]{:S(2)}, u32[]{:S(2)}) collective-permute-start(bf16[256,768]{1,0:T(8,128)(2,1)S(1)} %pad_maximum_fusion.8), channel_id=1, source_target_pairs={{0,4},{4,0},{8,12},{12,8},{16,20},{20,16},{24,28},{28,24},{1,5},{5... | collective-permute-start | bytes 1179656 | tf_op jit(solution)/shard_map/ppermute | solution.py:685
  476.0 58.9 %collective-permute-start.46 = (bf16[256,768]{1,0:T(8,128)(2,1)S(1)}, bf16[256,768]{1,0:T(8,128)(2,1)S(1)}, u32[]{:S(2)}, u32[]{:S(2)}) collective-permute-start(bf16[256,768]{1,0:T(8,128)(2,1)S(1)} %pad_maximum_fusion.10), channel_id=1, source_target_pairs={{0,4},{4,0},{8,12},{12,8},{16,20},{20,16},{24,28},{28,24},{1,5},{5... | collective-permute-start | bytes 1179656 | tf_op jit(solution)/shard_map/ppermute | solution.py:685
  477.6 8.2 %collective-permute-start.8 = (bf16[96,768]{1,0:T(8,128)(2,1)S(1)}, bf16[96,768]{1,0:T(8,128)(2,1)S(1)}, u32[]{:S(2)}, u32[]{:S(2)}) collective-permute-start(bf16[96,768]{1,0:T(8,128)(2,1)S(1)} %add_convert_fusion.18), channel_id=1, source_target_pairs={{0,16},{4,20},{8,24},{12,28},{16,0},{20,4},{24,8},{28,12},{1,17},{... | collective-permute-start | bytes 442376 | tf_op jit(solution)/shard_map/ppermute | solution.py:685
  485.8 7.6 %collective-permute-start.26 = (bf16[96,768]{1,0:T(8,128)(2,1)S(1)}, bf16[96,768]{1,0:T(8,128)(2,1)S(1)}, u32[]{:S(2)}, u32[]{:S(2)}) collective-permute-start(bf16[96,768]{1,0:T(8,128)(2,1)S(1)} %add_convert_fusion.17), channel_id=1, source_target_pairs={{0,16},{4,20},{8,24},{12,28},{16,0},{20,4},{24,8},{28,12},{1,17},{... | collective-permute-start | bytes 442376 | tf_op jit(solution)/shard_map/ppermute | solution.py:685
  493.3 9.6 %collective-permute-start.32 = (bf16[96,768]{1,0:T(8,128)(2,1)S(1)}, bf16[96,768]{1,0:T(8,128)(2,1)S(1)}, u32[]{:S(2)}, u32[]{:S(2)}) collective-permute-start(bf16[96,768]{1,0:T(8,128)(2,1)S(1)} %add_convert_fusion.16), channel_id=1, source_target_pairs={{0,16},{4,20},{8,24},{12,28},{16,0},{20,4},{24,8},{28,12},{1,17},{... | collective-permute-start | bytes 442376 | tf_op jit(solution)/shard_map/ppermute | solution.py:685
  503.0 35.6 %collective-permute-start.9 = (bf16[192,768]{1,0:T(8,128)(2,1)S(1)}, bf16[192,768]{1,0:T(8,128)(2,1)S(1)}, u32[]{:S(2)}, u32[]{:S(2)}) collective-permute-start(bf16[192,768]{1,0:T(8,128)(2,1)S(1)} %pad_maximum_fusion.11), channel_id=1, source_target_pairs={{0,8},{4,12},{8,0},{12,4},{16,24},{20,28},{24,16},{28,20},{1,9},{5... | collective-permute-start | bytes 884744 | tf_op jit(solution)/shard_map/ppermute | solution.py:685
  503.0 51.3 %collective-permute-start.27 = (bf16[192,768]{1,0:T(8,128)(2,1)S(1)}, bf16[192,768]{1,0:T(8,128)(2,1)S(1)}, u32[]{:S(2)}, u32[]{:S(2)}) collective-permute-start(bf16[192,768]{1,0:T(8,128)(2,1)S(1)} %pad_maximum_fusion.12), channel_id=1, source_target_pairs={{0,8},{4,12},{8,0},{12,4},{16,24},{20,28},{24,16},{28,20},{1,9},{5... | collective-permute-start | bytes 884744 | tf_op jit(solution)/shard_map/ppermute | solution.py:685
  505.3 14.9 %collective-permute-start.37 = (bf16[96,1024]{1,0:T(8,128)(2,1)S(1)}, bf16[96,1024]{1,0:T(8,128)(2,1)S(1)}, u32[]{:S(2)}, u32[]{:S(2)}) collective-permute-start(bf16[96,1024]{1,0:T(8,128)(2,1)S(1)} %constant_dynamic-slice_fusion.3), channel_id=1, source_target_pairs={{0,16},{4,20},{8,24},{12,28},{16,0},{20,4},{24,8},{28,12},{1,17},{... | collective-permute-start | bytes 589832 | tf_op jit(solution)/shard_map/ppermute | solution.py:681
  520.2 12.2 %collective-permute-start.13 = (bf16[96,1024]{1,0:T(8,128)(2,1)S(1)}, bf16[96,1024]{1,0:T(8,128)(2,1)S(1)}, u32[]{:S(2)}, u32[]{:S(2)}) collective-permute-start(bf16[96,1024]{1,0:T(8,128)(2,1)S(1)} %constant_dynamic-slice_fusion.15), channel_id=1, source_target_pairs={{0,16},{4,20},{8,24},{12,28},{16,0},{20,4},{24,8},{28,12},{1,17},{... | collective-permute-start | bytes 589832 | tf_op jit(solution)/shard_map/ppermute | solution.py:681
  532.4 12.6 %collective-permute-start.33 = (bf16[192,768]{1,0:T(8,128)(2,1)S(1)}, bf16[192,768]{1,0:T(8,128)(2,1)S(1)}, u32[]{:S(2)}, u32[]{:S(2)}) collective-permute-start(bf16[192,768]{1,0:T(8,128)(2,1)S(1)} %pad_maximum_fusion.13), channel_id=1, source_target_pairs={{0,8},{4,12},{8,0},{12,4},{16,24},{20,28},{24,16},{28,20},{1,9},{5... | collective-permute-start | bytes 884744 | tf_op jit(solution)/shard_map/ppermute | solution.py:685
  532.7 17.3 %collective-permute-start.38 = (bf16[96,1024]{1,0:T(8,128)(2,1)S(1)}, bf16[96,1024]{1,0:T(8,128)(2,1)S(1)}, u32[]{:S(2)}, u32[]{:S(2)}) collective-permute-start(bf16[96,1024]{1,0:T(8,128)(2,1)S(1)} %add_convert_fusion.13), channel_id=1, source_target_pairs={{0,16},{4,20},{8,24},{12,28},{16,0},{20,4},{24,8},{28,12},{1,17},{... | collective-permute-start | bytes 589832 | tf_op jit(solution)/shard_map/ppermute | solution.py:685
  534.9 17.3 %collective-permute-start.14 = (bf16[96,1024]{1,0:T(8,128)(2,1)S(1)}, bf16[96,1024]{1,0:T(8,128)(2,1)S(1)}, u32[]{:S(2)}, u32[]{:S(2)}) collective-permute-start(bf16[96,1024]{1,0:T(8,128)(2,1)S(1)} %add_convert_fusion.15), channel_id=1, source_target_pairs={{0,16},{4,20},{8,24},{12,28},{16,0},{20,4},{24,8},{28,12},{1,17},{... | collective-permute-start | bytes 589832 | tf_op jit(solution)/shard_map/ppermute | solution.py:685
  538.7 33.1 %collective-permute-start.10 = (bf16[384,768]{1,0:T(8,128)(2,1)S(1)}, bf16[384,768]{1,0:T(8,128)(2,1)S(1)}, u32[]{:S(2)}, u32[]{:S(2)}) collective-permute-start(bf16[384,768]{1,0:T(8,128)(2,1)S(1)} %pad_maximum_fusion.4), channel_id=1, source_target_pairs={{0,4},{4,0},{8,12},{12,8},{16,20},{20,16},{24,28},{28,24},{1,5},{5... | collective-permute-start | bytes 1769480 | tf_op jit(solution)/shard_map/ppermute | solution.py:685
  550.1 12.1 %collective-permute-start.39 = (bf16[192,1024]{1,0:T(8,128)(2,1)S(1)}, bf16[192,1024]{1,0:T(8,128)(2,1)S(1)}, u32[]{:S(2)}, u32[]{:S(2)}) collective-permute-start(bf16[192,1024]{1,0:T(8,128)(2,1)S(1)} %pad_maximum_fusion.9), channel_id=1, source_target_pairs={{0,8},{4,12},{8,0},{12,4},{16,24},{20,28},{24,16},{28,20},{1,9},{5... | collective-permute-start | bytes 1179656 | tf_op jit(solution)/shard_map/ppermute | solution.py:685
  552.2 14.7 %collective-permute-start.15 = (bf16[192,1024]{1,0:T(8,128)(2,1)S(1)}, bf16[192,1024]{1,0:T(8,128)(2,1)S(1)}, u32[]{:S(2)}, u32[]{:S(2)}) collective-permute-start(bf16[192,1024]{1,0:T(8,128)(2,1)S(1)} %pad_maximum_fusion.7), channel_id=1, source_target_pairs={{0,8},{4,12},{8,0},{12,4},{16,24},{20,28},{24,16},{28,20},{1,9},{5... | collective-permute-start | bytes 1179656 | tf_op jit(solution)/shard_map/ppermute | solution.py:685
  552.4 18.1 %collective-permute-start.34 = (bf16[384,768]{1,0:T(8,128)(2,1)S(1)}, bf16[384,768]{1,0:T(8,128)(2,1)S(1)}, u32[]{:S(2)}, u32[]{:S(2)}) collective-permute-start(bf16[384,768]{1,0:T(8,128)(2,1)S(1)} %pad_maximum_fusion.6), channel_id=1, source_target_pairs={{0,4},{4,0},{8,12},{12,8},{16,20},{20,16},{24,28},{28,24},{1,5},{5... | collective-permute-start | bytes 1769480 | tf_op jit(solution)/shard_map/ppermute | solution.py:685
  554.4 26.9 %collective-permute-start.28 = (bf16[384,768]{1,0:T(8,128)(2,1)S(1)}, bf16[384,768]{1,0:T(8,128)(2,1)S(1)}, u32[]{:S(2)}, u32[]{:S(2)}) collective-permute-start(bf16[384,768]{1,0:T(8,128)(2,1)S(1)} %pad_maximum_fusion.5), channel_id=1, source_target_pairs={{0,4},{4,0},{8,12},{12,8},{16,20},{20,16},{24,28},{28,24},{1,5},{5... | collective-permute-start | bytes 1769480 | tf_op jit(solution)/shard_map/ppermute | solution.py:685
  567.5 30.7 %collective-permute-start.16 = (bf16[384,1024]{1,0:T(8,128)(2,1)S(1)}, bf16[384,1024]{1,0:T(8,128)(2,1)S(1)}, u32[]{:S(2)}, u32[]{:S(2)}) collective-permute-start(bf16[384,1024]{1,0:T(8,128)(2,1)S(1)} %pad_maximum_fusion.2), channel_id=1, source_target_pairs={{0,4},{4,0},{8,12},{12,8},{16,20},{20,16},{24,28},{28,24},{1,5},{5... | collective-permute-start | bytes 2359304 | tf_op jit(solution)/shard_map/ppermute | solution.py:685
  570.3 42.0 %collective-permute-start.40 = (bf16[384,1024]{1,0:T(8,128)(2,1)}, bf16[384,1024]{1,0:T(8,128)(2,1)}, u32[]{:S(2)}, u32[]{:S(2)}) collective-permute-start(bf16[384,1024]{1,0:T(8,128)(2,1)} %pad_maximum_fusion.3), channel_id=1, source_target_pairs={{0,4},{4,0},{8,12},{12,8},{16,20},{20,16},{24,28},{28,24},{1,5},{5... | collective-permute-start | bytes 2359304 | tf_op jit(solution)/shard_map/ppermute | solution.py:685
  621.2 3.3 copy-start.10
  621.2 4.0 copy-start.16
  624.5 1.4 copy-start.6
  624.5 2.3 copy-start.11
  (4 other events, 3.1 us)
